TPU v7x, 32 devices: a whole 2x2x4 slice. The times are simulated.
32 devices in a mesh: sweep: 8 (over z, x), span: 4 (over y, core).
Axes of the slice: x: 2, y: 2, z: 4, core: 2. Of those that a mesh axis runs over, the one named last changes fastest.
Arguments:
- residual_in: float32 [8, 4, 4, 100, 128], P('sweep', 'span'), may hold values from -6 to 6
- diag_inverse: bfloat16 [8, 4, 100, 100, 128], P('sweep', 'span'), may hold values from -2 to 2
- up_block: bfloat16 [8, 4, 100, 100, 128], P('sweep', 'span'), may hold values from -0.4375 to 0.4375
- side_blocks: bfloat16 [8, 4, 3, 100, 100, 128], P('sweep', 'span'), may hold values from -1 to 1
- up_cols: int32 [8, 4, 128], P('sweep', 'span'), may hold values from 0 to 127, as said below
- down_cols: int32 [8, 4, 128], P('sweep', 'span'), may hold values from 0 to 127, as said below
- left_cols: int32 [8, 4, 128], P('sweep', 'span'), may hold values from 0 to 127, as said below
- right_cols: int32 [8, 4, 128], P('sweep', 'span'), may hold values from 0 to 127, as said below
Outputs:
- smoothed: float32 [8, 4, 4, 100, 128], P('sweep', 'span')
Inputs may be any that keep to these rules, and one draw needn't show every extreme that they name: For each slab and partition, a permutation of the 128 positions; down_cols of slab s is the inverse of up_cols of slab s + 1. `down_cols`: for each slab and partition, a permutation of the 128 positions. For each slab and partition, a permutation of the 128 positions; right_cols of partition p is the inverse of left_cols of partition p + 1. `right_cols`: for each slab and partition, a permutation of the 128 positions.
All inputs are finite; a program needn't handle non-finite values.
Results may differ from a plain program's by a relative error of at most 0.0003.
Values sent between devices are 32-bit elements; how exact they have to be, the bound alone decides.
No kernel may reach another device: no remote copies, remote signals or barrier semaphores. Data moves between devices by JAX's collectives and lax.ppermute only.
A program may use at most 128 MiB of HBM per device.

v0:
```python
import jax
import jax.numpy as jnp
from jax import lax
from jax.sharding import PartitionSpec as P


def passed_along(block, axis, distance):
    devices = range(lax.axis_size(axis))
    route = [(i - distance, i) for i in devices if i - distance in devices]
    return lax.ppermute(block, axis, route)


def extended(cells, sides, width):
    for axis, dim in sides:
        count = lax.axis_size(axis)
        ends = count - 1
        head = lax.slice_in_dim(cells, 0, width, axis=dim)
        tail = lax.slice_in_dim(cells, cells.shape[dim] - width, cells.shape[dim], axis=dim)
        cells = jnp.concatenate(
            [
                lax.ppermute(tail, axis, [(i, (i + 1) % count) for i in range(ends)]),
                cells,
                lax.ppermute(head, axis, [((i + 1) % count, i) for i in range(ends)]),
            ],
            axis=dim,
        )
    return cells


def product(block, field):
    vectors = field.shape[0]
    high_part = lax.optimization_barrier(field.astype(jnp.bfloat16))
    low_part = (field - high_part.astype(jnp.float32)).astype(jnp.bfloat16)
    stacked = jnp.concatenate([high_part, low_part], 0)
    both = jnp.einsum("ijm,kjm->kim", block, stacked, preferred_element_type=jnp.float32)
    return both[:vectors] + both[vectors:]


def select(field, columns):
    return jnp.take(field, columns, axis=2)


def send_forward_all(values):
    return passed_along(values, "sweep", 1)


def send_backward_all(values):
    return passed_along(values, "sweep", -1)


def chain_whole(known_part, order_rank, slab_count, finish, sender):
    empty = jnp.zeros_like(known_part)

    def section(section_no, state_pair):
        incoming, result = state_pair
        result = lax.cond(
            order_rank == section_no,
            lambda operands: finish(operands[0], operands[1]),
            lambda operands: operands[2],
            (known_part, incoming, result),
        )
        received = sender(result)
        incoming = jnp.where(order_rank == section_no + 1, received, incoming)
        return (incoming, result)

    incoming, result = lax.fori_loop(0, slab_count, section, (empty, empty))
    return (result, incoming)


def per_device(
    residual_in, diag_inverse, up_block, side_blocks, up_cols, down_cols, left_cols, right_cols
):
    source = residual_in[0, 0]
    inverse = diag_inverse[0, 0]
    upward = up_block[0, 0]
    sideway = side_blocks[0, 0]
    up_index = up_cols[0, 0]
    down_index = down_cols[0, 0]
    left_index = left_cols[0, 0]
    right_index = right_cols[0, 0]
    position = lax.axis_index("sweep")
    slab_count = lax.axis_size("sweep")

    def lateral(old_field):
        padded_field = extended(old_field[None, None], (("span", 1),), 1)
        return product(sideway[1], select(padded_field[0, 0], left_index)) + product(
            sideway[2], select(padded_field[0, 2], right_index)
        )

    def finish_forward(known, incoming):
        return product(inverse, known - product(upward, select(incoming, up_index)))

    def finish_backward(known, incoming):
        return product(inverse, known - product(sideway[0], select(incoming, down_index)))

    def run_chain(known_part, forward):
        if forward:
            order_rank = position
            finish = finish_forward
        else:
            order_rank = slab_count - 1 - position
            finish = finish_backward
        sender = send_forward_all if forward else send_backward_all
        return chain_whole(known_part, order_rank, slab_count, finish, sender)

    field_one, upstream_one = run_chain(source, True)
    known_two = source - lateral(field_one) - product(upward, select(upstream_one, up_index))
    field_two, downstream_two = run_chain(known_two, False)
    known_three = (
        source - lateral(field_two) - product(sideway[0], select(downstream_two, down_index))
    )
    field_three, upstream_three = run_chain(known_three, True)
    known_four = source - lateral(field_three) - product(upward, select(upstream_three, up_index))
    field_four, _ = run_chain(known_four, False)
    return field_four[None, None]


def solution(mesh):
    return jax.shard_map(
        per_device,
        mesh=mesh,
        in_specs=(
            P("sweep", "span", None, None, None),
            P("sweep", "span", None, None, None),
            P("sweep", "span", None, None, None),
            P("sweep", "span", None, None, None, None),
            P("sweep", "span", None),
            P("sweep", "span", None),
            P("sweep", "span", None),
            P("sweep", "span", None),
        ),
        out_specs=P("sweep", "span", None, None, None),
        check_vma=False,
    )
```

profile of v0, /device:TPU:0, one launch (start us, length us, event | category | flops | bytes accessed | tf_op | source)
XLA Modules:
  0.0 885.0 jit_solution(18274868795096063952)
XLA Ops:
  12.7 151.1 %while.76 = (s32[]{:T(128)}, f32[4,100,128]{1,0,2:T(4,128)}, f32[4,100,128]{1,0,2:T(4,128)}, s32[]{:T(128)}, s32[128]{0:T(128)S(1)}, /*index=5*/bf16[100,100,128...) while((s32[]{:T(128)}, f32[4,100,128]{1,0,2:T(4,128)}, ...), condition=%wide.region_3.5_spmd.clone, body=%wide.region_0.4_spmd.clone.sunk | while | flops 42651780 | bytes 12295292 | solution.py:66
  13.5 11.5 %conditional.12 = (f32[4,100,128]{1,0,2:T(4,128)}) conditional(s32[]{:T(128)} %convert_element_type.267, f32[4,100,128]{1,0,2:T(4,128)} %get-tuple-element.1064, (f32[4,100,128]{1,0,2:T(4,128)}, s32[128]{0:T(128)S(1)}, bf16[100,100,128]{1,0,2:T(8,128)(2,1)}, f32[4,100,128]{1,0,2:T(4,128)}, bf16[100,100,128]{1,0,2:T(8,128)(2,1)S(1)}) %tuple.163), branch_computations={%region_1.0_spmd, %region_2.3_spmd} | conditional | flops 42498176 | bytes 10451876 | solution.py:56
  35.5 17.5 %collective-permute-start = (f32[4,100,128]{1,0,2:T(4,128)}, f32[4,100,128]{1,0,2:T(4,128)}, u32[]{:S(2)}, u32[]{:S(2)}) collective-permute-start(f32[4,100,128]{1,0,2:T(4,128)} %get-tuple-element.1172), channel_id=1, source_target_pairs={{0,4},{4,8},{8,12},{12,16},{16,20},{20,24},{24,28},{1,5},{5,9},{9,... | collective-permute-start | bytes 614408 | tf_op jit(solution)/shard_map/while/body/eval_jaxpr/ppermute | solution.py:10
  74.6 15.7 %collective-permute-start = (f32[4,100,128]{1,0,2:T(4,128)}, f32[4,100,128]{1,0,2:T(4,128)}, u32[]{:S(2)}, u32[]{:S(2)}) collective-permute-start(f32[4,100,128]{1,0,2:T(4,128)} %get-tuple-element.1172), channel_id=1, source_target_pairs={{0,4},{4,8},{8,12},{12,16},{16,20},{20,24},{24,28},{1,5},{5,9},{9,... | collective-permute-start | bytes 614408 | tf_op jit(solution)/shard_map/while/body/eval_jaxpr/ppermute | solution.py:10
  110.4 13.9 %collective-permute-start = (f32[4,100,128]{1,0,2:T(4,128)}, f32[4,100,128]{1,0,2:T(4,128)}, u32[]{:S(2)}, u32[]{:S(2)}) collective-permute-start(f32[4,100,128]{1,0,2:T(4,128)} %get-tuple-element.1172), channel_id=1, source_target_pairs={{0,4},{4,8},{8,12},{12,16},{16,20},{20,24},{24,28},{1,5},{5,9},{9,... | collective-permute-start | bytes 614408 | tf_op jit(solution)/shard_map/while/body/eval_jaxpr/ppermute | solution.py:10
  144.1 14.5 %collective-permute-start = (f32[4,100,128]{1,0,2:T(4,128)}, f32[4,100,128]{1,0,2:T(4,128)}, u32[]{:S(2)}, u32[]{:S(2)}) collective-permute-start(f32[4,100,128]{1,0,2:T(4,128)} %get-tuple-element.1172), channel_id=1, source_target_pairs={{0,4},{4,8},{8,12},{12,16},{16,20},{20,24},{24,28},{1,5},{5,9},{9,... | collective-permute-start | bytes 614408 | tf_op jit(solution)/shard_map/while/body/eval_jaxpr/ppermute | solution.py:10
  167.3 13.3 %copy.21 = bf16[1,1,3,100,100,128]{4,3,5,2,1,0:T(8,128)(2,1)} copy(bf16[1,1,3,100,100,128]{5,4,3,2,1,0:T(8,128)(2,1)} %param.29) | data formatting | bytes 15360000 | tf_op args[3]
  210.7 227.2 %while.77 = (s32[]{:T(128)}, f32[4,100,128]{1,0,2:T(4,128)}, f32[4,100,128]{1,0,2:T(4,128)}, s32[]{:T(128)}, s32[128]{0:T(128)S(1)}, /*index=5*/bf16[3,100,100,1...) while((s32[]{:T(128)}, f32[4,100,128]{1,0,2:T(4,128)}, ...), condition=%wide.region_7.9_spmd.clone, body=%wide.region_4.0_spmd.clone.sunk | while | flops 42651780 | bytes 13143164 | solution.py:66
  227.7 18.4 %collective-permute-done.1 = f32[4,100,128]{1,0,2:T(4,128)} collective-permute-done((f32[4,100,128]{1,0,2:T(4,128)}, f32[4,100,128]{1,0,2:T(4,128)}, u32[]{:S(2)}, u32[]{:S(2)}) %collective-permute-start.1) | collective-permute-done | bytes 204832 | tf_op jit(solution)/shard_map/while/body/eval_jaxpr/ppermute | solution.py:10
  266.1 18.1 %collective-permute-done.1 = f32[4,100,128]{1,0,2:T(4,128)} collective-permute-done((f32[4,100,128]{1,0,2:T(4,128)}, f32[4,100,128]{1,0,2:T(4,128)}, u32[]{:S(2)}, u32[]{:S(2)}) %collective-permute-start.1) | collective-permute-done | bytes 204832 | tf_op jit(solution)/shard_map/while/body/eval_jaxpr/ppermute | solution.py:10
  302.9 15.9 %collective-permute-done.1 = f32[4,100,128]{1,0,2:T(4,128)} collective-permute-done((f32[4,100,128]{1,0,2:T(4,128)}, f32[4,100,128]{1,0,2:T(4,128)}, u32[]{:S(2)}, u32[]{:S(2)}) %collective-permute-start.1) | collective-permute-done | bytes 204832 | tf_op jit(solution)/shard_map/while/body/eval_jaxpr/ppermute | solution.py:10
  323.6 88.9 %collective-permute-done.1 = f32[4,100,128]{1,0,2:T(4,128)} collective-permute-done((f32[4,100,128]{1,0,2:T(4,128)}, f32[4,100,128]{1,0,2:T(4,128)}, u32[]{:S(2)}, u32[]{:S(2)}) %collective-permute-start.1) | collective-permute-done | bytes 204832 | tf_op jit(solution)/shard_map/while/body/eval_jaxpr/ppermute | solution.py:10
  416.0 11.5 %conditional.13 = (f32[4,100,128]{1,0,2:T(4,128)}) conditional(s32[]{:T(128)} %convert_element_type.268, f32[4,100,128]{1,0,2:T(4,128)} %get-tuple-element.1094, (f32[4,100,128]{1,0,2:T(4,128)}, s32[128]{0:T(128)S(1)}, bf16[3,100,100,128]{2,1,3,0:T(8,128)(2,1)}, f32[4,100,128]{1,0,2:T(4,128)}, bf16[100,100,128]{1,0,2:T(8,128)(2,1)S(1)}) %tuple.165), branch_computations={%region_5.6_spmd, %region_6.7_spmd} | conditional | flops 42498176 | bytes 11299748 | solution.py:56
  470.6 152.5 %while.78 = (s32[]{:T(128)}, f32[4,100,128]{1,0,2:T(4,128)}, f32[4,100,128]{1,0,2:T(4,128)}, s32[]{:T(128)}, s32[128]{0:T(128)S(1)}, /*index=5*/bf16[100,100,128...) while((s32[]{:T(128)}, f32[4,100,128]{1,0,2:T(4,128)}, ...), condition=%wide.region_11.13_spmd.clone, body=%wide.region_8.0_spmd.clone.sunk | while | flops 42651780 | bytes 12295292 | solution.py:66
  471.4 11.5 %conditional.14 = (f32[4,100,128]{1,0,2:T(4,128)}) conditional(s32[]{:T(128)} %convert_element_type.269, f32[4,100,128]{1,0,2:T(4,128)} %get-tuple-element.1124, (f32[4,100,128]{1,0,2:T(4,128)}, s32[128]{0:T(128)S(1)}, bf16[100,100,128]{1,0,2:T(8,128)(2,1)}, f32[4,100,128]{1,0,2:T(4,128)}, bf16[100,100,128]{1,0,2:T(8,128)(2,1)S(1)}) %tuple.167), branch_computations={%region_9.10_spmd, %region_10.11_spmd} | conditional | flops 42498176 | bytes 10451876 | solution.py:56
  493.3 17.5 %collective-permute-start.2 = (f32[4,100,128]{1,0,2:T(4,128)}, f32[4,100,128]{1,0,2:T(4,128)}, u32[]{:S(2)}, u32[]{:S(2)}) collective-permute-start(f32[4,100,128]{1,0,2:T(4,128)} %get-tuple-element.1174), channel_id=1, source_target_pairs={{0,4},{4,8},{8,12},{12,16},{16,20},{20,24},{24,28},{1,5},{5,9},{9,... | collective-permute-start | bytes 614408 | tf_op jit(solution)/shard_map/while/body/eval_jaxpr/ppermute | solution.py:10
  533.1 15.7 %collective-permute-start.2 = (f32[4,100,128]{1,0,2:T(4,128)}, f32[4,100,128]{1,0,2:T(4,128)}, u32[]{:S(2)}, u32[]{:S(2)}) collective-permute-start(f32[4,100,128]{1,0,2:T(4,128)} %get-tuple-element.1174), channel_id=1, source_target_pairs={{0,4},{4,8},{8,12},{12,16},{16,20},{20,24},{24,28},{1,5},{5,9},{9,... | collective-permute-start | bytes 614408 | tf_op jit(solution)/shard_map/while/body/eval_jaxpr/ppermute | solution.py:10
  569.3 13.9 %collective-permute-start.2 = (f32[4,100,128]{1,0,2:T(4,128)}, f32[4,100,128]{1,0,2:T(4,128)}, u32[]{:S(2)}, u32[]{:S(2)}) collective-permute-start(f32[4,100,128]{1,0,2:T(4,128)} %get-tuple-element.1174), channel_id=1, source_target_pairs={{0,4},{4,8},{8,12},{12,16},{16,20},{20,24},{24,28},{1,5},{5,9},{9,... | collective-permute-start | bytes 614408 | tf_op jit(solution)/shard_map/while/body/eval_jaxpr/ppermute | solution.py:10
  603.1 14.8 %collective-permute-start.2 = (f32[4,100,128]{1,0,2:T(4,128)}, f32[4,100,128]{1,0,2:T(4,128)}, u32[]{:S(2)}, u32[]{:S(2)}) collective-permute-start(f32[4,100,128]{1,0,2:T(4,128)} %get-tuple-element.1174), channel_id=1, source_target_pairs={{0,4},{4,8},{8,12},{12,16},{16,20},{20,24},{24,28},{1,5},{5,9},{9,... | collective-permute-start | bytes 614408 | tf_op jit(solution)/shard_map/while/body/eval_jaxpr/ppermute | solution.py:10
  655.9 227.3 %while.79 = (s32[]{:T(128)}, f32[4,100,128]{1,0,2:T(4,128)}, f32[4,100,128]{1,0,2:T(4,128)}, s32[]{:T(128)}, s32[128]{0:T(128)S(1)}, /*index=5*/bf16[3,100,100,1...) while((s32[]{:T(128)}, f32[4,100,128]{1,0,2:T(4,128)}, ...), condition=%wide.region_15.17_spmd.clone, body=%wide.region_12.0_spmd.clone.sunk | while | flops 42651780 | bytes 13143164 | solution.py:66
  672.9 18.6 %collective-permute-done.3 = f32[4,100,128]{1,0,2:T(4,128)} collective-permute-done((f32[4,100,128]{1,0,2:T(4,128)}, f32[4,100,128]{1,0,2:T(4,128)}, u32[]{:S(2)}, u32[]{:S(2)}) %collective-permute-start.3) | collective-permute-done | bytes 204832 | tf_op jit(solution)/shard_map/while/body/eval_jaxpr/ppermute | solution.py:10
  711.4 18.1 %collective-permute-done.3 = f32[4,100,128]{1,0,2:T(4,128)} collective-permute-done((f32[4,100,128]{1,0,2:T(4,128)}, f32[4,100,128]{1,0,2:T(4,128)}, u32[]{:S(2)}, u32[]{:S(2)}) %collective-permute-start.3) | collective-permute-done | bytes 204832 | tf_op jit(solution)/shard_map/while/body/eval_jaxpr/ppermute | solution.py:10
  748.3 15.9 %collective-permute-done.3 = f32[4,100,128]{1,0,2:T(4,128)} collective-permute-done((f32[4,100,128]{1,0,2:T(4,128)}, f32[4,100,128]{1,0,2:T(4,128)}, u32[]{:S(2)}, u32[]{:S(2)}) %collective-permute-start.3) | collective-permute-done | bytes 204832 | tf_op jit(solution)/shard_map/while/body/eval_jaxpr/ppermute | solution.py:10
  769.0 88.9 %collective-permute-done.3 = f32[4,100,128]{1,0,2:T(4,128)} collective-permute-done((f32[4,100,128]{1,0,2:T(4,128)}, f32[4,100,128]{1,0,2:T(4,128)}, u32[]{:S(2)}, u32[]{:S(2)}) %collective-permute-start.3) | collective-permute-done | bytes 204832 | tf_op jit(solution)/shard_map/while/body/eval_jaxpr/ppermute | solution.py:10
  (302 shorter events, 476.0 us)
Async XLA Ops:
  35.5 22.7 %collective-permute-start = (f32[4,100,128]{1,0,2:T(4,128)}, f32[4,100,128]{1,0,2:T(4,128)}, u32[]{:S(2)}, u32[]{:S(2)}) collective-permute-start(f32[4,100,128]{1,0,2:T(4,128)} %get-tuple-element.1172), channel_id=1, source_target_pairs={{0,4},{4,8},{8,12},{12,16},{16,20},{20,24},{24,28},{1,5},{5,9},{9,... | collective-permute-start | bytes 614408 | tf_op jit(solution)/shard_map/while/body/eval_jaxpr/ppermute | solution.py:10
  74.6 19.4 %collective-permute-start = (f32[4,100,128]{1,0,2:T(4,128)}, f32[4,100,128]{1,0,2:T(4,128)}, u32[]{:S(2)}, u32[]{:S(2)}) collective-permute-start(f32[4,100,128]{1,0,2:T(4,128)} %get-tuple-element.1172), channel_id=1, source_target_pairs={{0,4},{4,8},{8,12},{12,16},{16,20},{20,24},{24,28},{1,5},{5,9},{9,... | collective-permute-start | bytes 614408 | tf_op jit(solution)/shard_map/while/body/eval_jaxpr/ppermute | solution.py:10
  110.4 17.4 %collective-permute-start = (f32[4,100,128]{1,0,2:T(4,128)}, f32[4,100,128]{1,0,2:T(4,128)}, u32[]{:S(2)}, u32[]{:S(2)}) collective-permute-start(f32[4,100,128]{1,0,2:T(4,128)} %get-tuple-element.1172), channel_id=1, source_target_pairs={{0,4},{4,8},{8,12},{12,16},{16,20},{20,24},{24,28},{1,5},{5,9},{9,... | collective-permute-start | bytes 614408 | tf_op jit(solution)/shard_map/while/body/eval_jaxpr/ppermute | solution.py:10
  144.1 18.0 %collective-permute-start = (f32[4,100,128]{1,0,2:T(4,128)}, f32[4,100,128]{1,0,2:T(4,128)}, u32[]{:S(2)}, u32[]{:S(2)}) collective-permute-start(f32[4,100,128]{1,0,2:T(4,128)} %get-tuple-element.1172), channel_id=1, source_target_pairs={{0,4},{4,8},{8,12},{12,16},{16,20},{20,24},{24,28},{1,5},{5,9},{9,... | collective-permute-start | bytes 614408 | tf_op jit(solution)/shard_map/while/body/eval_jaxpr/ppermute | solution.py:10
  163.8 27.3 %collective-permute-start.4 = (f32[1,1,4,100,128]{3,2,4,1,0:T(4,128)}, f32[1,1,4,100,128]{3,2,4,1,0:T(4,128)}, u32[]{:S(2)}, u32[]{:S(2)}) collective-permute-start(f32[1,1,4,100,128]{3,2,4,1,0:T(4,128)} %bitcast.193), channel_id=1, source_target_pairs={{0,1},{1,2},{2,3},{4,5},{5,6},{6,7},{8,9},{9,10},{10,11},{12,13},{... | collective-permute-start | bytes 614408 | tf_op jit(solution)/shard_map/ppermute | solution.py:21
  165.8 30.7 %collective-permute-start.5 = (f32[1,1,4,100,128]{3,2,4,1,0:T(4,128)}, f32[1,1,4,100,128]{3,2,4,1,0:T(4,128)}, u32[]{:S(2)}, u32[]{:S(2)}) collective-permute-start(f32[1,1,4,100,128]{3,2,4,1,0:T(4,128)} %bitcast.194), channel_id=1, source_target_pairs={{1,0},{2,1},{3,2},{5,4},{6,5},{7,6},{9,8},{10,9},{11,10},{13,12},{... | collective-permute-start | bytes 614408 | tf_op jit(solution)/shard_map/ppermute | solution.py:23
  211.5 12.4 %collective-permute-start.1 = (f32[4,100,128]{1,0,2:T(4,128)}, f32[4,100,128]{1,0,2:T(4,128)}, u32[]{:S(2)}, u32[]{:S(2)}) collective-permute-start(f32[4,100,128]{1,0,2:T(4,128)} %get-tuple-element.1173), channel_id=1, source_target_pairs={{4,0},{8,4},{12,8},{16,12},{20,16},{24,20},{28,24},{5,1},{9,5},{13... | collective-permute-start | bytes 614408 | tf_op jit(solution)/shard_map/while/body/eval_jaxpr/ppermute | solution.py:10
  226.4 19.7 %collective-permute-start.1 = (f32[4,100,128]{1,0,2:T(4,128)}, f32[4,100,128]{1,0,2:T(4,128)}, u32[]{:S(2)}, u32[]{:S(2)}) collective-permute-start(f32[4,100,128]{1,0,2:T(4,128)} %get-tuple-element.1173), channel_id=1, source_target_pairs={{4,0},{8,4},{12,8},{16,12},{20,16},{24,20},{28,24},{5,1},{9,5},{13... | collective-permute-start | bytes 614408 | tf_op jit(solution)/shard_map/while/body/eval_jaxpr/ppermute | solution.py:10
  264.8 19.4 %collective-permute-start.1 = (f32[4,100,128]{1,0,2:T(4,128)}, f32[4,100,128]{1,0,2:T(4,128)}, u32[]{:S(2)}, u32[]{:S(2)}) collective-permute-start(f32[4,100,128]{1,0,2:T(4,128)} %get-tuple-element.1173), channel_id=1, source_target_pairs={{4,0},{8,4},{12,8},{16,12},{20,16},{24,20},{28,24},{5,1},{9,5},{13... | collective-permute-start | bytes 614408 | tf_op jit(solution)/shard_map/while/body/eval_jaxpr/ppermute | solution.py:10
  301.6 17.2 %collective-permute-start.1 = (f32[4,100,128]{1,0,2:T(4,128)}, f32[4,100,128]{1,0,2:T(4,128)}, u32[]{:S(2)}, u32[]{:S(2)}) collective-permute-start(f32[4,100,128]{1,0,2:T(4,128)} %get-tuple-element.1173), channel_id=1, source_target_pairs={{4,0},{8,4},{12,8},{16,12},{20,16},{24,20},{28,24},{5,1},{9,5},{13... | collective-permute-start | bytes 614408 | tf_op jit(solution)/shard_map/while/body/eval_jaxpr/ppermute | solution.py:10
  322.3 90.2 %collective-permute-start.1 = (f32[4,100,128]{1,0,2:T(4,128)}, f32[4,100,128]{1,0,2:T(4,128)}, u32[]{:S(2)}, u32[]{:S(2)}) collective-permute-start(f32[4,100,128]{1,0,2:T(4,128)} %get-tuple-element.1173), channel_id=1, source_target_pairs={{4,0},{8,4},{12,8},{16,12},{20,16},{24,20},{28,24},{5,1},{9,5},{13... | collective-permute-start | bytes 614408 | tf_op jit(solution)/shard_map/while/body/eval_jaxpr/ppermute | solution.py:10
  437.8 12.9 %collective-permute-start.6 = (f32[1,1,4,100,128]{3,2,4,1,0:T(4,128)}, f32[1,1,4,100,128]{3,2,4,1,0:T(4,128)}, u32[]{:S(2)}, u32[]{:S(2)}) collective-permute-start(f32[1,1,4,100,128]{3,2,4,1,0:T(4,128)} %bitcast.195), channel_id=1, source_target_pairs={{0,1},{1,2},{2,3},{4,5},{5,6},{6,7},{8,9},{9,10},{10,11},{12,13},{... | collective-permute-start | bytes 614408 | tf_op jit(solution)/shard_map/ppermute | solution.py:21
  439.8 20.4 %collective-permute-start.7 = (f32[1,1,4,100,128]{3,2,4,1,0:T(4,128)}, f32[1,1,4,100,128]{3,2,4,1,0:T(4,128)}, u32[]{:S(2)}, u32[]{:S(2)}) collective-permute-start(f32[1,1,4,100,128]{3,2,4,1,0:T(4,128)} %bitcast.196), channel_id=1, source_target_pairs={{1,0},{2,1},{3,2},{5,4},{6,5},{7,6},{9,8},{10,9},{11,10},{13,12},{... | collective-permute-start | bytes 614408 | tf_op jit(solution)/shard_map/ppermute | solution.py:23
  493.3 23.1 %collective-permute-start.2 = (f32[4,100,128]{1,0,2:T(4,128)}, f32[4,100,128]{1,0,2:T(4,128)}, u32[]{:S(2)}, u32[]{:S(2)}) collective-permute-start(f32[4,100,128]{1,0,2:T(4,128)} %get-tuple-element.1174), channel_id=1, source_target_pairs={{0,4},{4,8},{8,12},{12,16},{16,20},{20,24},{24,28},{1,5},{5,9},{9,... | collective-permute-start | bytes 614408 | tf_op jit(solution)/shard_map/while/body/eval_jaxpr/ppermute | solution.py:10
  533.1 19.8 %collective-permute-start.2 = (f32[4,100,128]{1,0,2:T(4,128)}, f32[4,100,128]{1,0,2:T(4,128)}, u32[]{:S(2)}, u32[]{:S(2)}) collective-permute-start(f32[4,100,128]{1,0,2:T(4,128)} %get-tuple-element.1174), channel_id=1, source_target_pairs={{0,4},{4,8},{8,12},{12,16},{16,20},{20,24},{24,28},{1,5},{5,9},{9,... | collective-permute-start | bytes 614408 | tf_op jit(solution)/shard_map/while/body/eval_jaxpr/ppermute | solution.py:10
  569.3 17.4 %collective-permute-start.2 = (f32[4,100,128]{1,0,2:T(4,128)}, f32[4,100,128]{1,0,2:T(4,128)}, u32[]{:S(2)}, u32[]{:S(2)}) collective-permute-start(f32[4,100,128]{1,0,2:T(4,128)} %get-tuple-element.1174), channel_id=1, source_target_pairs={{0,4},{4,8},{8,12},{12,16},{16,20},{20,24},{24,28},{1,5},{5,9},{9,... | collective-permute-start | bytes 614408 | tf_op jit(solution)/shard_map/while/body/eval_jaxpr/ppermute | solution.py:10
  603.1 18.3 %collective-permute-start.2 = (f32[4,100,128]{1,0,2:T(4,128)}, f32[4,100,128]{1,0,2:T(4,128)}, u32[]{:S(2)}, u32[]{:S(2)}) collective-permute-start(f32[4,100,128]{1,0,2:T(4,128)} %get-tuple-element.1174), channel_id=1, source_target_pairs={{0,4},{4,8},{8,12},{12,16},{16,20},{20,24},{24,28},{1,5},{5,9},{9,... | collective-permute-start | bytes 614408 | tf_op jit(solution)/shard_map/while/body/eval_jaxpr/ppermute | solution.py:10
  623.1 13.0 %collective-permute-start.8 = (f32[1,1,4,100,128]{3,2,4,1,0:T(4,128)}, f32[1,1,4,100,128]{3,2,4,1,0:T(4,128)}, u32[]{:S(2)}, u32[]{:S(2)}) collective-permute-start(f32[1,1,4,100,128]{3,2,4,1,0:T(4,128)} %bitcast.197), channel_id=1, source_target_pairs={{0,1},{1,2},{2,3},{4,5},{5,6},{6,7},{8,9},{9,10},{10,11},{12,13},{... | collective-permute-start | bytes 614408 | tf_op jit(solution)/shard_map/ppermute | solution.py:21
  625.1 20.5 %collective-permute-start.9 = (f32[1,1,4,100,128]{3,2,4,1,0:T(4,128)}, f32[1,1,4,100,128]{3,2,4,1,0:T(4,128)}, u32[]{:S(2)}, u32[]{:S(2)}) collective-permute-start(f32[1,1,4,100,128]{3,2,4,1,0:T(4,128)} %bitcast.198), channel_id=1, source_target_pairs={{1,0},{2,1},{3,2},{5,4},{6,5},{7,6},{9,8},{10,9},{11,10},{13,12},{... | collective-permute-start | bytes 614408 | tf_op jit(solution)/shard_map/ppermute | solution.py:23
  656.7 12.4 %collective-permute-start.3 = (f32[4,100,128]{1,0,2:T(4,128)}, f32[4,100,128]{1,0,2:T(4,128)}, u32[]{:S(2)}, u32[]{:S(2)}) collective-permute-start(f32[4,100,128]{1,0,2:T(4,128)} %get-tuple-element.1175), channel_id=1, source_target_pairs={{4,0},{8,4},{12,8},{16,12},{20,16},{24,20},{28,24},{5,1},{9,5},{13... | collective-permute-start | bytes 614408 | tf_op jit(solution)/shard_map/while/body/eval_jaxpr/ppermute | solution.py:10
  671.6 19.8 %collective-permute-start.3 = (f32[4,100,128]{1,0,2:T(4,128)}, f32[4,100,128]{1,0,2:T(4,128)}, u32[]{:S(2)}, u32[]{:S(2)}) collective-permute-start(f32[4,100,128]{1,0,2:T(4,128)} %get-tuple-element.1175), channel_id=1, source_target_pairs={{4,0},{8,4},{12,8},{16,12},{20,16},{24,20},{28,24},{5,1},{9,5},{13... | collective-permute-start | bytes 614408 | tf_op jit(solution)/shard_map/while/body/eval_jaxpr/ppermute | solution.py:10
  710.1 19.4 %collective-permute-start.3 = (f32[4,100,128]{1,0,2:T(4,128)}, f32[4,100,128]{1,0,2:T(4,128)}, u32[]{:S(2)}, u32[]{:S(2)}) collective-permute-start(f32[4,100,128]{1,0,2:T(4,128)} %get-tuple-element.1175), channel_id=1, source_target_pairs={{4,0},{8,4},{12,8},{16,12},{20,16},{24,20},{28,24},{5,1},{9,5},{13... | collective-permute-start | bytes 614408 | tf_op jit(solution)/shard_map/while/body/eval_jaxpr/ppermute | solution.py:10
  747.0 17.2 %collective-permute-start.3 = (f32[4,100,128]{1,0,2:T(4,128)}, f32[4,100,128]{1,0,2:T(4,128)}, u32[]{:S(2)}, u32[]{:S(2)}) collective-permute-start(f32[4,100,128]{1,0,2:T(4,128)} %get-tuple-element.1175), channel_id=1, source_target_pairs={{4,0},{8,4},{12,8},{16,12},{20,16},{24,20},{28,24},{5,1},{9,5},{13... | collective-permute-start | bytes 614408 | tf_op jit(solution)/shard_map/while/body/eval_jaxpr/ppermute | solution.py:10
  767.7 90.2 %collective-permute-start.3 = (f32[4,100,128]{1,0,2:T(4,128)}, f32[4,100,128]{1,0,2:T(4,128)}, u32[]{:S(2)}, u32[]{:S(2)}) collective-permute-start(f32[4,100,128]{1,0,2:T(4,128)} %get-tuple-element.1175), channel_id=1, source_target_pairs={{4,0},{8,4},{12,8},{16,12},{20,16},{24,20},{28,24},{5,1},{9,5},{13... | collective-permute-start | bytes 614408 | tf_op jit(solution)/shard_map/while/body/eval_jaxpr/ppermute | solution.py:10
  (35 other events, 816.4 us)
where the time goes:
time: 890 us; the launch traced here: 885 us
  waiting for transfers between devices  426 us (48%)
  starting transfers between devices  192 us (22%)
  other arithmetic  142 us (16%)
  local copies, waits for them, and re-layouts  61.8 us (7%)
  matrix products  61.2 us (7%)
    ppermute x32, waiting for transfers between devices, passed_along(): return lax.ppermute(block, axis, route)  426 us
    ppermute x32, starting transfers between devices, passed_along(): return lax.ppermute(block, axis, route)  182 us
    dot_general x17, matrix products, product(): jnp.einsum('ijm,kjm->kim', block, stacked, preferred_element_type=jnp.flo...  61.2 us
    select_n x32, other arithmetic, section(): incoming = jnp.where(order_rank == section_no + 1, received, incoming)  52.2 us
    while x32, other arithmetic  51.1 us
    gather x13, local copies, waits for them, and re-layouts, select(): return jnp.take(field, columns, axis=2)  31.7 us
    unnamed x38, local copies, waits for them, and re-layouts  25.3 us
  transfers between devices with their start and end apart: 38, of which 32 were waited for; matrix products, arithmetic and copies ran while one was open for 8% of the time, Pallas kernels for 0%

commit v1 on v0

v1 whole, which is shorter than its diff:
```python
import functools

import jax
import jax.numpy as jnp
from jax import lax
from jax.experimental import pallas as pl
from jax.experimental.pallas import tpu as pltpu
from jax.sharding import PartitionSpec as P

LANES = 128
SUBLANES = 8
VMEM_LIMIT = 16 * 1024 * 1024


def product(matrix, vector, rows, unroll=10):
    count = matrix.shape[0]

    def body(step, total):
        for inner in range(unroll):
            j = step * unroll + inner
            total = total + matrix[j] * vector[pl.ds(j, 1), :]
        return total

    start = jnp.zeros((rows, matrix.shape[2]), jnp.float32)
    return lax.fori_loop(0, count // unroll, body, start)


def gathered(value, columns):
    index = jnp.broadcast_to(columns, value.shape)
    return jnp.take_along_axis(value, index, axis=1, mode="promise_in_bounds")


def lateral_sum(left, right, from_left, from_right, index, spare):
    rows = spare.shape[0]
    spare[...] = gathered(from_left[...], index[2:3, :])
    total = product(left, spare, rows)
    spare[...] = gathered(from_right[...], index[3:4, :])
    return total + product(right, spare, rows)


def task_kernel(
    flags, diag, up, down, left, right, index, source, incoming, from_left, from_right, chain_in, side_in,
    value, chain, side, spare
):
    rows = spare.shape[0]
    vector = flags[1]

    @pl.when(flags[5] == 1)
    def _():
        side[flags[7]] = lateral_sum(left, right, from_left, from_right, index, spare)

    @pl.when(flags[0] == 1)
    def _():
        base = source[vector] - chain[vector] - side[vector]
        value[...] = base
        chain[vector] = jnp.zeros_like(base)

        def take_chain(matrix, row):
            spare[...] = gathered(incoming[...], index[row : row + 1, :])
            term = product(matrix, spare, rows)
            chain[vector] = term
            value[...] = value[...] - term

        @pl.when((flags[2] == 1) & (flags[3] == 1))
        def _():
            take_chain(up, 0)

        @pl.when((flags[2] == 1) & (flags[3] == 0))
        def _():
            take_chain(down, 1)

        spare[...] = value[...]
        value[...] = product(diag, spare, rows)


def side_kernel(flags, left, right, index, from_left, from_right, side_in, side, spare):
    @pl.when(flags[6] == 1)
    def _():
        side[flags[7]] = lateral_sum(left, right, from_left, from_right, index, spare)


def in_vmem(count):
    return [pl.BlockSpec(memory_space=pltpu.VMEM)] * count


def run_task(flags, mats, index, source, incoming, sides, chain, side):
    shape = incoming.shape
    return pl.pallas_call(
        task_kernel,
        out_shape=(
            pltpu.VMEM(shape, jnp.float32),
            pltpu.VMEM(chain.shape, jnp.float32),
            pltpu.VMEM(side.shape, jnp.float32),
        ),
        in_specs=[pl.BlockSpec(memory_space=pltpu.SMEM)] + in_vmem(12),
        out_specs=tuple(in_vmem(3)),
        scratch_shapes=[pltpu.VMEM(shape, jnp.float32)],
        input_output_aliases={11: 1, 12: 2},
        compiler_params=pltpu.CompilerParams(vmem_limit_bytes=VMEM_LIMIT),
        name="task",
    )(flags, *mats, index, source, incoming, *sides, chain, side)


def run_side(flags, mats, index, sides, side):
    shape = sides[0].shape
    return pl.pallas_call(
        side_kernel,
        out_shape=pltpu.VMEM(side.shape, jnp.float32),
        in_specs=[pl.BlockSpec(memory_space=pltpu.SMEM)] + in_vmem(6),
        out_specs=pl.BlockSpec(memory_space=pltpu.VMEM),
        scratch_shapes=[pltpu.VMEM(shape, jnp.float32)],
        input_output_aliases={6: 0},
        compiler_params=pltpu.CompilerParams(vmem_limit_bytes=VMEM_LIMIT),
        name="side",
    )(flags, mats[3], mats[4], index, *sides, side)


def turned(block):
    padded = -block.shape[0] % SUBLANES
    out = jnp.pad(jnp.transpose(block, (1, 0, 2)), ((0, 0), (0, padded), (0, 0))).astype(jnp.float32)
    return pltpu.with_memory_space_constraint(out, pltpu.VMEM)


def at_tick(tick, place, count, vectors):
    forward = lax.rem(tick - place + 2 * count, 2) == 0
    rank = jnp.where(forward, place, count - 1 - place)
    since = jnp.where(forward, tick - place, tick - rank - count)
    late = since >= 2 * count
    since = jnp.where(late, since - 2 * count, since)
    active = (since >= 0) & (since < 2 * vectors)
    vector = jnp.clip(since // 2, 0, vectors - 1)
    half = jnp.where(forward, 0, 1) + jnp.where(late, 2, 0)
    return active, vector, rank, forward, half


def per_device(
    residual_in, diag_inverse, up_block, side_blocks, up_cols, down_cols, left_cols, right_cols
):
    source = residual_in[0, 0]
    vectors, size, _ = source.shape
    rows = size + -size % SUBLANES
    source = jnp.pad(source, ((0, 0), (0, rows - size), (0, 0)))
    mats = tuple(
        turned(block)
        for block in (
            diag_inverse[0, 0], up_block[0, 0], side_blocks[0, 0, 0], side_blocks[0, 0, 1], side_blocks[0, 0, 2]
        )
    )
    index = jnp.stack([up_cols[0, 0], down_cols[0, 0], left_cols[0, 0], right_cols[0, 0]])
    place = lax.axis_index("sweep")
    count = lax.axis_size("sweep")
    parts = lax.axis_size("span")
    ticks = 4 * count + 2 * (vectors - 1)

    def one_tick(tick, parity, state):
        incoming, from_left, from_right, chain, side, out = state
        active, vector, rank, forward, half = at_tick(tick, place, count, vectors)
        was_active, was_vector, _, _, was_half = at_tick(tick - 1, place, count, vectors)
        crossing = was_active & (was_half < 3)
        first = crossing & active & (rank == 0) & (half > 0) & (vector == was_vector)
        flags = jnp.stack(
            [
                jnp.where(flag, 1, 0) if flag.dtype == jnp.bool_ else flag
                for flag in (
                    active, vector, rank > 0, forward, half == 3, first, crossing & ~first, was_vector
                )
            ]
        ).astype(jnp.int32)
        value, chain, side = run_task(
            flags, mats, index, source, incoming, (from_left, from_right), chain, side
        )
        swap = [(s, s + 1) for s in range(parity, count - 1, 2)]
        incoming = lax.ppermute(value, "sweep", swap + [(b, a) for a, b in swap])
        new_left = lax.ppermute(value, "span", [(p, p + 1) for p in range(parts - 1)])
        new_right = lax.ppermute(value, "span", [(p + 1, p) for p in range(parts - 1)])
        side = run_side(flags, mats, index, (from_left, from_right), side)
        out = jnp.where(
            (active & (half == 3) & (jnp.arange(vectors) == vector))[:, None, None], value[:size], out
        )
        return incoming, new_left, new_right, chain, side, out

    def two_ticks(pair, state):
        state = one_tick(2 * pair, 0, state)
        return one_tick(2 * pair + 1, 1, state)

    single = jnp.zeros((rows, LANES), jnp.float32)
    several = jnp.zeros((vectors, rows, LANES), jnp.float32)
    state = (single, single, single, several, several, jnp.zeros_like(residual_in[0, 0]))
    state = lax.fori_loop(0, ticks // 2, two_ticks, state)
    return state[5][None, None]


def solution(mesh):
    return jax.shard_map(
        per_device,
        mesh=mesh,
        in_specs=(
            P("sweep", "span", None, None, None),
            P("sweep", "span", None, None, None),
            P("sweep", "span", None, None, None),
            P("sweep", "span", None, None, None, None),
            P("sweep", "span", None),
            P("sweep", "span", None),
            P("sweep", "span", None),
            P("sweep", "span", None),
        ),
        out_specs=P("sweep", "span", None, None, None),
        check_vma=False,
    )
```

time: 890 us -> 1010 us (1.13)
  local copies, waits for them, and re-layouts: 61.8 us -> 583 us
  waiting for transfers between devices: 426 us -> 33.7 us
  other arithmetic: 142 us -> 14.6 us
  starting transfers between devices: 192 us -> 294 us
  Pallas kernels: 0 us -> 64.7 us
  matrix products: 61.2 us -> 0 us
    while x1 -> x457, local copies, waits for them, and re-layouts: 1.77 us -> 573 us  [chain_whole(): incoming, result = lax.fori_loop(0, slab_count, section, (empty, empty))]
    ppermute x38 -> x114, waiting for transfers between devices: 426 us -> 33.7 us  [the longest x38 33.5 us: one_tick(): lax.ppermute(value, 'span', [(p + 1, p) for p in range(parts - 1)])]
    ppermute x38 -> x114, starting transfers between devices: 192 us -> 294 us  [the longest x38 140 us: one_tick(): lax.ppermute(value, 'span', [(p, p + 1) for p in range(parts - 1)])]
    pallas_call x0 -> x76, Pallas kernels: none -> 64.7 us  [the longest x38 35.9 us: run_task(): pl.pallas_call(task_kernel, out_shape=(pltpu.VMEM(shape, jnp.float32), pl...]
    dot_general x17 -> x0, matrix products: 61.2 us -> none  [product(): jnp.einsum('ijm,kjm->kim', block, stacked, preferred_element_type=jnp.flo...]
    while x32 -> x0, other arithmetic: 51.1 us -> none
    select_n x40 -> x19, other arithmetic: 52.2 us -> 1.84 us  [one_tick(): jnp.where((active & (half == 3) & (jnp.arange(vectors) == vector))[:, Non...]
    gather x13 -> x0, local copies, waits for them, and re-layouts: 31.7 us -> none  [select(): return jnp.take(field, columns, axis=2)]
  transfers between devices with their start and end apart: 38 -> 114, of which waited for: 32 -> 19; matrix products, arithmetic and copies ran while one was open for 8% -> 0% of each run, Pallas kernels for 0% -> 3%
where the time goes in v1:
time: 1010 us; the launch traced here: 996 us
  local copies, waits for them, and re-layouts  583 us (58%)
  starting transfers between devices  294 us (29%)
  Pallas kernels  64.7 us (6%)
  waiting for transfers between devices  33.7 us (3%)
  other arithmetic  14.6 us (1%)
    while x456, local copies, waits for them, and re-layouts  572 us
    ppermute x38, starting transfers between devices, one_tick(): lax.ppermute(value, 'span', [(p, p + 1) for p in range(parts - 1)])  140 us
    ppermute x38, starting transfers between devices, one_tick(): incoming = lax.ppermute(value, 'sweep', swap + [(b, a) for a, b in swap])  104 us
    ppermute x38, starting transfers between devices, one_tick(): lax.ppermute(value, 'span', [(p + 1, p) for p in range(parts - 1)])  49.1 us
    pallas_call x38, Pallas kernels, run_task(): pl.pallas_call(task_kernel, out_shape=(pltpu.VMEM(shape, jnp.float32), pl...  35.9 us
    ppermute x38, waiting for transfers between devices, one_tick(): lax.ppermute(value, 'span', [(p + 1, p) for p in range(parts - 1)])  33.5 us
    pallas_call x38, Pallas kernels, run_side(): pl.pallas_call(side_kernel, out_shape=pltpu.VMEM(side.shape, jnp.float32)...  28.8 us
  transfers between devices with their start and end apart: 114, of which 19 were waited for; matrix products, arithmetic and copies ran while one was open for 0% of the time, Pallas kernels for 3%

profile of v1, /device:TPU:0, one launch (start us, length us, event | category | flops | bytes accessed | tf_op | source)
XLA Modules:
  0.0 996.0 jit_solution(9516497397757227296)
XLA Ops:
  12.2 4.6 pad_convert_fusion.2
  20.1 975.1 %while.29 = (s32[]{:T(128)}, f32[104,128]{1,0:T(8,128)S(1)}, f32[104,128]{1,0:T(8,128)S(1)}, f32[104,128]{1,0:T(8,128)S(1)}, f32[4,104,128]{2,1,0:T(8,128)S(1)},...) while((s32[]{:T(128)}, f32[104,128]{1,0:T(8,128)S(1)}, ...), condition=%wide.region_1.2_spmd.clone, body=%wide.region_0.1_spmd.clone.sunk | while | flops 153779 | bytes 257382928 | solution.py:189
  58.9 4.6 collective-permute-start.4
  85.4 4.4 collective-permute-start.1
  135.5 4.4 collective-permute-start.1
  185.6 4.4 collective-permute-start.1
  231.4 5.1 collective-permute-start
  236.5 4.4 collective-permute-start.1
  282.2 5.2 collective-permute-start
  287.5 4.4 collective-permute-start.1
  333.2 5.2 collective-permute-start
  338.5 4.4 collective-permute-start.1
  384.2 10.8 %collective-permute-start = (f32[104,128]{1,0:T(8,128)S(1)}, f32[104,128]{1,0:T(8,128)S(1)}, u32[]{:S(2)}, u32[]{:S(2)}) collective-permute-start(f32[104,128]{1,0:T(8,128)S(1)} %get-tuple-element.729), channel_id=1, source_target_pairs={{0,4},{8,12},{16,20},{24,28},{4,0},{12,8},{20,16},{28,24},{1,5},{9... | collective-permute-start | bytes 159752 | tf_op jit(solution)/shard_map/while/body/eval_jaxpr/ppermute | solution.py:173
  395.0 4.4 collective-permute-start.1
  443.1 5.2 collective-permute-start
  448.4 4.4 collective-permute-start.1
  500.0 4.4 collective-permute-start.1
  651.1 4.4 collective-permute-start.1
  696.9 5.2 collective-permute-start
  747.9 5.2 collective-permute-start
  798.9 10.8 %collective-permute-start = (f32[104,128]{1,0:T(8,128)S(1)}, f32[104,128]{1,0:T(8,128)S(1)}, u32[]{:S(2)}, u32[]{:S(2)}) collective-permute-start(f32[104,128]{1,0:T(8,128)S(1)} %get-tuple-element.729), channel_id=1, source_target_pairs={{0,4},{8,12},{16,20},{24,28},{4,0},{12,8},{20,16},{28,24},{1,5},{9... | collective-permute-start | bytes 159752 | tf_op jit(solution)/shard_map/while/body/eval_jaxpr/ppermute | solution.py:173
  906.6 5.0 collective-permute-start
  911.6 4.4 collective-permute-start.1
  961.8 4.4 collective-permute-start.1
  (846 shorter events, 869.9 us)
Async XLA Ops:
  81.5 15.5 %collective-permute-start = (f32[104,128]{1,0:T(8,128)S(1)}, f32[104,128]{1,0:T(8,128)S(1)}, u32[]{:S(2)}, u32[]{:S(2)}) collective-permute-start(f32[104,128]{1,0:T(8,128)S(1)} %get-tuple-element.729), channel_id=1, source_target_pairs={{0,4},{8,12},{16,20},{24,28},{4,0},{12,8},{20,16},{28,24},{1,5},{9... | collective-permute-start | bytes 159752 | tf_op jit(solution)/shard_map/while/body/eval_jaxpr/ppermute | solution.py:173
  85.4 11.6 %collective-permute-start.1 = (f32[104,128]{1,0:T(8,128)S(1)}, f32[104,128]{1,0:T(8,128)S(1)}, u32[]{:S(2)}, u32[]{:S(2)}) collective-permute-start(f32[104,128]{1,0:T(8,128)S(1)} %get-tuple-element.729), channel_id=1, source_target_pairs={{0,1},{1,2},{2,3},{4,5},{5,6},{6,7},{8,9},{9,10},{10,11},{12,13},{... | collective-permute-start | bytes 159752 | tf_op jit(solution)/shard_map/while/body/eval_jaxpr/ppermute | solution.py:174
  131.6 15.5 %collective-permute-start = (f32[104,128]{1,0:T(8,128)S(1)}, f32[104,128]{1,0:T(8,128)S(1)}, u32[]{:S(2)}, u32[]{:S(2)}) collective-permute-start(f32[104,128]{1,0:T(8,128)S(1)} %get-tuple-element.729), channel_id=1, source_target_pairs={{0,4},{8,12},{16,20},{24,28},{4,0},{12,8},{20,16},{28,24},{1,5},{9... | collective-permute-start | bytes 159752 | tf_op jit(solution)/shard_map/while/body/eval_jaxpr/ppermute | solution.py:173
  135.5 11.6 %collective-permute-start.1 = (f32[104,128]{1,0:T(8,128)S(1)}, f32[104,128]{1,0:T(8,128)S(1)}, u32[]{:S(2)}, u32[]{:S(2)}) collective-permute-start(f32[104,128]{1,0:T(8,128)S(1)} %get-tuple-element.729), channel_id=1, source_target_pairs={{0,1},{1,2},{2,3},{4,5},{5,6},{6,7},{8,9},{9,10},{10,11},{12,13},{... | collective-permute-start | bytes 159752 | tf_op jit(solution)/shard_map/while/body/eval_jaxpr/ppermute | solution.py:174
  181.7 15.5 %collective-permute-start = (f32[104,128]{1,0:T(8,128)S(1)}, f32[104,128]{1,0:T(8,128)S(1)}, u32[]{:S(2)}, u32[]{:S(2)}) collective-permute-start(f32[104,128]{1,0:T(8,128)S(1)} %get-tuple-element.729), channel_id=1, source_target_pairs={{0,4},{8,12},{16,20},{24,28},{4,0},{12,8},{20,16},{28,24},{1,5},{9... | collective-permute-start | bytes 159752 | tf_op jit(solution)/shard_map/while/body/eval_jaxpr/ppermute | solution.py:173
  185.6 11.6 %collective-permute-start.1 = (f32[104,128]{1,0:T(8,128)S(1)}, f32[104,128]{1,0:T(8,128)S(1)}, u32[]{:S(2)}, u32[]{:S(2)}) collective-permute-start(f32[104,128]{1,0:T(8,128)S(1)} %get-tuple-element.729), channel_id=1, source_target_pairs={{0,1},{1,2},{2,3},{4,5},{5,6},{6,7},{8,9},{9,10},{10,11},{12,13},{... | collective-permute-start | bytes 159752 | tf_op jit(solution)/shard_map/while/body/eval_jaxpr/ppermute | solution.py:174
  231.4 16.7 %collective-permute-start = (f32[104,128]{1,0:T(8,128)S(1)}, f32[104,128]{1,0:T(8,128)S(1)}, u32[]{:S(2)}, u32[]{:S(2)}) collective-permute-start(f32[104,128]{1,0:T(8,128)S(1)} %get-tuple-element.729), channel_id=1, source_target_pairs={{0,4},{8,12},{16,20},{24,28},{4,0},{12,8},{20,16},{28,24},{1,5},{9... | collective-permute-start | bytes 159752 | tf_op jit(solution)/shard_map/while/body/eval_jaxpr/ppermute | solution.py:173
  236.5 11.6 %collective-permute-start.1 = (f32[104,128]{1,0:T(8,128)S(1)}, f32[104,128]{1,0:T(8,128)S(1)}, u32[]{:S(2)}, u32[]{:S(2)}) collective-permute-start(f32[104,128]{1,0:T(8,128)S(1)} %get-tuple-element.729), channel_id=1, source_target_pairs={{0,1},{1,2},{2,3},{4,5},{5,6},{6,7},{8,9},{9,10},{10,11},{12,13},{... | collective-permute-start | bytes 159752 | tf_op jit(solution)/shard_map/while/body/eval_jaxpr/ppermute | solution.py:174
  282.2 16.8 %collective-permute-start = (f32[104,128]{1,0:T(8,128)S(1)}, f32[104,128]{1,0:T(8,128)S(1)}, u32[]{:S(2)}, u32[]{:S(2)}) collective-permute-start(f32[104,128]{1,0:T(8,128)S(1)} %get-tuple-element.729), channel_id=1, source_target_pairs={{0,4},{8,12},{16,20},{24,28},{4,0},{12,8},{20,16},{28,24},{1,5},{9... | collective-permute-start | bytes 159752 | tf_op jit(solution)/shard_map/while/body/eval_jaxpr/ppermute | solution.py:173
  287.5 11.6 %collective-permute-start.1 = (f32[104,128]{1,0:T(8,128)S(1)}, f32[104,128]{1,0:T(8,128)S(1)}, u32[]{:S(2)}, u32[]{:S(2)}) collective-permute-start(f32[104,128]{1,0:T(8,128)S(1)} %get-tuple-element.729), channel_id=1, source_target_pairs={{0,1},{1,2},{2,3},{4,5},{5,6},{6,7},{8,9},{9,10},{10,11},{12,13},{... | collective-permute-start | bytes 159752 | tf_op jit(solution)/shard_map/while/body/eval_jaxpr/ppermute | solution.py:174
  333.2 16.8 %collective-permute-start = (f32[104,128]{1,0:T(8,128)S(1)}, f32[104,128]{1,0:T(8,128)S(1)}, u32[]{:S(2)}, u32[]{:S(2)}) collective-permute-start(f32[104,128]{1,0:T(8,128)S(1)} %get-tuple-element.729), channel_id=1, source_target_pairs={{0,4},{8,12},{16,20},{24,28},{4,0},{12,8},{20,16},{28,24},{1,5},{9... | collective-permute-start | bytes 159752 | tf_op jit(solution)/shard_map/while/body/eval_jaxpr/ppermute | solution.py:173
  338.5 11.6 %collective-permute-start.1 = (f32[104,128]{1,0:T(8,128)S(1)}, f32[104,128]{1,0:T(8,128)S(1)}, u32[]{:S(2)}, u32[]{:S(2)}) collective-permute-start(f32[104,128]{1,0:T(8,128)S(1)} %get-tuple-element.729), channel_id=1, source_target_pairs={{0,1},{1,2},{2,3},{4,5},{5,6},{6,7},{8,9},{9,10},{10,11},{12,13},{... | collective-permute-start | bytes 159752 | tf_op jit(solution)/shard_map/while/body/eval_jaxpr/ppermute | solution.py:174
  384.2 22.4 %collective-permute-start = (f32[104,128]{1,0:T(8,128)S(1)}, f32[104,128]{1,0:T(8,128)S(1)}, u32[]{:S(2)}, u32[]{:S(2)}) collective-permute-start(f32[104,128]{1,0:T(8,128)S(1)} %get-tuple-element.729), channel_id=1, source_target_pairs={{0,4},{8,12},{16,20},{24,28},{4,0},{12,8},{20,16},{28,24},{1,5},{9... | collective-permute-start | bytes 159752 | tf_op jit(solution)/shard_map/while/body/eval_jaxpr/ppermute | solution.py:173
  443.1 16.8 %collective-permute-start = (f32[104,128]{1,0:T(8,128)S(1)}, f32[104,128]{1,0:T(8,128)S(1)}, u32[]{:S(2)}, u32[]{:S(2)}) collective-permute-start(f32[104,128]{1,0:T(8,128)S(1)} %get-tuple-element.729), channel_id=1, source_target_pairs={{0,4},{8,12},{16,20},{24,28},{4,0},{12,8},{20,16},{28,24},{1,5},{9... | collective-permute-start | bytes 159752 | tf_op jit(solution)/shard_map/while/body/eval_jaxpr/ppermute | solution.py:173
  496.5 15.1 %collective-permute-start = (f32[104,128]{1,0:T(8,128)S(1)}, f32[104,128]{1,0:T(8,128)S(1)}, u32[]{:S(2)}, u32[]{:S(2)}) collective-permute-start(f32[104,128]{1,0:T(8,128)S(1)} %get-tuple-element.729), channel_id=1, source_target_pairs={{0,4},{8,12},{16,20},{24,28},{4,0},{12,8},{20,16},{28,24},{1,5},{9... | collective-permute-start | bytes 159752 | tf_op jit(solution)/shard_map/while/body/eval_jaxpr/ppermute | solution.py:173
  548.2 13.6 %collective-permute-start = (f32[104,128]{1,0:T(8,128)S(1)}, f32[104,128]{1,0:T(8,128)S(1)}, u32[]{:S(2)}, u32[]{:S(2)}) collective-permute-start(f32[104,128]{1,0:T(8,128)S(1)} %get-tuple-element.729), channel_id=1, source_target_pairs={{0,4},{8,12},{16,20},{24,28},{4,0},{12,8},{20,16},{28,24},{1,5},{9... | collective-permute-start | bytes 159752 | tf_op jit(solution)/shard_map/while/body/eval_jaxpr/ppermute | solution.py:173
  598.4 14.3 %collective-permute-start = (f32[104,128]{1,0:T(8,128)S(1)}, f32[104,128]{1,0:T(8,128)S(1)}, u32[]{:S(2)}, u32[]{:S(2)}) collective-permute-start(f32[104,128]{1,0:T(8,128)S(1)} %get-tuple-element.729), channel_id=1, source_target_pairs={{0,4},{8,12},{16,20},{24,28},{4,0},{12,8},{20,16},{28,24},{1,5},{9... | collective-permute-start | bytes 159752 | tf_op jit(solution)/shard_map/while/body/eval_jaxpr/ppermute | solution.py:173
  647.0 15.8 %collective-permute-start = (f32[104,128]{1,0:T(8,128)S(1)}, f32[104,128]{1,0:T(8,128)S(1)}, u32[]{:S(2)}, u32[]{:S(2)}) collective-permute-start(f32[104,128]{1,0:T(8,128)S(1)} %get-tuple-element.729), channel_id=1, source_target_pairs={{0,4},{8,12},{16,20},{24,28},{4,0},{12,8},{20,16},{28,24},{1,5},{9... | collective-permute-start | bytes 159752 | tf_op jit(solution)/shard_map/while/body/eval_jaxpr/ppermute | solution.py:173
  696.9 16.8 %collective-permute-start = (f32[104,128]{1,0:T(8,128)S(1)}, f32[104,128]{1,0:T(8,128)S(1)}, u32[]{:S(2)}, u32[]{:S(2)}) collective-permute-start(f32[104,128]{1,0:T(8,128)S(1)} %get-tuple-element.729), channel_id=1, source_target_pairs={{0,4},{8,12},{16,20},{24,28},{4,0},{12,8},{20,16},{28,24},{1,5},{9... | collective-permute-start | bytes 159752 | tf_op jit(solution)/shard_map/while/body/eval_jaxpr/ppermute | solution.py:173
  747.9 16.8 %collective-permute-start = (f32[104,128]{1,0:T(8,128)S(1)}, f32[104,128]{1,0:T(8,128)S(1)}, u32[]{:S(2)}, u32[]{:S(2)}) collective-permute-start(f32[104,128]{1,0:T(8,128)S(1)} %get-tuple-element.729), channel_id=1, source_target_pairs={{0,4},{8,12},{16,20},{24,28},{4,0},{12,8},{20,16},{28,24},{1,5},{9... | collective-permute-start | bytes 159752 | tf_op jit(solution)/shard_map/while/body/eval_jaxpr/ppermute | solution.py:173
  798.9 22.4 %collective-permute-start = (f32[104,128]{1,0:T(8,128)S(1)}, f32[104,128]{1,0:T(8,128)S(1)}, u32[]{:S(2)}, u32[]{:S(2)}) collective-permute-start(f32[104,128]{1,0:T(8,128)S(1)} %get-tuple-element.729), channel_id=1, source_target_pairs={{0,4},{8,12},{16,20},{24,28},{4,0},{12,8},{20,16},{28,24},{1,5},{9... | collective-permute-start | bytes 159752 | tf_op jit(solution)/shard_map/while/body/eval_jaxpr/ppermute | solution.py:173
  856.4 15.1 %collective-permute-start = (f32[104,128]{1,0:T(8,128)S(1)}, f32[104,128]{1,0:T(8,128)S(1)}, u32[]{:S(2)}, u32[]{:S(2)}) collective-permute-start(f32[104,128]{1,0:T(8,128)S(1)} %get-tuple-element.729), channel_id=1, source_target_pairs={{0,4},{8,12},{16,20},{24,28},{4,0},{12,8},{20,16},{28,24},{1,5},{9... | collective-permute-start | bytes 159752 | tf_op jit(solution)/shard_map/while/body/eval_jaxpr/ppermute | solution.py:173
  906.6 16.6 %collective-permute-start = (f32[104,128]{1,0:T(8,128)S(1)}, f32[104,128]{1,0:T(8,128)S(1)}, u32[]{:S(2)}, u32[]{:S(2)}) collective-permute-start(f32[104,128]{1,0:T(8,128)S(1)} %get-tuple-element.729), channel_id=1, source_target_pairs={{0,4},{8,12},{16,20},{24,28},{4,0},{12,8},{20,16},{28,24},{1,5},{9... | collective-permute-start | bytes 159752 | tf_op jit(solution)/shard_map/while/body/eval_jaxpr/ppermute | solution.py:173
  958.3 15.1 %collective-permute-start = (f32[104,128]{1,0:T(8,128)S(1)}, f32[104,128]{1,0:T(8,128)S(1)}, u32[]{:S(2)}, u32[]{:S(2)}) collective-permute-start(f32[104,128]{1,0:T(8,128)S(1)} %get-tuple-element.729), channel_id=1, source_target_pairs={{0,4},{8,12},{16,20},{24,28},{4,0},{12,8},{20,16},{28,24},{1,5},{9... | collective-permute-start | bytes 159752 | tf_op jit(solution)/shard_map/while/body/eval_jaxpr/ppermute | solution.py:173
  (325 other events, 1188.1 us)

commit v2 on v1

v2 whole, which is shorter than its diff:
```python
import functools

import jax
import jax.numpy as jnp
from jax import lax
from jax.experimental import pallas as pl
from jax.experimental.pallas import tpu as pltpu
from jax.sharding import PartitionSpec as P

LANES = 128
SUBLANES = 8
VMEM_LIMIT = 8 * 1024 * 1024


def product(matrix, vector, rows, unroll=10):
    count = matrix.shape[0]

    def body(step, total):
        for inner in range(unroll):
            j = step * unroll + inner
            total = total + matrix[j] * vector[pl.ds(j, 1), :]
        return total

    start = jnp.zeros((rows, matrix.shape[2]), jnp.float32)
    return lax.fori_loop(0, count // unroll, body, start)


def gathered(value, columns):
    index = jnp.broadcast_to(columns, value.shape)
    return jnp.take_along_axis(value, index, axis=1, mode="promise_in_bounds")


def lateral_sum(flags, left, right, from_left, from_right, index, spare, slot):
    rows = spare.shape[0]
    spare[...] = gathered(from_left[slot], index[2:3, :])
    total = product(left, spare, rows)
    total = jnp.where(flags[8] == 1, total, 0.0)
    spare[...] = gathered(from_right[slot], index[3:4, :])
    return total + jnp.where(flags[9] == 1, product(right, spare, rows), 0.0)


def task_kernel(
    flags, index, source, incoming, from_left, from_right,
    diag_in, up_in, down_in, left_in, right_in, pair_in, chain_in, side_in,
    value, diag, up, down, left, right, pair, chain, side, spare
):
    rows = spare.shape[0]
    vector = flags[1]

    @pl.when(flags[5] == 1)
    def _():
        side[flags[7]] = lateral_sum(flags, left, right, from_left, from_right, index, spare, 1)

    @pl.when(flags[0] == 1)
    def _():
        base = source[vector] - chain[vector] - side[vector]
        value[...] = base
        chain[vector] = jnp.zeros_like(base)

        def take_chain(matrix, row):
            spare[...] = gathered(incoming[...], index[row : row + 1, :])
            term = product(matrix, spare, rows)
            chain[vector] = term
            value[...] = value[...] - term

        @pl.when((flags[2] == 1) & (flags[3] == 1))
        def _():
            take_chain(up, 0)

        @pl.when((flags[2] == 1) & (flags[3] == 0))
        def _():
            take_chain(down, 1)

        spare[...] = value[...]
        fresh = product(diag, spare, rows)
        value[...] = fresh
        pair[flags[4]] = fresh


def side_kernel(flags, index, from_left, from_right, left_in, right_in, side_in, left, right, side, spare):
    @pl.when(flags[6] == 1)
    def _():
        side[flags[7]] = lateral_sum(flags, left, right, from_left, from_right, index, spare, flags[4])


def in_vmem(count):
    return [pl.BlockSpec(memory_space=pltpu.VMEM)] * count


def held(*arrays):
    return tuple(pltpu.VMEM(array.shape, array.dtype) for array in arrays)


def run_task(flags, index, source, incoming, sides, kept):
    return pl.pallas_call(
        task_kernel,
        out_shape=held(incoming, *kept),
        in_specs=[pl.BlockSpec(memory_space=pltpu.SMEM)] + in_vmem(5 + len(kept)),
        out_specs=tuple(in_vmem(1 + len(kept))),
        scratch_shapes=[pltpu.VMEM(incoming.shape, jnp.float32)],
        input_output_aliases={6 + n: 1 + n for n in range(len(kept))},
        compiler_params=pltpu.CompilerParams(vmem_limit_bytes=VMEM_LIMIT),
        name="task",
    )(flags, index, source, incoming, *sides, *kept)


def run_side(flags, index, sides, kept):
    return pl.pallas_call(
        side_kernel,
        out_shape=held(*kept),
        in_specs=[pl.BlockSpec(memory_space=pltpu.SMEM)] + in_vmem(3 + len(kept)),
        out_specs=tuple(in_vmem(len(kept))),
        scratch_shapes=[pltpu.VMEM(sides[0].shape[1:], jnp.float32)],
        input_output_aliases={4 + n: n for n in range(len(kept))},
        compiler_params=pltpu.CompilerParams(vmem_limit_bytes=VMEM_LIMIT),
        name="side",
    )(flags, index, *sides, *kept)


def turned(block):
    padded = -block.shape[0] % SUBLANES
    return jnp.pad(jnp.transpose(block, (1, 0, 2)), ((0, 0), (0, padded), (0, 0))).astype(jnp.float32)


def at_tick(tick, place, count, vectors):
    forward = lax.rem(tick - place + 2 * count, 2) == 0
    rank = jnp.where(forward, place, count - 1 - place)
    since = jnp.where(forward, tick - place, tick - rank - count)
    late = since >= 2 * count
    since = jnp.where(late, since - 2 * count, since)
    active = (since >= 0) & (since < 2 * vectors)
    vector = jnp.clip(since // 2, 0, vectors - 1)
    half = jnp.where(forward, 0, 1) + jnp.where(late, 2, 0)
    return active, vector, rank, forward, half


def per_device(
    residual_in, diag_inverse, up_block, side_blocks, up_cols, down_cols, left_cols, right_cols
):
    source = residual_in[0, 0]
    vectors, size, _ = source.shape
    rows = size + -size % SUBLANES
    source = jnp.pad(source, ((0, 0), (0, rows - size), (0, 0)))
    mats = tuple(
        turned(block)
        for block in (
            diag_inverse[0, 0], up_block[0, 0], side_blocks[0, 0, 0], side_blocks[0, 0, 1], side_blocks[0, 0, 2]
        )
    )
    index = jnp.stack([up_cols[0, 0], down_cols[0, 0], left_cols[0, 0], right_cols[0, 0]])
    place = lax.axis_index("sweep")
    count = lax.axis_size("sweep")
    parts = lax.axis_size("span")
    part = lax.axis_index("span")
    ticks = 4 * count + 2 * (vectors - 1)

    def one_tick(tick, parity, state):
        incoming, from_left, from_right, kept, out = state
        active, vector, rank, forward, half = at_tick(tick, place, count, vectors)
        was_active, was_vector, _, _, was_half = at_tick(tick - 2, place, count, vectors)
        crossing = was_active & (was_half < 3)
        if parity == 0:
            last_active, last_vector, _, _, last_half = at_tick(tick - 1, place, count, vectors)
            first = last_active & (last_half < 3) & active & (rank == 0) & (vector == last_vector)
            later = crossing
        else:
            first = jnp.zeros((), jnp.bool_)
            now_active, now_vector, now_rank, _, _ = at_tick(tick - 1, place, count, vectors)
            later = crossing & ~(now_active & (now_rank == 0) & (now_vector == was_vector))
        side_vector = jnp.where(first, vector, was_vector)
        flags = [
            active, vector, rank > 0, forward, parity, first, later, side_vector, part > 0, part < parts - 1
        ]
        later_flags = list(flags)
        later_flags[7] = was_vector
        flags, later_flags = (
            jnp.stack([jnp.asarray(flag).astype(jnp.int32) for flag in group]) for group in (flags, later_flags)
        )
        value, *kept = run_task(flags, index, source, incoming, (from_left, from_right), kept)
        diag, up, down, left, right, pair, chain, side = kept
        swap = [(s, s + 1) for s in range(parity, count - 1, 2)]
        alone = [s for s in range(count) if all(s not in two for two in swap)]
        incoming = lax.ppermute(value, "sweep", swap + [(b, a) for a, b in swap] + [(s, s) for s in alone])
        left, right, side = run_side(later_flags, index, (from_left, from_right), (left, right, side))
        if parity == 1:
            from_left = lax.ppermute(pair, "span", [(p, (p + 1) % parts) for p in range(parts)])
            from_right = lax.ppermute(pair, "span", [((p + 1) % parts, p) for p in range(parts)])
        out = jnp.where(
            (active & (half == 3) & (jnp.arange(vectors) == vector))[:, None, None], value[:size], out
        )
        return incoming, from_left, from_right, [diag, up, down, left, right, pair, chain, side], out

    def two_ticks(pair, state):
        state = one_tick(2 * pair, 0, state)
        return one_tick(2 * pair + 1, 1, state)

    single = jnp.zeros((rows, LANES), jnp.float32)
    double = jnp.zeros((2, rows, LANES), jnp.float32)
    several = jnp.zeros((vectors, rows, LANES), jnp.float32)
    state = (single, double, double, [*mats, double, several, several], jnp.zeros_like(residual_in[0, 0]))
    state = lax.fori_loop(0, ticks // 2, two_ticks, state)
    return state[4][None, None]


def solution(mesh):
    return jax.shard_map(
        per_device,
        mesh=mesh,
        in_specs=(
            P("sweep", "span", None, None, None),
            P("sweep", "span", None, None, None),
            P("sweep", "span", None, None, None),
            P("sweep", "span", None, None, None, None),
            P("sweep", "span", None),
            P("sweep", "span", None),
            P("sweep", "span", None),
            P("sweep", "span", None),
        ),
        out_specs=P("sweep", "span", None, None, None),
        check_vma=False,
    )
```

time: 1010 us -> 1250 us (1.24)
  local copies, waits for them, and re-layouts: 583 us -> 1060 us
  starting transfers between devices: 294 us -> 94 us
  waiting for transfers between devices: 33.7 us -> 0.2 us
    while x456 -> x950, local copies, waits for them, and re-layouts: 572 us -> 1050 us
    ppermute x114 -> x76, starting transfers between devices: 294 us -> 94 us  [the longest x38 72 us: one_tick(): lax.ppermute(value, 'sweep', swap + [(b, a) for a, b in swap] + [(s, s) f...]
    ppermute x114 -> x76, waiting for transfers between devices: 33.7 us -> 0.2 us  [the longest x38 0.1 us: one_tick(): lax.ppermute(value, 'sweep', swap + [(b, a) for a, b in swap] + [(s, s) f...]
  transfers between devices with their start and end apart: 114 -> 76, of which waited for: 19 -> 0; matrix products, arithmetic and copies ran while one was open for 0% -> 0% of each run, Pallas kernels for 3% -> 2%
where the time goes in v2:
time: 1250 us; the launch traced here: 1240 us
  local copies, waits for them, and re-layouts  1060 us (85%)
  starting transfers between devices  94 us (8%)
  Pallas kernels  64.9 us (5%)
  other arithmetic  15.7 us (1%)
    while x950, local copies, waits for them, and re-layouts  1050 us
    ppermute x38, starting transfers between devices, one_tick(): lax.ppermute(value, 'sweep', swap + [(b, a) for a, b in swap] + [(s, s) f...  72 us
    pallas_call x38, Pallas kernels, run_task(): pl.pallas_call(task_kernel, out_shape=held(incoming, *kept), in_specs=[pl...  36.1 us
    pallas_call x38, Pallas kernels, run_side(): pl.pallas_call(side_kernel, out_shape=held(*kept), in_specs=[pl.BlockSpec...  28.8 us
  transfers between devices with their start and end apart: 76, of which 0 were waited for; matrix products, arithmetic and copies ran while one was open for 0% of the time, Pallas kernels for 2%

profile of v2, /device:TPU:0, one launch (start us, length us, event | category | flops | bytes accessed | tf_op | source)
XLA Modules:
  0.0 1242.0 jit_solution(6208789129536258199)
XLA Ops:
  4.0 3.1 pad_convert_fusion.4
  11.1 2.7 pad_convert_fusion
  14.1 2.7 pad_convert_fusion.1
  16.8 4.6 pad_convert_fusion.2
  21.5 1219.8 %while.41 = (s32[]{:T(128)}, f32[104,128]{1,0:T(8,128)S(1)}, f32[2,104,128]{2,1,0:T(8,128)S(1)}, f32[2,104,128]{2,1,0:T(8,128)S(1)}, f32[100,104,128]{2,1,0:T(8,...) while((s32[]{:T(128)}, f32[104,128]{1,0:T(8,128)S(1)}, ...), condition=%wide.region_1.2_spmd.clone, body=%wide.region_0.1_spmd.clone.sunk | while | flops 153810 | bytes 513399904 | solution.py:201
  49.7 2.5 copy-done.2
  111.8 2.5 copy-done.2
  147.7 2.5 copy-done
  175.4 2.5 copy-done.2
  211.3 2.5 copy-done
  239.0 2.5 copy-done.2
  274.9 2.5 copy-done
  299.8 3.5 collective-permute-start
  303.3 2.5 copy-done.2
  364.1 2.6 collective-permute-start
  366.8 2.5 copy-done.2
  426.6 3.6 collective-permute-start
  490.0 9.4 collective-permute-start
  623.9 2.9 collective-permute-start
  816.5 4.4 collective-permute-start
  881.8 2.8 collective-permute-start
  944.4 3.4 collective-permute-start
  1007.7 8.9 collective-permute-start
  1140.2 2.8 collective-permute-start
  (1277 shorter events, 1155.0 us)
Async XLA Ops:
  47.1 13.0 %collective-permute-start = (f32[104,128]{1,0:T(8,128)S(1)}, f32[104,128]{1,0:T(8,128)S(1)}, u32[]{:S(2)}, u32[]{:S(2)}) collective-permute-start(f32[104,128]{1,0:T(8,128)S(1)} %get-tuple-element.964), channel_id=1, source_target_pairs={{0,4},{8,12},{16,20},{24,28},{4,0},{12,8},{20,16},{28,24},{1,5},{9... | collective-permute-start | bytes 159752 | tf_op jit(solution)/shard_map/while/body/eval_jaxpr/ppermute | solution.py:183
  75.5 8.8 collective-permute-start.3
  109.9 13.3 %collective-permute-start = (f32[104,128]{1,0:T(8,128)S(1)}, f32[104,128]{1,0:T(8,128)S(1)}, u32[]{:S(2)}, u32[]{:S(2)}) collective-permute-start(f32[104,128]{1,0:T(8,128)S(1)} %get-tuple-element.964), channel_id=1, source_target_pairs={{0,4},{8,12},{16,20},{24,28},{4,0},{12,8},{20,16},{28,24},{1,5},{9... | collective-permute-start | bytes 159752 | tf_op jit(solution)/shard_map/while/body/eval_jaxpr/ppermute | solution.py:183
  138.6 8.8 collective-permute-start.3
  173.0 13.8 %collective-permute-start = (f32[104,128]{1,0:T(8,128)S(1)}, f32[104,128]{1,0:T(8,128)S(1)}, u32[]{:S(2)}, u32[]{:S(2)}) collective-permute-start(f32[104,128]{1,0:T(8,128)S(1)} %get-tuple-element.964), channel_id=1, source_target_pairs={{0,4},{8,12},{16,20},{24,28},{4,0},{12,8},{20,16},{28,24},{1,5},{9... | collective-permute-start | bytes 159752 | tf_op jit(solution)/shard_map/while/body/eval_jaxpr/ppermute | solution.py:183
  202.2 8.8 collective-permute-start.3
  236.6 13.8 %collective-permute-start = (f32[104,128]{1,0:T(8,128)S(1)}, f32[104,128]{1,0:T(8,128)S(1)}, u32[]{:S(2)}, u32[]{:S(2)}) collective-permute-start(f32[104,128]{1,0:T(8,128)S(1)} %get-tuple-element.964), channel_id=1, source_target_pairs={{0,4},{8,12},{16,20},{24,28},{4,0},{12,8},{20,16},{28,24},{1,5},{9... | collective-permute-start | bytes 159752 | tf_op jit(solution)/shard_map/while/body/eval_jaxpr/ppermute | solution.py:183
  265.8 8.8 collective-permute-start.3
  299.8 14.9 %collective-permute-start = (f32[104,128]{1,0:T(8,128)S(1)}, f32[104,128]{1,0:T(8,128)S(1)}, u32[]{:S(2)}, u32[]{:S(2)}) collective-permute-start(f32[104,128]{1,0:T(8,128)S(1)} %get-tuple-element.964), channel_id=1, source_target_pairs={{0,4},{8,12},{16,20},{24,28},{4,0},{12,8},{20,16},{28,24},{1,5},{9... | collective-permute-start | bytes 159752 | tf_op jit(solution)/shard_map/while/body/eval_jaxpr/ppermute | solution.py:183
  364.1 13.1 %collective-permute-start = (f32[104,128]{1,0:T(8,128)S(1)}, f32[104,128]{1,0:T(8,128)S(1)}, u32[]{:S(2)}, u32[]{:S(2)}) collective-permute-start(f32[104,128]{1,0:T(8,128)S(1)} %get-tuple-element.964), channel_id=1, source_target_pairs={{0,4},{8,12},{16,20},{24,28},{4,0},{12,8},{20,16},{28,24},{1,5},{9... | collective-permute-start | bytes 159752 | tf_op jit(solution)/shard_map/while/body/eval_jaxpr/ppermute | solution.py:183
  426.6 14.0 %collective-permute-start = (f32[104,128]{1,0:T(8,128)S(1)}, f32[104,128]{1,0:T(8,128)S(1)}, u32[]{:S(2)}, u32[]{:S(2)}) collective-permute-start(f32[104,128]{1,0:T(8,128)S(1)} %get-tuple-element.964), channel_id=1, source_target_pairs={{0,4},{8,12},{16,20},{24,28},{4,0},{12,8},{20,16},{28,24},{1,5},{9... | collective-permute-start | bytes 159752 | tf_op jit(solution)/shard_map/while/body/eval_jaxpr/ppermute | solution.py:183
  490.0 19.8 %collective-permute-start = (f32[104,128]{1,0:T(8,128)S(1)}, f32[104,128]{1,0:T(8,128)S(1)}, u32[]{:S(2)}, u32[]{:S(2)}) collective-permute-start(f32[104,128]{1,0:T(8,128)S(1)} %get-tuple-element.964), channel_id=1, source_target_pairs={{0,4},{8,12},{16,20},{24,28},{4,0},{12,8},{20,16},{28,24},{1,5},{9... | collective-permute-start | bytes 159752 | tf_op jit(solution)/shard_map/while/body/eval_jaxpr/ppermute | solution.py:183
  561.6 10.5 collective-permute-start
  623.9 14.4 %collective-permute-start = (f32[104,128]{1,0:T(8,128)S(1)}, f32[104,128]{1,0:T(8,128)S(1)}, u32[]{:S(2)}, u32[]{:S(2)}) collective-permute-start(f32[104,128]{1,0:T(8,128)S(1)} %get-tuple-element.964), channel_id=1, source_target_pairs={{0,4},{8,12},{16,20},{24,28},{4,0},{12,8},{20,16},{28,24},{1,5},{9... | collective-permute-start | bytes 159752 | tf_op jit(solution)/shard_map/while/body/eval_jaxpr/ppermute | solution.py:183
  690.0 13.9 %collective-permute-start = (f32[104,128]{1,0:T(8,128)S(1)}, f32[104,128]{1,0:T(8,128)S(1)}, u32[]{:S(2)}, u32[]{:S(2)}) collective-permute-start(f32[104,128]{1,0:T(8,128)S(1)} %get-tuple-element.964), channel_id=1, source_target_pairs={{0,4},{8,12},{16,20},{24,28},{4,0},{12,8},{20,16},{28,24},{1,5},{9... | collective-permute-start | bytes 159752 | tf_op jit(solution)/shard_map/while/body/eval_jaxpr/ppermute | solution.py:183
  755.6 11.5 collective-permute-start
  816.5 15.9 %collective-permute-start = (f32[104,128]{1,0:T(8,128)S(1)}, f32[104,128]{1,0:T(8,128)S(1)}, u32[]{:S(2)}, u32[]{:S(2)}) collective-permute-start(f32[104,128]{1,0:T(8,128)S(1)} %get-tuple-element.964), channel_id=1, source_target_pairs={{0,4},{8,12},{16,20},{24,28},{4,0},{12,8},{20,16},{28,24},{1,5},{9... | collective-permute-start | bytes 159752 | tf_op jit(solution)/shard_map/while/body/eval_jaxpr/ppermute | solution.py:183
  881.8 13.2 %collective-permute-start = (f32[104,128]{1,0:T(8,128)S(1)}, f32[104,128]{1,0:T(8,128)S(1)}, u32[]{:S(2)}, u32[]{:S(2)}) collective-permute-start(f32[104,128]{1,0:T(8,128)S(1)} %get-tuple-element.964), channel_id=1, source_target_pairs={{0,4},{8,12},{16,20},{24,28},{4,0},{12,8},{20,16},{28,24},{1,5},{9... | collective-permute-start | bytes 159752 | tf_op jit(solution)/shard_map/while/body/eval_jaxpr/ppermute | solution.py:183
  944.4 13.9 %collective-permute-start = (f32[104,128]{1,0:T(8,128)S(1)}, f32[104,128]{1,0:T(8,128)S(1)}, u32[]{:S(2)}, u32[]{:S(2)}) collective-permute-start(f32[104,128]{1,0:T(8,128)S(1)} %get-tuple-element.964), channel_id=1, source_target_pairs={{0,4},{8,12},{16,20},{24,28},{4,0},{12,8},{20,16},{28,24},{1,5},{9... | collective-permute-start | bytes 159752 | tf_op jit(solution)/shard_map/while/body/eval_jaxpr/ppermute | solution.py:183
  1007.7 19.3 %collective-permute-start = (f32[104,128]{1,0:T(8,128)S(1)}, f32[104,128]{1,0:T(8,128)S(1)}, u32[]{:S(2)}, u32[]{:S(2)}) collective-permute-start(f32[104,128]{1,0:T(8,128)S(1)} %get-tuple-element.964), channel_id=1, source_target_pairs={{0,4},{8,12},{16,20},{24,28},{4,0},{12,8},{20,16},{28,24},{1,5},{9... | collective-permute-start | bytes 159752 | tf_op jit(solution)/shard_map/while/body/eval_jaxpr/ppermute | solution.py:183
  1077.4 12.4 %collective-permute-start = (f32[104,128]{1,0:T(8,128)S(1)}, f32[104,128]{1,0:T(8,128)S(1)}, u32[]{:S(2)}, u32[]{:S(2)}) collective-permute-start(f32[104,128]{1,0:T(8,128)S(1)} %get-tuple-element.964), channel_id=1, source_target_pairs={{0,4},{8,12},{16,20},{24,28},{4,0},{12,8},{20,16},{28,24},{1,5},{9... | collective-permute-start | bytes 159752 | tf_op jit(solution)/shard_map/while/body/eval_jaxpr/ppermute | solution.py:183
  1140.2 13.3 %collective-permute-start = (f32[104,128]{1,0:T(8,128)S(1)}, f32[104,128]{1,0:T(8,128)S(1)}, u32[]{:S(2)}, u32[]{:S(2)}) collective-permute-start(f32[104,128]{1,0:T(8,128)S(1)} %get-tuple-element.964), channel_id=1, source_target_pairs={{0,4},{8,12},{16,20},{24,28},{4,0},{12,8},{20,16},{28,24},{1,5},{9... | collective-permute-start | bytes 159752 | tf_op jit(solution)/shard_map/while/body/eval_jaxpr/ppermute | solution.py:183
  1169.8 8.8 collective-permute-start.3
  1203.8 12.3 collective-permute-start
  (511 other events, 1568.5 us)

commit v3 on v2

v3 whole, which is shorter than its diff:
```python
import functools

import jax
import jax.numpy as jnp
from jax import lax
from jax.experimental import pallas as pl
from jax.experimental.pallas import tpu as pltpu
from jax.sharding import PartitionSpec as P

SUBLANES = 8
VMEM_LIMIT = 8 * 1024 * 1024


def task_at(tick, place, count, vectors, choose=jnp.where):
    forward = ((tick - place) & 1) == 0
    rank = choose(forward, place, count - 1 - place)
    since = tick - rank - choose(forward, 0, count)
    late = since >= 2 * count
    since = choose(late, since - 2 * count, since)
    active = (since >= 0) & (since < 2 * vectors)
    half = choose(forward, 0, 1) + choose(late, 2, 0)
    return active, choose(active, since >> 1, 0), rank, forward, half


def turns(task):
    active, _, rank, _, half = task
    return active & (rank == 0) & (half > 0)


def crosses(task):
    return task[0] & (task[4] < 3)


def left_for_later(tick, at):
    taken = turns(at(tick - 1)) if tick & 1 else False
    return crosses(at(tick - 2)) & (taken ^ True)


def product(matrix, vector, rows, unroll=10):
    def body(step, total):
        for inner in range(unroll):
            j = step * unroll + inner
            total = total + matrix[j] * vector[pl.ds(j, 1), :]
        return total

    start = jnp.zeros((rows, matrix.shape[2]), jnp.float32)
    return lax.fori_loop(0, matrix.shape[0] // unroll, body, start)


def gathered(value, columns):
    index = jnp.broadcast_to(columns, value.shape)
    return jnp.take_along_axis(value, index, axis=1, mode="promise_in_bounds")


def add_lateral(side, vector, left, right, from_left, from_right, index, spare, slot):
    rows = spare.shape[0]
    part = lax.axis_index("span")
    side[vector] = jnp.zeros(side.shape[1:], jnp.float32)

    @pl.when(part > 0)
    def _():
        spare[...] = gathered(from_left[slot], index[2:3, :])
        side[vector] = product(left, spare, rows)

    @pl.when(part < lax.axis_size("span") - 1)
    def _():
        spare[...] = gathered(from_right[slot], index[3:4, :])
        side[vector] = side[vector] + product(right, spare, rows)


def task_kernel(
    tick, tasks, index, source, incoming, from_left, from_right,
    diag_in, up_in, down_in, left_in, right_in, pair_in, chain_in, side_in, out_in,
    value, diag, up, down, left, right, pair, chain, side, out, spare
):
    rows = spare.shape[0]
    vectors, size, _ = out.shape
    task = task_at(tick, lax.axis_index("sweep"), lax.axis_size("sweep"), vectors)
    active, vector, rank, forward, half = task

    if any(turns(one) for one in tasks):

        @pl.when(turns(task))
        def _():
            add_lateral(side, vector, left, right, from_left, from_right, index, spare, 1)

    @pl.when(active)
    def _():
        base = source[vector] - chain[vector] - side[vector]
        value[...] = base
        chain[vector] = jnp.zeros_like(base)

        def take_chain(matrix, row):
            spare[...] = gathered(incoming[...], index[row : row + 1, :])
            term = product(matrix, spare, rows)
            chain[vector] = term
            value[...] = value[...] - term

        if any(one[0] and one[2] > 0 and one[3] for one in tasks):

            @pl.when((rank > 0) & forward)
            def _():
                take_chain(up, 0)

        if any(one[0] and one[2] > 0 and not one[3] for one in tasks):

            @pl.when((rank > 0) & (forward ^ True))
            def _():
                take_chain(down, 1)

        spare[...] = value[...]
        fresh = product(diag, spare, rows)
        value[...] = fresh
        pair[tick & 1] = fresh

        if any(one[0] and one[4] == 3 for one in tasks):

            @pl.when(half == 3)
            def _():
                out[vector] = fresh[:size]


def side_kernel(tick, vectors, index, from_left, from_right, left_in, right_in, side_in, left, right, side, spare):
    def at(when):
        return task_at(when, lax.axis_index("sweep"), lax.axis_size("sweep"), vectors)

    @pl.when(left_for_later(tick, at))
    def _():
        add_lateral(side, at(tick - 2)[1], left, right, from_left, from_right, index, spare, tick & 1)


def in_vmem(count):
    return [pl.BlockSpec(memory_space=pltpu.VMEM)] * count


def call(kernel, name, fixed, kept, fresh, spare):
    return pl.pallas_call(
        kernel,
        out_shape=tuple(pltpu.VMEM(a.shape, a.dtype) for a in (*fresh, *kept)),
        in_specs=in_vmem(len(fixed) + len(kept)),
        out_specs=tuple(in_vmem(len(fresh) + len(kept))),
        scratch_shapes=[pltpu.VMEM(spare, jnp.float32)],
        input_output_aliases={len(fixed) + n: len(fresh) + n for n in range(len(kept))},
        compiler_params=pltpu.CompilerParams(vmem_limit_bytes=VMEM_LIMIT),
        name=name,
    )(*fixed, *kept)


def turned(block):
    padded = -block.shape[0] % SUBLANES
    return jnp.pad(jnp.transpose(block, (1, 0, 2)), ((0, 0), (0, padded), (0, 0))).astype(jnp.float32)


def per_device(
    residual_in, diag_inverse, up_block, side_blocks, up_cols, down_cols, left_cols, right_cols
):
    source = residual_in[0, 0]
    vectors, size, lanes = source.shape
    rows = size + -size % SUBLANES
    single = (rows, lanes)
    source = jnp.pad(source, ((0, 0), (0, rows - size), (0, 0)))
    diag, up, down, left, right = (
        turned(block)
        for block in (
            diag_inverse[0, 0], up_block[0, 0], side_blocks[0, 0, 0], side_blocks[0, 0, 1], side_blocks[0, 0, 2]
        )
    )
    index = jnp.stack([up_cols[0, 0], down_cols[0, 0], left_cols[0, 0], right_cols[0, 0]])
    count = lax.axis_size("sweep")
    parts = lax.axis_size("span")
    ticks = 4 * count + 2 * (vectors - 1)

    incoming = jnp.zeros(single, jnp.float32)
    pair = from_left = from_right = jnp.zeros((2, *single), jnp.float32)
    chain = side = jnp.zeros((vectors, *single), jnp.float32)
    out = jnp.zeros((vectors, size, lanes), jnp.float32)

    def at(place):
        return lambda when: task_at(when, place, count, vectors, lambda which, a, b: a if which else b)

    def any_task(when, test):
        return any(test(at(place)(when)) for place in range(count))

    for tick in range(ticks):
        value, diag, up, down, left, right, pair, chain, side, out = call(
            functools.partial(task_kernel, tick, [at(place)(tick) for place in range(count)]),
            "task",
            (index, source, incoming, from_left, from_right),
            (diag, up, down, left, right, pair, chain, side, out),
            (incoming,),
            single,
        )
        if any_task(tick + 1, lambda one: one[0] and one[2] > 0):
            swap = [(s, s + 1) for s in range(tick & 1, count - 1, 2)]
            alone = [s for s in range(count) if all(s not in two for two in swap)]
            incoming = lax.ppermute(value, "sweep", swap + [(b, a) for a, b in swap] + [(s, s) for s in alone])
        if any(left_for_later(tick, at(place)) for place in range(count)):
            left, right, side = call(
                functools.partial(side_kernel, tick, vectors),
                "side",
                (index, from_left, from_right),
                (left, right, side),
                (),
                single,
            )
        if tick & 1 and (any_task(tick, crosses) or any_task(tick - 1, crosses)):
            from_left = lax.ppermute(pair, "span", [(p, (p + 1) % parts) for p in range(parts)])
            from_right = lax.ppermute(pair, "span", [((p + 1) % parts, p) for p in range(parts)])
    return out[None, None]


def solution(mesh):
    return jax.shard_map(
        per_device,
        mesh=mesh,
        in_specs=(
            P("sweep", "span", None, None, None),
            P("sweep", "span", None, None, None),
            P("sweep", "span", None, None, None),
            P("sweep", "span", None, None, None, None),
            P("sweep", "span", None),
            P("sweep", "span", None),
            P("sweep", "span", None),
            P("sweep", "span", None),
        ),
        out_specs=P("sweep", "span", None, None, None),
        check_vma=False,
    )
```

time: 1250 us -> 260 us (0.21)
  local copies, waits for them, and re-layouts: 1060 us -> 18.1 us
  waiting for transfers between devices: 0.2 us -> 91.1 us
  Pallas kernels: 64.9 us -> 18.1 us
  starting transfers between devices: 94 us -> 125 us
    while x951 -> x0, local copies, waits for them, and re-layouts: 1050 us -> none
    ppermute x76 -> x67, waiting for transfers between devices: 0.2 us -> 91.1 us  [the longest x37 36.2 us: per_device(): lax.ppermute(value, 'sweep', swap + [(b, a) for a, b in swap] + [(s, s) f...]
    pallas_call x76 -> x67, Pallas kernels: 64.9 us -> 18.1 us  [call(): pl.pallas_call(kernel, out_shape=tuple((pltpu.VMEM(a.shape, a.dtype) for...]
    ppermute x76 -> x67, starting transfers between devices: 94 us -> 125 us  [the longest x37 117 us: per_device(): lax.ppermute(value, 'sweep', swap + [(b, a) for a, b in swap] + [(s, s) f...]
  transfers between devices with their start and end apart: 76 -> 67, of which waited for: 0 -> 49; matrix products, arithmetic and copies ran while one was open for 0% -> 0% of each run, Pallas kernels for 2% -> 2%
where the time goes in v3:
time: 260 us
  starting transfers between devices  125 us (48%)
  waiting for transfers between devices  91.1 us (35%)
  local copies, waits for them, and re-layouts  18.1 us (7%)
  Pallas kernels  18.1 us (7%)
  other arithmetic  6.49 us (2%)
    ppermute x37, starting transfers between devices, per_device(): lax.ppermute(value, 'sweep', swap + [(b, a) for a, b in swap] + [(s, s) f...  117 us
    ppermute x37, waiting for transfers between devices, per_device(): lax.ppermute(value, 'sweep', swap + [(b, a) for a, b in swap] + [(s, s) f...  36.2 us
    ppermute x15, waiting for transfers between devices, per_device(): lax.ppermute(pair, 'span', [(p, (p + 1) % parts) for p in range(parts)])  28.7 us
    ppermute x15, waiting for transfers between devices, per_device(): lax.ppermute(pair, 'span', [((p + 1) % parts, p) for p in range(parts)])  26.3 us
    pallas_call x67, Pallas kernels, call(): pl.pallas_call(kernel, out_shape=tuple((pltpu.VMEM(a.shape, a.dtype) for...  18.1 us
    unnamed x22, local copies, waits for them, and re-layouts  15.2 us
    ppermute x15, starting transfers between devices, per_device(): lax.ppermute(pair, 'span', [(p, (p + 1) % parts) for p in range(parts)])  7.06 us
    convert_element_type x4, other arithmetic, turned(): jnp.pad(jnp.transpose(block, (1, 0, 2)), ((0, 0), (0, padded), (0, 0)))  5.82 us
  transfers between devices with their start and end apart: 67, of which 49 were waited for; matrix products, arithmetic and copies ran while one was open for 0% of the time, Pallas kernels for 2%

profile of v3, /device:TPU:0, one launch (start us, length us, event | category | flops | bytes accessed | tf_op | source)
XLA Modules:
  0.0 259.7 jit_solution(17951838817375310298)
XLA Ops:
  11.1 4.8 %pad_convert_fusion.2 = (f32[100,104,128]{2,1,0:T(8,128)S(1)}, f32[100,104,128]{2,1,0:T(8,128)}) fusion(bf16[100,100,128]{2,1,0:T(8,128)(2,1)} %bitcast.33, bf16[100,100,128]{2,1,0:T(8,128)(2,1)S(1)} %bitcast.32), kind=kLoop, calls=%fused_computation.7 | loop fusion | flops 2662400 | bytes 15769600 | tf_op jit(solution)/shard_map/convert_element_type | solution.py:151
  16.7 2.5 copy-done
  19.6 2.5 collective-permute-start
  24.2 2.3 copy-done.1
  29.7 2.9 %collective-permute-done.2.from_left = f32[2,104,128]{2,1,0:T(8,128)S(1)} collective-permute-done((f32[2,104,128]{2,1,0:T(8,128)S(1)}, f32[2,104,128]{2,1,0:T(8,128)S(1)}, u32[]{:S(2)}, u32[]{:S(2)}) %collective-permute-start.2) | collective-permute-done | bytes 106528 | tf_op jit(solution)/shard_map/ppermute | solution.py:207
  32.6 2.5 copy-done.2
  35.5 4.4 %collective-permute-start.4 = (f32[104,128]{1,0:T(8,128)S(1)}, f32[104,128]{1,0:T(8,128)S(1)}, u32[]{:S(2)}, u32[]{:S(2)}) collective-permute-start(f32[104,128]{1,0:T(8,128)S(1)} %get-tuple-element.483), channel_id=1, source_target_pairs={{0,4},{8,12},{16,20},{24,28},{4,0},{12,8},{20,16},{28,24},{1,5},{9... | collective-permute-start | bytes 159752 | tf_op jit(solution)/shard_map/ppermute | solution.py:196
  47.4 5.5 %collective-permute-start.8 = (f32[104,128]{1,0:T(8,128)S(1)}, f32[104,128]{1,0:T(8,128)S(1)}, u32[]{:S(2)}, u32[]{:S(2)}) collective-permute-start(f32[104,128]{1,0:T(8,128)S(1)} %get-tuple-element.509), channel_id=1, source_target_pairs={{0,4},{8,12},{16,20},{24,28},{4,0},{12,8},{20,16},{28,24},{1,5},{9... | collective-permute-start | bytes 159752 | tf_op jit(solution)/shard_map/ppermute | solution.py:196
  60.2 5.5 %collective-permute-start.12 = (f32[104,128]{1,0:T(8,128)S(1)}, f32[104,128]{1,0:T(8,128)S(1)}, u32[]{:S(2)}, u32[]{:S(2)}) collective-permute-start(f32[104,128]{1,0:T(8,128)S(1)} %get-tuple-element.535), channel_id=1, source_target_pairs={{0,4},{8,12},{16,20},{24,28},{4,0},{12,8},{20,16},{28,24},{1,5},{9... | collective-permute-start | bytes 159752 | tf_op jit(solution)/shard_map/ppermute | solution.py:196
  72.7 5.9 %collective-permute-start.16 = (f32[104,128]{1,0:T(8,128)S(1)}, f32[104,128]{1,0:T(8,128)S(1)}, u32[]{:S(2)}, u32[]{:S(2)}) collective-permute-start(f32[104,128]{1,0:T(8,128)S(1)} %get-tuple-element.561), channel_id=1, source_target_pairs={{0,4},{8,12},{16,20},{24,28},{4,0},{12,8},{20,16},{28,24},{1,5},{9... | collective-permute-start | bytes 159752 | tf_op jit(solution)/shard_map/ppermute | solution.py:196
  85.5 4.9 %collective-permute-start.20 = (f32[104,128]{1,0:T(8,128)S(1)}, f32[104,128]{1,0:T(8,128)S(1)}, u32[]{:S(2)}, u32[]{:S(2)}) collective-permute-start(f32[104,128]{1,0:T(8,128)S(1)} %get-tuple-element.587), channel_id=1, source_target_pairs={{0,4},{8,12},{16,20},{24,28},{4,0},{12,8},{20,16},{28,24},{1,5},{9... | collective-permute-start | bytes 159752 | tf_op jit(solution)/shard_map/ppermute | solution.py:196
  97.5 4.9 %collective-permute-start.24 = (f32[104,128]{1,0:T(8,128)S(1)}, f32[104,128]{1,0:T(8,128)S(1)}, u32[]{:S(2)}, u32[]{:S(2)}) collective-permute-start(f32[104,128]{1,0:T(8,128)S(1)} %get-tuple-element.613), channel_id=1, source_target_pairs={{0,4},{8,12},{16,20},{24,28},{4,0},{12,8},{20,16},{28,24},{1,5},{9... | collective-permute-start | bytes 159752 | tf_op jit(solution)/shard_map/ppermute | solution.py:196
  109.2 6.3 %collective-permute-start.28 = (f32[104,128]{1,0:T(8,128)S(1)}, f32[104,128]{1,0:T(8,128)S(1)}, u32[]{:S(2)}, u32[]{:S(2)}) collective-permute-start(f32[104,128]{1,0:T(8,128)S(1)} %get-tuple-element.639), channel_id=1, source_target_pairs={{0,4},{8,12},{16,20},{24,28},{4,0},{12,8},{20,16},{28,24},{1,5},{9... | collective-permute-start | bytes 159752 | tf_op jit(solution)/shard_map/ppermute | solution.py:196
  124.4 4.3 %collective-permute-start.32 = (f32[104,128]{1,0:T(8,128)S(1)}, f32[104,128]{1,0:T(8,128)S(1)}, u32[]{:S(2)}, u32[]{:S(2)}) collective-permute-start(f32[104,128]{1,0:T(8,128)S(1)} %get-tuple-element.665), channel_id=1, source_target_pairs={{0,4},{8,12},{16,20},{24,28},{4,0},{12,8},{20,16},{28,24},{1,5},{9... | collective-permute-start | bytes 159752 | tf_op jit(solution)/shard_map/ppermute | solution.py:196
  137.5 5.0 %collective-permute-start.36 = (f32[104,128]{1,0:T(8,128)S(1)}, f32[104,128]{1,0:T(8,128)S(1)}, u32[]{:S(2)}, u32[]{:S(2)}) collective-permute-start(f32[104,128]{1,0:T(8,128)S(1)} %get-tuple-element.691), channel_id=1, source_target_pairs={{0,4},{8,12},{16,20},{24,28},{4,0},{12,8},{20,16},{28,24},{1,5},{9... | collective-permute-start | bytes 159752 | tf_op jit(solution)/shard_map/ppermute | solution.py:196
  151.4 5.0 %collective-permute-start.40 = (f32[104,128]{1,0:T(8,128)S(1)}, f32[104,128]{1,0:T(8,128)S(1)}, u32[]{:S(2)}, u32[]{:S(2)}) collective-permute-start(f32[104,128]{1,0:T(8,128)S(1)} %get-tuple-element.717), channel_id=1, source_target_pairs={{0,4},{8,12},{16,20},{24,28},{4,0},{12,8},{20,16},{28,24},{1,5},{9... | collective-permute-start | bytes 159752 | tf_op jit(solution)/shard_map/ppermute | solution.py:196
  165.2 4.0 %collective-permute-start.44 = (f32[104,128]{1,0:T(8,128)S(1)}, f32[104,128]{1,0:T(8,128)S(1)}, u32[]{:S(2)}, u32[]{:S(2)}) collective-permute-start(f32[104,128]{1,0:T(8,128)S(1)} %get-tuple-element.743), channel_id=1, source_target_pairs={{0,4},{8,12},{16,20},{24,28},{4,0},{12,8},{20,16},{28,24},{1,5},{9... | collective-permute-start | bytes 159752 | tf_op jit(solution)/shard_map/ppermute | solution.py:196
  176.3 5.9 %collective-permute-start.48 = (f32[104,128]{1,0:T(8,128)S(1)}, f32[104,128]{1,0:T(8,128)S(1)}, u32[]{:S(2)}, u32[]{:S(2)}) collective-permute-start(f32[104,128]{1,0:T(8,128)S(1)} %get-tuple-element.769), channel_id=1, source_target_pairs={{0,4},{8,12},{16,20},{24,28},{4,0},{12,8},{20,16},{28,24},{1,5},{9... | collective-permute-start | bytes 159752 | tf_op jit(solution)/shard_map/ppermute | solution.py:196
  189.1 4.9 %collective-permute-start.52 = (f32[104,128]{1,0:T(8,128)S(1)}, f32[104,128]{1,0:T(8,128)S(1)}, u32[]{:S(2)}, u32[]{:S(2)}) collective-permute-start(f32[104,128]{1,0:T(8,128)S(1)} %get-tuple-element.795), channel_id=1, source_target_pairs={{0,4},{8,12},{16,20},{24,28},{4,0},{12,8},{20,16},{28,24},{1,5},{9... | collective-permute-start | bytes 159752 | tf_op jit(solution)/shard_map/ppermute | solution.py:196
  201.0 4.9 %collective-permute-start.56 = (f32[104,128]{1,0:T(8,128)S(1)}, f32[104,128]{1,0:T(8,128)S(1)}, u32[]{:S(2)}, u32[]{:S(2)}) collective-permute-start(f32[104,128]{1,0:T(8,128)S(1)} %get-tuple-element.821), channel_id=1, source_target_pairs={{0,4},{8,12},{16,20},{24,28},{4,0},{12,8},{20,16},{28,24},{1,5},{9... | collective-permute-start | bytes 159752 | tf_op jit(solution)/shard_map/ppermute | solution.py:196
  212.8 6.3 %collective-permute-start.60 = (f32[104,128]{1,0:T(8,128)S(1)}, f32[104,128]{1,0:T(8,128)S(1)}, u32[]{:S(2)}, u32[]{:S(2)}) collective-permute-start(f32[104,128]{1,0:T(8,128)S(1)} %get-tuple-element.847), channel_id=1, source_target_pairs={{0,4},{8,12},{16,20},{24,28},{4,0},{12,8},{20,16},{28,24},{1,5},{9... | collective-permute-start | bytes 159752 | tf_op jit(solution)/shard_map/ppermute | solution.py:196
  222.8 8.3 %collective-permute-start.62 = (f32[104,128]{1,0:T(8,128)S(1)}, f32[104,128]{1,0:T(8,128)S(1)}, u32[]{:S(2)}, u32[]{:S(2)}) collective-permute-start(f32[104,128]{1,0:T(8,128)S(1)} %get-tuple-element.870), channel_id=1, source_target_pairs={{0,4},{8,12},{16,20},{24,28},{4,0},{12,8},{20,16},{28,24},{1,5},{9... | collective-permute-start | bytes 159752 | tf_op jit(solution)/shard_map/ppermute | solution.py:196
  234.9 8.4 %collective-permute-start.64 = (f32[104,128]{1,0:T(8,128)S(1)}, f32[104,128]{1,0:T(8,128)S(1)}, u32[]{:S(2)}, u32[]{:S(2)}) collective-permute-start(f32[104,128]{1,0:T(8,128)S(1)} %get-tuple-element.890), channel_id=1, source_target_pairs={{0,4},{8,12},{16,20},{24,28},{4,0},{12,8},{20,16},{28,24},{1,5},{9... | collective-permute-start | bytes 159752 | tf_op jit(solution)/shard_map/ppermute | solution.py:196
  247.1 8.3 %collective-permute-start.66 = (f32[104,128]{1,0:T(8,128)S(1)}, f32[104,128]{1,0:T(8,128)S(1)}, u32[]{:S(2)}, u32[]{:S(2)}) collective-permute-start(f32[104,128]{1,0:T(8,128)S(1)} %get-tuple-element.910), channel_id=1, source_target_pairs={{0,4},{8,12},{16,20},{24,28},{4,0},{12,8},{20,16},{28,24},{1,5},{9... | collective-permute-start | bytes 159752 | tf_op jit(solution)/shard_map/ppermute | solution.py:196
  (215 shorter events, 138.7 us)
Async XLA Ops:
  27.4 5.2 %collective-permute-start.2 = (f32[2,104,128]{2,1,0:T(8,128)S(1)}, f32[2,104,128]{2,1,0:T(8,128)S(1)}, u32[]{:S(2)}, u32[]{:S(2)}) collective-permute-start(f32[2,104,128]{2,1,0:T(8,128)S(1)} %get-tuple-element.474.pair_in), channel_id=1, source_target_pairs={{0,1},{1,2},{2,3},{3,0},{4,5},{5,6},{6,7},{7,4},{8,9},{9,10},{10,1... | collective-permute-start | bytes 319496 | tf_op jit(solution)/shard_map/ppermute | solution.py:207
  35.5 6.5 %collective-permute-start.4 = (f32[104,128]{1,0:T(8,128)S(1)}, f32[104,128]{1,0:T(8,128)S(1)}, u32[]{:S(2)}, u32[]{:S(2)}) collective-permute-start(f32[104,128]{1,0:T(8,128)S(1)} %get-tuple-element.483), channel_id=1, source_target_pairs={{0,4},{8,12},{16,20},{24,28},{4,0},{12,8},{20,16},{28,24},{1,5},{9... | collective-permute-start | bytes 159752 | tf_op jit(solution)/shard_map/ppermute | solution.py:196
  42.0 4.9 %collective-permute-start.6 = (f32[2,104,128]{2,1,0:T(8,128)S(1)}, f32[2,104,128]{2,1,0:T(8,128)S(1)}, u32[]{:S(2)}, u32[]{:S(2)}) collective-permute-start(f32[2,104,128]{2,1,0:T(8,128)S(1)} %get-tuple-element.497.pair_in), channel_id=1, source_target_pairs={{0,1},{1,2},{2,3},{3,0},{4,5},{5,6},{6,7},{7,4},{8,9},{9,10},{10,1... | collective-permute-start | bytes 319496 | tf_op jit(solution)/shard_map/ppermute | solution.py:207
  47.4 7.6 %collective-permute-start.8 = (f32[104,128]{1,0:T(8,128)S(1)}, f32[104,128]{1,0:T(8,128)S(1)}, u32[]{:S(2)}, u32[]{:S(2)}) collective-permute-start(f32[104,128]{1,0:T(8,128)S(1)} %get-tuple-element.509), channel_id=1, source_target_pairs={{0,4},{8,12},{16,20},{24,28},{4,0},{12,8},{20,16},{28,24},{1,5},{9... | collective-permute-start | bytes 159752 | tf_op jit(solution)/shard_map/ppermute | solution.py:196
  60.2 7.6 %collective-permute-start.12 = (f32[104,128]{1,0:T(8,128)S(1)}, f32[104,128]{1,0:T(8,128)S(1)}, u32[]{:S(2)}, u32[]{:S(2)}) collective-permute-start(f32[104,128]{1,0:T(8,128)S(1)} %get-tuple-element.535), channel_id=1, source_target_pairs={{0,4},{8,12},{16,20},{24,28},{4,0},{12,8},{20,16},{28,24},{1,5},{9... | collective-permute-start | bytes 159752 | tf_op jit(solution)/shard_map/ppermute | solution.py:196
  67.8 4.9 %collective-permute-start.14 = (f32[2,104,128]{2,1,0:T(8,128)S(1)}, f32[2,104,128]{2,1,0:T(8,128)S(1)}, u32[]{:S(2)}, u32[]{:S(2)}) collective-permute-start(f32[2,104,128]{2,1,0:T(8,128)S(1)} %get-tuple-element.549.pair_in), channel_id=1, source_target_pairs={{0,1},{1,2},{2,3},{3,0},{4,5},{5,6},{6,7},{7,4},{8,9},{9,10},{10,1... | collective-permute-start | bytes 319496 | tf_op jit(solution)/shard_map/ppermute | solution.py:207
  72.7 8.1 %collective-permute-start.16 = (f32[104,128]{1,0:T(8,128)S(1)}, f32[104,128]{1,0:T(8,128)S(1)}, u32[]{:S(2)}, u32[]{:S(2)}) collective-permute-start(f32[104,128]{1,0:T(8,128)S(1)} %get-tuple-element.561), channel_id=1, source_target_pairs={{0,4},{8,12},{16,20},{24,28},{4,0},{12,8},{20,16},{28,24},{1,5},{9... | collective-permute-start | bytes 159752 | tf_op jit(solution)/shard_map/ppermute | solution.py:196
  85.5 7.0 %collective-permute-start.20 = (f32[104,128]{1,0:T(8,128)S(1)}, f32[104,128]{1,0:T(8,128)S(1)}, u32[]{:S(2)}, u32[]{:S(2)}) collective-permute-start(f32[104,128]{1,0:T(8,128)S(1)} %get-tuple-element.587), channel_id=1, source_target_pairs={{0,4},{8,12},{16,20},{24,28},{4,0},{12,8},{20,16},{28,24},{1,5},{9... | collective-permute-start | bytes 159752 | tf_op jit(solution)/shard_map/ppermute | solution.py:196
  92.6 4.9 %collective-permute-start.22 = (f32[2,104,128]{2,1,0:T(8,128)S(1)}, f32[2,104,128]{2,1,0:T(8,128)S(1)}, u32[]{:S(2)}, u32[]{:S(2)}) collective-permute-start(f32[2,104,128]{2,1,0:T(8,128)S(1)} %get-tuple-element.601.pair_in), channel_id=1, source_target_pairs={{0,1},{1,2},{2,3},{3,0},{4,5},{5,6},{6,7},{7,4},{8,9},{9,10},{10,1... | collective-permute-start | bytes 319496 | tf_op jit(solution)/shard_map/ppermute | solution.py:207
  97.5 7.0 %collective-permute-start.24 = (f32[104,128]{1,0:T(8,128)S(1)}, f32[104,128]{1,0:T(8,128)S(1)}, u32[]{:S(2)}, u32[]{:S(2)}) collective-permute-start(f32[104,128]{1,0:T(8,128)S(1)} %get-tuple-element.613), channel_id=1, source_target_pairs={{0,4},{8,12},{16,20},{24,28},{4,0},{12,8},{20,16},{28,24},{1,5},{9... | collective-permute-start | bytes 159752 | tf_op jit(solution)/shard_map/ppermute | solution.py:196
  109.2 8.5 %collective-permute-start.28 = (f32[104,128]{1,0:T(8,128)S(1)}, f32[104,128]{1,0:T(8,128)S(1)}, u32[]{:S(2)}, u32[]{:S(2)}) collective-permute-start(f32[104,128]{1,0:T(8,128)S(1)} %get-tuple-element.639), channel_id=1, source_target_pairs={{0,4},{8,12},{16,20},{24,28},{4,0},{12,8},{20,16},{28,24},{1,5},{9... | collective-permute-start | bytes 159752 | tf_op jit(solution)/shard_map/ppermute | solution.py:196
  124.4 6.4 %collective-permute-start.32 = (f32[104,128]{1,0:T(8,128)S(1)}, f32[104,128]{1,0:T(8,128)S(1)}, u32[]{:S(2)}, u32[]{:S(2)}) collective-permute-start(f32[104,128]{1,0:T(8,128)S(1)} %get-tuple-element.665), channel_id=1, source_target_pairs={{0,4},{8,12},{16,20},{24,28},{4,0},{12,8},{20,16},{28,24},{1,5},{9... | collective-permute-start | bytes 159752 | tf_op jit(solution)/shard_map/ppermute | solution.py:196
  137.5 7.1 %collective-permute-start.36 = (f32[104,128]{1,0:T(8,128)S(1)}, f32[104,128]{1,0:T(8,128)S(1)}, u32[]{:S(2)}, u32[]{:S(2)}) collective-permute-start(f32[104,128]{1,0:T(8,128)S(1)} %get-tuple-element.691), channel_id=1, source_target_pairs={{0,4},{8,12},{16,20},{24,28},{4,0},{12,8},{20,16},{28,24},{1,5},{9... | collective-permute-start | bytes 159752 | tf_op jit(solution)/shard_map/ppermute | solution.py:196
  151.4 7.1 %collective-permute-start.40 = (f32[104,128]{1,0:T(8,128)S(1)}, f32[104,128]{1,0:T(8,128)S(1)}, u32[]{:S(2)}, u32[]{:S(2)}) collective-permute-start(f32[104,128]{1,0:T(8,128)S(1)} %get-tuple-element.717), channel_id=1, source_target_pairs={{0,4},{8,12},{16,20},{24,28},{4,0},{12,8},{20,16},{28,24},{1,5},{9... | collective-permute-start | bytes 159752 | tf_op jit(solution)/shard_map/ppermute | solution.py:196
  165.2 6.1 %collective-permute-start.44 = (f32[104,128]{1,0:T(8,128)S(1)}, f32[104,128]{1,0:T(8,128)S(1)}, u32[]{:S(2)}, u32[]{:S(2)}) collective-permute-start(f32[104,128]{1,0:T(8,128)S(1)} %get-tuple-element.743), channel_id=1, source_target_pairs={{0,4},{8,12},{16,20},{24,28},{4,0},{12,8},{20,16},{28,24},{1,5},{9... | collective-permute-start | bytes 159752 | tf_op jit(solution)/shard_map/ppermute | solution.py:196
  171.3 4.9 %collective-permute-start.46 = (f32[2,104,128]{2,1,0:T(8,128)S(1)}, f32[2,104,128]{2,1,0:T(8,128)S(1)}, u32[]{:S(2)}, u32[]{:S(2)}) collective-permute-start(f32[2,104,128]{2,1,0:T(8,128)S(1)} %get-tuple-element.757.pair_in), channel_id=1, source_target_pairs={{0,1},{1,2},{2,3},{3,0},{4,5},{5,6},{6,7},{7,4},{8,9},{9,10},{10,1... | collective-permute-start | bytes 319496 | tf_op jit(solution)/shard_map/ppermute | solution.py:207
  176.3 8.1 %collective-permute-start.48 = (f32[104,128]{1,0:T(8,128)S(1)}, f32[104,128]{1,0:T(8,128)S(1)}, u32[]{:S(2)}, u32[]{:S(2)}) collective-permute-start(f32[104,128]{1,0:T(8,128)S(1)} %get-tuple-element.769), channel_id=1, source_target_pairs={{0,4},{8,12},{16,20},{24,28},{4,0},{12,8},{20,16},{28,24},{1,5},{9... | collective-permute-start | bytes 159752 | tf_op jit(solution)/shard_map/ppermute | solution.py:196
  189.1 7.0 %collective-permute-start.52 = (f32[104,128]{1,0:T(8,128)S(1)}, f32[104,128]{1,0:T(8,128)S(1)}, u32[]{:S(2)}, u32[]{:S(2)}) collective-permute-start(f32[104,128]{1,0:T(8,128)S(1)} %get-tuple-element.795), channel_id=1, source_target_pairs={{0,4},{8,12},{16,20},{24,28},{4,0},{12,8},{20,16},{28,24},{1,5},{9... | collective-permute-start | bytes 159752 | tf_op jit(solution)/shard_map/ppermute | solution.py:196
  196.1 4.9 %collective-permute-start.54 = (f32[2,104,128]{2,1,0:T(8,128)S(1)}, f32[2,104,128]{2,1,0:T(8,128)S(1)}, u32[]{:S(2)}, u32[]{:S(2)}) collective-permute-start(f32[2,104,128]{2,1,0:T(8,128)S(1)} %get-tuple-element.809.pair_in), channel_id=1, source_target_pairs={{0,1},{1,2},{2,3},{3,0},{4,5},{5,6},{6,7},{7,4},{8,9},{9,10},{10,1... | collective-permute-start | bytes 319496 | tf_op jit(solution)/shard_map/ppermute | solution.py:207
  201.0 7.0 %collective-permute-start.56 = (f32[104,128]{1,0:T(8,128)S(1)}, f32[104,128]{1,0:T(8,128)S(1)}, u32[]{:S(2)}, u32[]{:S(2)}) collective-permute-start(f32[104,128]{1,0:T(8,128)S(1)} %get-tuple-element.821), channel_id=1, source_target_pairs={{0,4},{8,12},{16,20},{24,28},{4,0},{12,8},{20,16},{28,24},{1,5},{9... | collective-permute-start | bytes 159752 | tf_op jit(solution)/shard_map/ppermute | solution.py:196
  212.8 8.4 %collective-permute-start.60 = (f32[104,128]{1,0:T(8,128)S(1)}, f32[104,128]{1,0:T(8,128)S(1)}, u32[]{:S(2)}, u32[]{:S(2)}) collective-permute-start(f32[104,128]{1,0:T(8,128)S(1)} %get-tuple-element.847), channel_id=1, source_target_pairs={{0,4},{8,12},{16,20},{24,28},{4,0},{12,8},{20,16},{28,24},{1,5},{9... | collective-permute-start | bytes 159752 | tf_op jit(solution)/shard_map/ppermute | solution.py:196
  222.8 10.4 %collective-permute-start.62 = (f32[104,128]{1,0:T(8,128)S(1)}, f32[104,128]{1,0:T(8,128)S(1)}, u32[]{:S(2)}, u32[]{:S(2)}) collective-permute-start(f32[104,128]{1,0:T(8,128)S(1)} %get-tuple-element.870), channel_id=1, source_target_pairs={{0,4},{8,12},{16,20},{24,28},{4,0},{12,8},{20,16},{28,24},{1,5},{9... | collective-permute-start | bytes 159752 | tf_op jit(solution)/shard_map/ppermute | solution.py:196
  234.9 10.5 %collective-permute-start.64 = (f32[104,128]{1,0:T(8,128)S(1)}, f32[104,128]{1,0:T(8,128)S(1)}, u32[]{:S(2)}, u32[]{:S(2)}) collective-permute-start(f32[104,128]{1,0:T(8,128)S(1)} %get-tuple-element.890), channel_id=1, source_target_pairs={{0,4},{8,12},{16,20},{24,28},{4,0},{12,8},{20,16},{28,24},{1,5},{9... | collective-permute-start | bytes 159752 | tf_op jit(solution)/shard_map/ppermute | solution.py:196
  247.1 10.4 %collective-permute-start.66 = (f32[104,128]{1,0:T(8,128)S(1)}, f32[104,128]{1,0:T(8,128)S(1)}, u32[]{:S(2)}, u32[]{:S(2)}) collective-permute-start(f32[104,128]{1,0:T(8,128)S(1)} %get-tuple-element.910), channel_id=1, source_target_pairs={{0,4},{8,12},{16,20},{24,28},{4,0},{12,8},{20,16},{28,24},{1,5},{9... | collective-permute-start | bytes 159752 | tf_op jit(solution)/shard_map/ppermute | solution.py:196
  (52 other events, 136.1 us)

commit v4 on v3

v4 whole, which is shorter than its diff:
```python
import functools

import jax
import jax.numpy as jnp
from jax import lax
from jax.experimental import pallas as pl
from jax.experimental.pallas import tpu as pltpu
from jax.sharding import PartitionSpec as P

SUBLANES = 8
VMEM_LIMIT = 16 * 1024 * 1024
LATERAL_START = 4


def task_at(tick, place, count, vectors, choose=jnp.where):
    forward = ((tick - place) & 1) == 0
    rank = choose(forward, place, count - 1 - place)
    since = tick - rank - choose(forward, 0, count)
    late = since >= 2 * count
    since = choose(late, since - 2 * count, since)
    active = (since >= 0) & (since < 2 * vectors)
    half = choose(forward, 0, 1) + choose(late, 2, 0)
    return active, choose(active, since >> 1, 0), rank, forward, half


def turns(task):
    active, _, rank, _, half = task
    return active & (rank == 0) & (half > 0)


def lateral_plan(count, vectors):
    ticks = 4 * count + 2 * (vectors - 1)
    sent = [[-1] * count for _ in range(ticks)]
    urgent = [[False] * count for _ in range(ticks)]
    for slab in range(count):
        waiting = []
        for half in range(3):
            rank = count - 1 - slab if half & 1 else slab
            for vector in range(vectors):
                made = 2 * vector + half * count + rank
                used = 2 * vector + (half + 1) * count + count - 1 - rank
                if used == made + 1:
                    sent[made][slab] = vector
                    urgent[made][slab] = True
                else:
                    waiting.append((used, made, vector))
        for parity in range(2):
            left = sorted(waiting)
            for tick in range(LATERAL_START + parity, ticks, 2):
                ready = [one for one in left if one[1] <= tick]
                if sent[tick][slab] >= 0 or not ready:
                    continue
                assert tick <= ready[0][0] - 2
                sent[tick][slab] = ready[0][2]
                left.remove(ready[0])
            assert not left
    return sent, urgent


def pick(values, place):
    result = jnp.int32(values[0])
    for at, value in enumerate(values):
        if value != values[0]:
            result = jnp.where(place == at, value, result)
    return result


def product(matrix, vector, rows, unroll=20):
    def body(step, total):
        for inner in range(unroll):
            j = step * unroll + inner
            total = total + matrix[j] * vector[pl.ds(j, 1), :]
        return total

    start = jnp.zeros((rows, matrix.shape[2]), jnp.float32)
    return lax.fori_loop(0, matrix.shape[0] // unroll, body, start)


def gathered(value, columns):
    index = jnp.broadcast_to(columns, value.shape)
    return jnp.take_along_axis(value, index, axis=1, mode="promise_in_bounds")


def take_lateral(base, vector, left, right, left_cols, right_cols, arrived, spare, parity):
    rows = spare.shape[0]
    part = lax.axis_index("span")
    on_right = (part & 1) == parity

    @pl.when(on_right & (part < lax.axis_size("span") - 1))
    def _():
        spare[...] = gathered(arrived[...], right_cols[...])
        base[vector] = base[vector] - product(right, spare, rows)

    @pl.when((on_right ^ True) & (part > 0))
    def _():
        spare[...] = gathered(arrived[...], left_cols[...])
        base[vector] = base[vector] - product(left, spare, rows)


def prepare_kernel(block, ready, wide):
    size, _, lanes = block.shape[-3:]
    rows = ready.shape[1]
    lead = (0,) * (len(block.shape) - 3)
    wide[pl.ds(size * rows, (rows - size) * rows), :] = jnp.zeros(((rows - size) * rows, lanes), jnp.float32)

    def widen(i, _):
        wide[pl.ds(pl.multiple_of(i * rows, SUBLANES), size), :] = block[(*lead, i)].astype(jnp.float32)
        return 0

    lax.fori_loop(0, size, widen, 0, unroll=4)

    def turn(j, _):
        for i in range(0, rows, SUBLANES):
            ready[j, pl.ds(i, SUBLANES), :] = wide[pl.ds(i * rows + j, SUBLANES, stride=rows), :]
        return 0

    lax.fori_loop(0, size, turn, 0, unroll=4)


def first_kernel(block, residual, ready, base, source, blank, wide):
    prepare_kernel(block, ready, wide)
    vectors, size, lanes = residual.shape
    rows = base.shape[1]
    base[:, pl.ds(rows - SUBLANES, SUBLANES), :] = jnp.zeros((vectors, SUBLANES, lanes), jnp.float32)
    base[:, pl.ds(0, size), :] = residual[...]
    source[...] = base[...]
    blank[...] = jnp.zeros_like(blank)


def later_kernel(block, base_in, ready, base, wide):
    prepare_kernel(block, ready, wide)


def task_kernel(
    tick, tasks, sent, columns_and_inputs, kept, values, spare
):
    up_cols, down_cols, left_cols, right_cols, source, incoming, arrived = columns_and_inputs
    value, cross = values
    diag, up, down, left, right, base, latest, out = kept
    rows = spare.shape[0]
    vectors, size, _ = out.shape
    place = lax.axis_index("sweep")
    task = task_at(tick, place, lax.axis_size("sweep"), vectors)
    active, vector, rank, forward, half = task

    if any(turns(one) for one in tasks):

        @pl.when(turns(task))
        def _():
            take_lateral(base, vector, left, right, left_cols, right_cols, incoming, spare, 0)
            take_lateral(base, vector, left, right, left_cols, right_cols, arrived, spare, 1)

    @pl.when(active)
    def _():
        known = base[vector]
        value[...] = known
        base[vector] = source[vector]

        def take_chain(matrix, columns):
            spare[...] = gathered(incoming[...], columns[...])
            term = product(matrix, spare, rows)
            value[...] = known - term
            base[vector] = source[vector] - term

        if any(one[0] and one[2] > 0 and one[3] for one in tasks):

            @pl.when((rank > 0) & forward)
            def _():
                take_chain(up, up_cols)

        if any(one[0] and one[2] > 0 and not one[3] for one in tasks):

            @pl.when((rank > 0) & (forward ^ True))
            def _():
                take_chain(down, down_cols)

        spare[...] = value[...]
        fresh = product(diag, spare, rows)
        value[...] = fresh
        latest[vector] = fresh

        if any(one[0] and one[4] == 3 for one in tasks):

            @pl.when(half == 3)
            def _():
                out[vector] = fresh[:size]

    if any(one >= 0 for one in sent):
        chosen = pick(sent, place)

        @pl.when(chosen >= 0)
        def _():
            cross[...] = latest[chosen]


def side_kernel(parity, sent, columns_and_inputs, kept, values, spare):
    left_cols, right_cols, arrived = columns_and_inputs
    left, right, base = kept
    vector = pick(sent, lax.axis_index("sweep"))

    @pl.when(vector >= 0)
    def _():
        take_lateral(base, vector, left, right, left_cols, right_cols, arrived, spare, parity)


def in_vmem(count):
    return [pl.BlockSpec(memory_space=pltpu.VMEM)] * count


def held(shape):
    return pltpu.VMEM(shape, jnp.float32)


def call(kernel, name, fixed, kept, fresh, spare):
    def body(*refs):
        inputs, outputs = refs[: len(fixed)], refs[len(fixed) + len(kept) : -1]
        kernel(inputs, outputs[: len(kept)], outputs[len(kept) :], refs[-1])

    return pl.pallas_call(
        body,
        out_shape=tuple(held(shape) for shape in [*(a.shape for a in kept), *fresh]),
        in_specs=in_vmem(len(fixed) + len(kept)),
        out_specs=tuple(in_vmem(len(fresh) + len(kept))),
        scratch_shapes=[held(spare)],
        input_output_aliases={len(fixed) + n: n for n in range(len(kept))},
        compiler_params=pltpu.CompilerParams(vmem_limit_bytes=VMEM_LIMIT),
        name=name,
    )(*fixed, *kept)


def first_call(block, residual, rows):
    vectors, size, lanes = residual.shape
    several = (vectors, rows, lanes)
    return pl.pallas_call(
        first_kernel,
        out_shape=(held((size, rows, lanes)), held(several), held(several), held((rows, lanes))),
        in_specs=in_vmem(2),
        out_specs=tuple(in_vmem(4)),
        scratch_shapes=[held((rows * rows, lanes))],
        compiler_params=pltpu.CompilerParams(vmem_limit_bytes=VMEM_LIMIT),
        name="first",
    )(block, residual)


def later_call(block, face, base):
    size, _, lanes = block.shape[-3:]
    rows = base.shape[1]
    lead = block.shape[:-3]
    spec = pl.BlockSpec(
        (1,) * len(lead) + block.shape[-3:], lambda step: (0,) * (len(lead) - 1) + (face, 0, 0, 0), memory_space=pltpu.VMEM
    )
    whole = pl.BlockSpec(memory_space=pltpu.VMEM)
    return pl.pallas_call(
        later_kernel,
        grid=(1,),
        out_shape=(held((size, rows, lanes)), held(base.shape)),
        in_specs=[spec, whole],
        out_specs=(whole, whole),
        scratch_shapes=[held((rows * rows, lanes))],
        input_output_aliases={1: 1},
        compiler_params=pltpu.CompilerParams(vmem_limit_bytes=VMEM_LIMIT),
        name="later",
    )(block, base)


def per_device(
    residual_in, diag_inverse, up_block, side_blocks, up_cols, down_cols, left_cols, right_cols
):
    vectors, size, lanes = residual_in.shape[2:]
    rows = size + -size % SUBLANES
    columns = [one.reshape(1, lanes) for one in (up_cols, down_cols, left_cols, right_cols)]
    count = lax.axis_size("sweep")
    parts = lax.axis_size("span")
    ticks = 4 * count + 2 * (vectors - 1)
    sent, urgent = lateral_plan(count, vectors)
    even_pairs = [(p, p + 1) for p in range(0, parts - 1, 2)]
    odd_pairs = [(p, p + 1) for p in range(1, parts - 1, 2)]

    def closed(pairs, members):
        alone = [one for one in members if all(one not in two for two in pairs)]
        return [*pairs, *((b, a) for a, b in pairs), *((one, one) for one in alone)]

    def device(slab, part):
        return slab * parts + part

    diag, base, source, blank = first_call(diag_inverse[0, 0], residual_in[0, 0], rows)
    up = down = left = right = None
    latest, out = pl.pallas_call(
        lambda *refs: None,
        out_shape=(held((vectors, rows, lanes)), held((vectors, size, lanes))),
        out_specs=tuple(in_vmem(2)),
        name="room",
    )()
    incoming = arrived = blank
    late_blocks = [(up_block, 0), (side_blocks, 0), (side_blocks, 1), (side_blocks, 2)]
    mats = [diag, blank, blank, blank, blank]

    for tick in range(ticks):
        tasks = [task_at(tick, place, count, vectors, lambda which, a, b: a if which else b) for place in range(count)]
        used = 1 + sum(mat is not blank for mat in mats[1:])
        *kept, value, cross = call(
            lambda fixed, kept, fresh, spare, used=used, tick=tick, tasks=tasks: task_kernel(
                tick, tasks, sent[tick], fixed, [*kept[:used], *[None] * (5 - used), *kept[used:]], fresh, spare
            ),
            "task",
            (*columns, source, incoming, arrived),
            (*mats[:used], base, latest, out),
            ((rows, lanes), (rows, lanes)),
            (rows, lanes),
        )
        mats[:used] = kept[:used]
        base, latest, out = kept[used:]

        after = [
            task_at(tick + 1, place, count, vectors, lambda which, a, b: a if which else b) for place in range(count)
        ]
        previous, crossing = (arrived, sent[tick - 1] if tick else [-1] * count)
        if any(urgent[tick]) or any(one[0] and one[2] > 0 for one in after):
            swap = [(s, s + 1) for s in range(tick & 1, count - 1, 2)]
            alone = [s for s in range(count) if all(s not in two for two in swap)]
            pairs = [(device(a, p), device(b, p)) for a, b in swap for p in range(parts)]
            pairs += [(device(s, a), device(s, b)) for s in alone for a, b in even_pairs]
            incoming = lax.ppermute(value, ("sweep", "span"), closed(pairs, range(count * parts)))
        if any(one >= 0 for one in sent[tick]):
            arrived = lax.ppermute(cross, "span", closed(odd_pairs if tick & 1 else even_pairs, range(parts)))
        crossing = [-1 if tick and urgent[tick - 1][s] else one for s, one in enumerate(crossing)]
        if any(one >= 0 for one in crossing):
            mats[3], mats[4], base = call(
                functools.partial(side_kernel, (tick - 1) & 1, crossing),
                "side",
                (columns[2], columns[3], previous),
                (mats[3], mats[4], base),
                (),
                (rows, lanes),
            )
        if tick < len(late_blocks):
            mats[1 + tick], base = later_call(*late_blocks[tick], base)
    return out[None, None]


def solution(mesh):
    return jax.shard_map(
        per_device,
        mesh=mesh,
        in_specs=(
            P("sweep", "span", None, None, None),
            P("sweep", "span", None, None, None),
            P("sweep", "span", None, None, None),
            P("sweep", "span", None, None, None, None),
            P("sweep", "span", None),
            P("sweep", "span", None),
            P("sweep", "span", None),
            P("sweep", "span", None),
        ),
        out_specs=P("sweep", "span", None, None, None),
        check_vma=False,
    )
```

time: 260 us -> 237 us (0.912); the launches traced: 260 us -> 234 us
  waiting for transfers between devices: 91.1 us -> 26.5 us
  starting transfers between devices: 125 us -> 160 us
  Pallas kernels: 18.1 us -> 31.9 us
  other arithmetic: 6.49 us -> 0.01 us
  local copies, waits for them, and re-layouts: 18.1 us -> 15.2 us
    ppermute x67 -> x63, waiting for transfers between devices: 91.1 us -> 26.5 us  [the longest x37 16.7 us: per_device(): lax.ppermute(value, ('sweep', 'span'), closed(pairs, range(count * parts)))]
    ppermute x67 -> x63, starting transfers between devices: 125 us -> 160 us  [the longest x37 102 us: per_device(): lax.ppermute(value, ('sweep', 'span'), closed(pairs, range(count * parts)))]
    pallas_call x67 -> x70, Pallas kernels: 18.1 us -> 31.9 us  [the longest x64 24.5 us: call(): pl.pallas_call(body, out_shape=tuple((held(shape) for shape in [*(a.shape...]
    convert_element_type x4 -> x0, other arithmetic: 5.82 us -> none  [turned(): jnp.pad(jnp.transpose(block, (1, 0, 2)), ((0, 0), (0, padded), (0, 0)))]
    unnamed x22 -> x29, local copies, waits for them, and re-layouts: 15.2 us -> 14.4 us
  transfers between devices with their start and end apart: 67 -> 63, of which waited for: 49 -> 28; matrix products, arithmetic and copies ran while one was open for 0% -> 0% of each run, Pallas kernels for 2% -> 4%
where the time goes in v4:
time: 237 us; the launch traced here: 234 us
  starting transfers between devices  160 us (68%)
  Pallas kernels  31.9 us (13%)
  waiting for transfers between devices  26.5 us (11%)
  local copies, waits for them, and re-layouts  15.2 us (6%)
    ppermute x37, starting transfers between devices, per_device(): lax.ppermute(value, ('sweep', 'span'), closed(pairs, range(count * parts)))  102 us
    ppermute x26, starting transfers between devices, per_device(): lax.ppermute(cross, 'span', closed(odd_pairs if tick & 1 else even_pairs,...  57.3 us
    pallas_call x64, Pallas kernels, call(): pl.pallas_call(body, out_shape=tuple((held(shape) for shape in [*(a.shape...  24.5 us
    ppermute x37, waiting for transfers between devices, per_device(): lax.ppermute(value, ('sweep', 'span'), closed(pairs, range(count * parts)))  16.7 us
    unnamed x29, local copies, waits for them, and re-layouts  14.4 us
    ppermute x26, waiting for transfers between devices, per_device(): lax.ppermute(cross, 'span', closed(odd_pairs if tick & 1 else even_pairs,...  9.78 us
    pallas_call x4, Pallas kernels, later_call(): pl.pallas_call(later_kernel, grid=(1,), out_shape=(held((size, rows, lane...  5.89 us
  transfers between devices with their start and end apart: 63, of which 28 were waited for; matrix products, arithmetic and copies ran while one was open for 0% of the time, Pallas kernels for 4%

profile of v4, /device:TPU:0, one launch (start us, length us, event | category | flops | bytes accessed | tf_op | source)
XLA Modules:
  0.0 233.8 jit_solution(14430643328133406043)
XLA Ops:
  17.2 4.5 %collective-permute-start.2 = (f32[104,128]{1,0:T(8,128)S(1)}, f32[104,128]{1,0:T(8,128)S(1)}, u32[]{:S(2)}, u32[]{:S(2)}) collective-permute-start(f32[104,128]{1,0:T(8,128)S(1)} %get-tuple-element.468), channel_id=1, source_target_pairs={{0,4},{1,5},{2,6},{3,7},{8,12},{9,13},{10,14},{11,15},{16,20},{17,... | collective-permute-start | bytes 159752 | tf_op jit(solution)/shard_map/ppermute | solution.py:323
  29.7 5.3 %collective-permute-start.4 = (f32[104,128]{1,0:T(8,128)S(1)}, f32[104,128]{1,0:T(8,128)S(1)}, u32[]{:S(2)}, u32[]{:S(2)}) collective-permute-start(f32[104,128]{1,0:T(8,128)S(1)} %get-tuple-element.487), channel_id=1, source_target_pairs={{0,4},{1,5},{2,6},{3,7},{8,12},{9,13},{10,14},{11,15},{16,20},{17,... | collective-permute-start | bytes 159752 | tf_op jit(solution)/shard_map/ppermute | solution.py:323
  43.1 4.4 %collective-permute-start.8 = (f32[104,128]{1,0:T(8,128)S(1)}, f32[104,128]{1,0:T(8,128)S(1)}, u32[]{:S(2)}, u32[]{:S(2)}) collective-permute-start(f32[104,128]{1,0:T(8,128)S(1)} %get-tuple-element.510), channel_id=1, source_target_pairs={{0,4},{1,5},{2,6},{3,7},{8,12},{9,13},{10,14},{11,15},{16,20},{17,... | collective-permute-start | bytes 159752 | tf_op jit(solution)/shard_map/ppermute | solution.py:323
  51.7 6.1 %collective-permute-start.12 = (f32[104,128]{1,0:T(8,128)S(1)}, f32[104,128]{1,0:T(8,128)S(1)}, u32[]{:S(2)}, u32[]{:S(2)}) collective-permute-start(f32[104,128]{1,0:T(8,128)S(1)} %get-tuple-element.536), channel_id=1, source_target_pairs={{0,4},{1,5},{2,6},{3,7},{8,12},{9,13},{10,14},{11,15},{16,20},{17,... | collective-permute-start | bytes 159752 | tf_op jit(solution)/shard_map/ppermute | solution.py:323
  67.7 4.6 %collective-permute-start.17 = (f32[104,128]{1,0:T(8,128)S(1)}, f32[104,128]{1,0:T(8,128)S(1)}, u32[]{:S(2)}, u32[]{:S(2)}) collective-permute-start(f32[104,128]{1,0:T(8,128)S(1)} %get-tuple-element.563), channel_id=1, source_target_pairs={{0,1},{2,3},{1,0},{3,2},{4,5},{6,7},{5,4},{7,6},{8,9},{10,11},{9,8... | collective-permute-start | bytes 159752 | tf_op jit(solution)/shard_map/ppermute | solution.py:325
  75.1 3.7 %collective-permute-start.20 = (f32[104,128]{1,0:T(8,128)S(1)}, f32[104,128]{1,0:T(8,128)S(1)}, u32[]{:S(2)}, u32[]{:S(2)}) collective-permute-start(f32[104,128]{1,0:T(8,128)S(1)} %get-tuple-element.588), channel_id=1, source_target_pairs={{0,4},{1,5},{2,6},{3,7},{8,12},{9,13},{10,14},{11,15},{16,20},{17,... | collective-permute-start | bytes 159752 | tf_op jit(solution)/shard_map/ppermute | solution.py:323
  78.8 4.5 %collective-permute-start.21 = (f32[104,128]{1,0:T(8,128)S(1)}, f32[104,128]{1,0:T(8,128)S(1)}, u32[]{:S(2)}, u32[]{:S(2)}) collective-permute-start(f32[104,128]{1,0:T(8,128)S(1)} %get-tuple-element.589), channel_id=1, source_target_pairs={{0,1},{2,3},{1,0},{3,2},{4,5},{6,7},{5,4},{7,6},{8,9},{10,11},{9,8... | collective-permute-start | bytes 159752 | tf_op jit(solution)/shard_map/ppermute | solution.py:325
  85.7 9.2 %collective-permute-start.24 = (f32[104,128]{1,0:T(8,128)S(1)}, f32[104,128]{1,0:T(8,128)S(1)}, u32[]{:S(2)}, u32[]{:S(2)}) collective-permute-start(f32[104,128]{1,0:T(8,128)S(1)} %get-tuple-element.614), channel_id=1, source_target_pairs={{0,4},{1,5},{2,6},{3,7},{8,12},{9,13},{10,14},{11,15},{16,20},{17,... | collective-permute-start | bytes 159752 | tf_op jit(solution)/shard_map/ppermute | solution.py:323
  94.9 3.7 %collective-permute-start.25 = (f32[104,128]{1,0:T(8,128)S(1)}, f32[104,128]{1,0:T(8,128)S(1)}, u32[]{:S(2)}, u32[]{:S(2)}) collective-permute-start(f32[104,128]{1,0:T(8,128)S(1)} %get-tuple-element.615), channel_id=1, source_target_pairs={{0,1},{2,3},{1,0},{3,2},{4,5},{6,7},{5,4},{7,6},{8,9},{10,11},{9,8... | collective-permute-start | bytes 159752 | tf_op jit(solution)/shard_map/ppermute | solution.py:325
  103.1 3.7 %collective-permute-start.28 = (f32[104,128]{1,0:T(8,128)S(1)}, f32[104,128]{1,0:T(8,128)S(1)}, u32[]{:S(2)}, u32[]{:S(2)}) collective-permute-start(f32[104,128]{1,0:T(8,128)S(1)} %get-tuple-element.640), channel_id=1, source_target_pairs={{0,4},{1,5},{2,6},{3,7},{8,12},{9,13},{10,14},{11,15},{16,20},{17,... | collective-permute-start | bytes 159752 | tf_op jit(solution)/shard_map/ppermute | solution.py:323
  106.8 4.1 %collective-permute-start.29 = (f32[104,128]{1,0:T(8,128)S(1)}, f32[104,128]{1,0:T(8,128)S(1)}, u32[]{:S(2)}, u32[]{:S(2)}) collective-permute-start(f32[104,128]{1,0:T(8,128)S(1)} %get-tuple-element.641), channel_id=1, source_target_pairs={{0,1},{2,3},{1,0},{3,2},{4,5},{6,7},{5,4},{7,6},{8,9},{10,11},{9,8... | collective-permute-start | bytes 159752 | tf_op jit(solution)/shard_map/ppermute | solution.py:325
  115.6 4.9 %collective-permute-start.32 = (f32[104,128]{1,0:T(8,128)S(1)}, f32[104,128]{1,0:T(8,128)S(1)}, u32[]{:S(2)}, u32[]{:S(2)}) collective-permute-start(f32[104,128]{1,0:T(8,128)S(1)} %get-tuple-element.666), channel_id=1, source_target_pairs={{0,4},{1,5},{2,6},{3,7},{8,12},{9,13},{10,14},{11,15},{16,20},{17,... | collective-permute-start | bytes 159752 | tf_op jit(solution)/shard_map/ppermute | solution.py:323
  120.4 4.4 %collective-permute-start.33 = (f32[104,128]{1,0:T(8,128)S(1)}, f32[104,128]{1,0:T(8,128)S(1)}, u32[]{:S(2)}, u32[]{:S(2)}) collective-permute-start(f32[104,128]{1,0:T(8,128)S(1)} %get-tuple-element.667), channel_id=1, source_target_pairs={{0,1},{2,3},{1,0},{3,2},{4,5},{6,7},{5,4},{7,6},{8,9},{10,11},{9,8... | collective-permute-start | bytes 159752 | tf_op jit(solution)/shard_map/ppermute | solution.py:325
  133.1 3.8 %collective-permute-start.37 = (f32[104,128]{1,0:T(8,128)S(1)}, f32[104,128]{1,0:T(8,128)S(1)}, u32[]{:S(2)}, u32[]{:S(2)}) collective-permute-start(f32[104,128]{1,0:T(8,128)S(1)} %get-tuple-element.693), channel_id=1, source_target_pairs={{0,1},{2,3},{1,0},{3,2},{4,5},{6,7},{5,4},{7,6},{8,9},{10,11},{9,8... | collective-permute-start | bytes 159752 | tf_op jit(solution)/shard_map/ppermute | solution.py:325
  144.2 4.5 %collective-permute-start.41 = (f32[104,128]{1,0:T(8,128)S(1)}, f32[104,128]{1,0:T(8,128)S(1)}, u32[]{:S(2)}, u32[]{:S(2)}) collective-permute-start(f32[104,128]{1,0:T(8,128)S(1)} %get-tuple-element.719), channel_id=1, source_target_pairs={{0,1},{2,3},{1,0},{3,2},{4,5},{6,7},{5,4},{7,6},{8,9},{10,11},{9,8... | collective-permute-start | bytes 159752 | tf_op jit(solution)/shard_map/ppermute | solution.py:325
  151.8 4.4 %collective-permute-start.44 = (f32[104,128]{1,0:T(8,128)S(1)}, f32[104,128]{1,0:T(8,128)S(1)}, u32[]{:S(2)}, u32[]{:S(2)}) collective-permute-start(f32[104,128]{1,0:T(8,128)S(1)} %get-tuple-element.744), channel_id=1, source_target_pairs={{0,4},{1,5},{2,6},{3,7},{8,12},{9,13},{10,14},{11,15},{16,20},{17,... | collective-permute-start | bytes 159752 | tf_op jit(solution)/shard_map/ppermute | solution.py:323
  156.2 4.8 %collective-permute-start.45 = (f32[104,128]{1,0:T(8,128)S(1)}, f32[104,128]{1,0:T(8,128)S(1)}, u32[]{:S(2)}, u32[]{:S(2)}) collective-permute-start(f32[104,128]{1,0:T(8,128)S(1)} %get-tuple-element.745), channel_id=1, source_target_pairs={{0,1},{2,3},{1,0},{3,2},{4,5},{6,7},{5,4},{7,6},{8,9},{10,11},{9,8... | collective-permute-start | bytes 159752 | tf_op jit(solution)/shard_map/ppermute | solution.py:325
  163.5 3.9 %collective-permute-start.48 = (f32[104,128]{1,0:T(8,128)S(1)}, f32[104,128]{1,0:T(8,128)S(1)}, u32[]{:S(2)}, u32[]{:S(2)}) collective-permute-start(f32[104,128]{1,0:T(8,128)S(1)} %get-tuple-element.770), channel_id=1, source_target_pairs={{0,4},{1,5},{2,6},{3,7},{8,12},{9,13},{10,14},{11,15},{16,20},{17,... | collective-permute-start | bytes 159752 | tf_op jit(solution)/shard_map/ppermute | solution.py:323
  167.3 5.5 %collective-permute-start.49 = (f32[104,128]{1,0:T(8,128)S(1)}, f32[104,128]{1,0:T(8,128)S(1)}, u32[]{:S(2)}, u32[]{:S(2)}) collective-permute-start(f32[104,128]{1,0:T(8,128)S(1)} %get-tuple-element.771), channel_id=1, source_target_pairs={{0,1},{2,3},{1,0},{3,2},{4,5},{6,7},{5,4},{7,6},{8,9},{10,11},{9,8... | collective-permute-start | bytes 159752 | tf_op jit(solution)/shard_map/ppermute | solution.py:325
  175.3 3.9 %collective-permute-start.52 = (f32[104,128]{1,0:T(8,128)S(1)}, f32[104,128]{1,0:T(8,128)S(1)}, u32[]{:S(2)}, u32[]{:S(2)}) collective-permute-start(f32[104,128]{1,0:T(8,128)S(1)} %get-tuple-element.796), channel_id=1, source_target_pairs={{0,4},{1,5},{2,6},{3,7},{8,12},{9,13},{10,14},{11,15},{16,20},{17,... | collective-permute-start | bytes 159752 | tf_op jit(solution)/shard_map/ppermute | solution.py:323
  179.1 4.1 %collective-permute-start.53 = (f32[104,128]{1,0:T(8,128)S(1)}, f32[104,128]{1,0:T(8,128)S(1)}, u32[]{:S(2)}, u32[]{:S(2)}) collective-permute-start(f32[104,128]{1,0:T(8,128)S(1)} %get-tuple-element.797), channel_id=1, source_target_pairs={{0,1},{2,3},{1,0},{3,2},{4,5},{6,7},{5,4},{7,6},{8,9},{10,11},{9,8... | collective-permute-start | bytes 159752 | tf_op jit(solution)/shard_map/ppermute | solution.py:325
  186.4 9.0 %collective-permute-start.56 = (f32[104,128]{1,0:T(8,128)S(1)}, f32[104,128]{1,0:T(8,128)S(1)}, u32[]{:S(2)}, u32[]{:S(2)}) collective-permute-start(f32[104,128]{1,0:T(8,128)S(1)} %get-tuple-element.822), channel_id=1, source_target_pairs={{0,4},{1,5},{2,6},{3,7},{8,12},{9,13},{10,14},{11,15},{16,20},{17,... | collective-permute-start | bytes 159752 | tf_op jit(solution)/shard_map/ppermute | solution.py:323
  212.7 5.5 %collective-permute-start.60 = (f32[104,128]{1,0:T(8,128)S(1)}, f32[104,128]{1,0:T(8,128)S(1)}, u32[]{:S(2)}, u32[]{:S(2)}) collective-permute-start(f32[104,128]{1,0:T(8,128)S(1)} %get-tuple-element.861), channel_id=1, source_target_pairs={{0,4},{1,5},{2,6},{3,7},{8,12},{9,13},{10,14},{11,15},{16,20},{17,... | collective-permute-start | bytes 159752 | tf_op jit(solution)/shard_map/ppermute | solution.py:323
  223.6 5.8 %collective-permute-start.62 = (f32[104,128]{1,0:T(8,128)S(1)}, f32[104,128]{1,0:T(8,128)S(1)}, u32[]{:S(2)}, u32[]{:S(2)}) collective-permute-start(f32[104,128]{1,0:T(8,128)S(1)} %get-tuple-element.879), channel_id=1, source_target_pairs={{0,4},{1,5},{2,6},{3,7},{8,12},{9,13},{10,14},{11,15},{16,20},{17,... | collective-permute-start | bytes 159752 | tf_op jit(solution)/shard_map/ppermute | solution.py:323
  (204 shorter events, 114.9 us)
Async XLA Ops:
  17.2 6.6 %collective-permute-start.2 = (f32[104,128]{1,0:T(8,128)S(1)}, f32[104,128]{1,0:T(8,128)S(1)}, u32[]{:S(2)}, u32[]{:S(2)}) collective-permute-start(f32[104,128]{1,0:T(8,128)S(1)} %get-tuple-element.468), channel_id=1, source_target_pairs={{0,4},{1,5},{2,6},{3,7},{8,12},{9,13},{10,14},{11,15},{16,20},{17,... | collective-permute-start | bytes 159752 | tf_op jit(solution)/shard_map/ppermute | solution.py:323
  29.7 7.4 %collective-permute-start.4 = (f32[104,128]{1,0:T(8,128)S(1)}, f32[104,128]{1,0:T(8,128)S(1)}, u32[]{:S(2)}, u32[]{:S(2)}) collective-permute-start(f32[104,128]{1,0:T(8,128)S(1)} %get-tuple-element.487), channel_id=1, source_target_pairs={{0,4},{1,5},{2,6},{3,7},{8,12},{9,13},{10,14},{11,15},{16,20},{17,... | collective-permute-start | bytes 159752 | tf_op jit(solution)/shard_map/ppermute | solution.py:323
  43.1 6.6 %collective-permute-start.8 = (f32[104,128]{1,0:T(8,128)S(1)}, f32[104,128]{1,0:T(8,128)S(1)}, u32[]{:S(2)}, u32[]{:S(2)}) collective-permute-start(f32[104,128]{1,0:T(8,128)S(1)} %get-tuple-element.510), channel_id=1, source_target_pairs={{0,4},{1,5},{2,6},{3,7},{8,12},{9,13},{10,14},{11,15},{16,20},{17,... | collective-permute-start | bytes 159752 | tf_op jit(solution)/shard_map/ppermute | solution.py:323
  51.7 9.7 %collective-permute-start.12 = (f32[104,128]{1,0:T(8,128)S(1)}, f32[104,128]{1,0:T(8,128)S(1)}, u32[]{:S(2)}, u32[]{:S(2)}) collective-permute-start(f32[104,128]{1,0:T(8,128)S(1)} %get-tuple-element.536), channel_id=1, source_target_pairs={{0,4},{1,5},{2,6},{3,7},{8,12},{9,13},{10,14},{11,15},{16,20},{17,... | collective-permute-start | bytes 159752 | tf_op jit(solution)/shard_map/ppermute | solution.py:323
  64.2 8.1 %collective-permute-start.16 = (f32[104,128]{1,0:T(8,128)S(1)}, f32[104,128]{1,0:T(8,128)S(1)}, u32[]{:S(2)}, u32[]{:S(2)}) collective-permute-start(f32[104,128]{1,0:T(8,128)S(1)} %get-tuple-element.562), channel_id=1, source_target_pairs={{0,4},{1,5},{2,6},{3,7},{8,12},{9,13},{10,14},{11,15},{16,20},{17,... | collective-permute-start | bytes 159752 | tf_op jit(solution)/shard_map/ppermute | solution.py:323
  67.7 5.5 %collective-permute-start.17 = (f32[104,128]{1,0:T(8,128)S(1)}, f32[104,128]{1,0:T(8,128)S(1)}, u32[]{:S(2)}, u32[]{:S(2)}) collective-permute-start(f32[104,128]{1,0:T(8,128)S(1)} %get-tuple-element.563), channel_id=1, source_target_pairs={{0,1},{2,3},{1,0},{3,2},{4,5},{6,7},{5,4},{7,6},{8,9},{10,11},{9,8... | collective-permute-start | bytes 159752 | tf_op jit(solution)/shard_map/ppermute | solution.py:325
  75.1 8.2 %collective-permute-start.20 = (f32[104,128]{1,0:T(8,128)S(1)}, f32[104,128]{1,0:T(8,128)S(1)}, u32[]{:S(2)}, u32[]{:S(2)}) collective-permute-start(f32[104,128]{1,0:T(8,128)S(1)} %get-tuple-element.588), channel_id=1, source_target_pairs={{0,4},{1,5},{2,6},{3,7},{8,12},{9,13},{10,14},{11,15},{16,20},{17,... | collective-permute-start | bytes 159752 | tf_op jit(solution)/shard_map/ppermute | solution.py:323
  78.8 5.4 %collective-permute-start.21 = (f32[104,128]{1,0:T(8,128)S(1)}, f32[104,128]{1,0:T(8,128)S(1)}, u32[]{:S(2)}, u32[]{:S(2)}) collective-permute-start(f32[104,128]{1,0:T(8,128)S(1)} %get-tuple-element.589), channel_id=1, source_target_pairs={{0,1},{2,3},{1,0},{3,2},{4,5},{6,7},{5,4},{7,6},{8,9},{10,11},{9,8... | collective-permute-start | bytes 159752 | tf_op jit(solution)/shard_map/ppermute | solution.py:325
  85.7 12.9 %collective-permute-start.24 = (f32[104,128]{1,0:T(8,128)S(1)}, f32[104,128]{1,0:T(8,128)S(1)}, u32[]{:S(2)}, u32[]{:S(2)}) collective-permute-start(f32[104,128]{1,0:T(8,128)S(1)} %get-tuple-element.614), channel_id=1, source_target_pairs={{0,4},{1,5},{2,6},{3,7},{8,12},{9,13},{10,14},{11,15},{16,20},{17,... | collective-permute-start | bytes 159752 | tf_op jit(solution)/shard_map/ppermute | solution.py:323
  103.1 7.8 %collective-permute-start.28 = (f32[104,128]{1,0:T(8,128)S(1)}, f32[104,128]{1,0:T(8,128)S(1)}, u32[]{:S(2)}, u32[]{:S(2)}) collective-permute-start(f32[104,128]{1,0:T(8,128)S(1)} %get-tuple-element.640), channel_id=1, source_target_pairs={{0,4},{1,5},{2,6},{3,7},{8,12},{9,13},{10,14},{11,15},{16,20},{17,... | collective-permute-start | bytes 159752 | tf_op jit(solution)/shard_map/ppermute | solution.py:323
  115.6 9.3 %collective-permute-start.32 = (f32[104,128]{1,0:T(8,128)S(1)}, f32[104,128]{1,0:T(8,128)S(1)}, u32[]{:S(2)}, u32[]{:S(2)}) collective-permute-start(f32[104,128]{1,0:T(8,128)S(1)} %get-tuple-element.666), channel_id=1, source_target_pairs={{0,4},{1,5},{2,6},{3,7},{8,12},{9,13},{10,14},{11,15},{16,20},{17,... | collective-permute-start | bytes 159752 | tf_op jit(solution)/shard_map/ppermute | solution.py:323
  120.4 5.3 %collective-permute-start.33 = (f32[104,128]{1,0:T(8,128)S(1)}, f32[104,128]{1,0:T(8,128)S(1)}, u32[]{:S(2)}, u32[]{:S(2)}) collective-permute-start(f32[104,128]{1,0:T(8,128)S(1)} %get-tuple-element.667), channel_id=1, source_target_pairs={{0,1},{2,3},{1,0},{3,2},{4,5},{6,7},{5,4},{7,6},{8,9},{10,11},{9,8... | collective-permute-start | bytes 159752 | tf_op jit(solution)/shard_map/ppermute | solution.py:325
  129.5 7.4 %collective-permute-start.36 = (f32[104,128]{1,0:T(8,128)S(1)}, f32[104,128]{1,0:T(8,128)S(1)}, u32[]{:S(2)}, u32[]{:S(2)}) collective-permute-start(f32[104,128]{1,0:T(8,128)S(1)} %get-tuple-element.692), channel_id=1, source_target_pairs={{0,4},{1,5},{2,6},{3,7},{8,12},{9,13},{10,14},{11,15},{16,20},{17,... | collective-permute-start | bytes 159752 | tf_op jit(solution)/shard_map/ppermute | solution.py:323
  141.5 7.2 %collective-permute-start.40 = (f32[104,128]{1,0:T(8,128)S(1)}, f32[104,128]{1,0:T(8,128)S(1)}, u32[]{:S(2)}, u32[]{:S(2)}) collective-permute-start(f32[104,128]{1,0:T(8,128)S(1)} %get-tuple-element.718), channel_id=1, source_target_pairs={{0,4},{1,5},{2,6},{3,7},{8,12},{9,13},{10,14},{11,15},{16,20},{17,... | collective-permute-start | bytes 159752 | tf_op jit(solution)/shard_map/ppermute | solution.py:323
  144.2 5.4 %collective-permute-start.41 = (f32[104,128]{1,0:T(8,128)S(1)}, f32[104,128]{1,0:T(8,128)S(1)}, u32[]{:S(2)}, u32[]{:S(2)}) collective-permute-start(f32[104,128]{1,0:T(8,128)S(1)} %get-tuple-element.719), channel_id=1, source_target_pairs={{0,1},{2,3},{1,0},{3,2},{4,5},{6,7},{5,4},{7,6},{8,9},{10,11},{9,8... | collective-permute-start | bytes 159752 | tf_op jit(solution)/shard_map/ppermute | solution.py:325
  151.8 9.2 %collective-permute-start.44 = (f32[104,128]{1,0:T(8,128)S(1)}, f32[104,128]{1,0:T(8,128)S(1)}, u32[]{:S(2)}, u32[]{:S(2)}) collective-permute-start(f32[104,128]{1,0:T(8,128)S(1)} %get-tuple-element.744), channel_id=1, source_target_pairs={{0,4},{1,5},{2,6},{3,7},{8,12},{9,13},{10,14},{11,15},{16,20},{17,... | collective-permute-start | bytes 159752 | tf_op jit(solution)/shard_map/ppermute | solution.py:323
  156.2 5.7 %collective-permute-start.45 = (f32[104,128]{1,0:T(8,128)S(1)}, f32[104,128]{1,0:T(8,128)S(1)}, u32[]{:S(2)}, u32[]{:S(2)}) collective-permute-start(f32[104,128]{1,0:T(8,128)S(1)} %get-tuple-element.745), channel_id=1, source_target_pairs={{0,1},{2,3},{1,0},{3,2},{4,5},{6,7},{5,4},{7,6},{8,9},{10,11},{9,8... | collective-permute-start | bytes 159752 | tf_op jit(solution)/shard_map/ppermute | solution.py:325
  163.5 9.3 %collective-permute-start.48 = (f32[104,128]{1,0:T(8,128)S(1)}, f32[104,128]{1,0:T(8,128)S(1)}, u32[]{:S(2)}, u32[]{:S(2)}) collective-permute-start(f32[104,128]{1,0:T(8,128)S(1)} %get-tuple-element.770), channel_id=1, source_target_pairs={{0,4},{1,5},{2,6},{3,7},{8,12},{9,13},{10,14},{11,15},{16,20},{17,... | collective-permute-start | bytes 159752 | tf_op jit(solution)/shard_map/ppermute | solution.py:323
  167.3 6.3 %collective-permute-start.49 = (f32[104,128]{1,0:T(8,128)S(1)}, f32[104,128]{1,0:T(8,128)S(1)}, u32[]{:S(2)}, u32[]{:S(2)}) collective-permute-start(f32[104,128]{1,0:T(8,128)S(1)} %get-tuple-element.771), channel_id=1, source_target_pairs={{0,1},{2,3},{1,0},{3,2},{4,5},{6,7},{5,4},{7,6},{8,9},{10,11},{9,8... | collective-permute-start | bytes 159752 | tf_op jit(solution)/shard_map/ppermute | solution.py:325
  175.3 8.0 %collective-permute-start.52 = (f32[104,128]{1,0:T(8,128)S(1)}, f32[104,128]{1,0:T(8,128)S(1)}, u32[]{:S(2)}, u32[]{:S(2)}) collective-permute-start(f32[104,128]{1,0:T(8,128)S(1)} %get-tuple-element.796), channel_id=1, source_target_pairs={{0,4},{1,5},{2,6},{3,7},{8,12},{9,13},{10,14},{11,15},{16,20},{17,... | collective-permute-start | bytes 159752 | tf_op jit(solution)/shard_map/ppermute | solution.py:323
  186.4 11.1 %collective-permute-start.56 = (f32[104,128]{1,0:T(8,128)S(1)}, f32[104,128]{1,0:T(8,128)S(1)}, u32[]{:S(2)}, u32[]{:S(2)}) collective-permute-start(f32[104,128]{1,0:T(8,128)S(1)} %get-tuple-element.822), channel_id=1, source_target_pairs={{0,4},{1,5},{2,6},{3,7},{8,12},{9,13},{10,14},{11,15},{16,20},{17,... | collective-permute-start | bytes 159752 | tf_op jit(solution)/shard_map/ppermute | solution.py:323
  203.7 5.1 %collective-permute-start.58 = (f32[104,128]{1,0:T(8,128)S(1)}, f32[104,128]{1,0:T(8,128)S(1)}, u32[]{:S(2)}, u32[]{:S(2)}) collective-permute-start(f32[104,128]{1,0:T(8,128)S(1)} %get-tuple-element.843), channel_id=1, source_target_pairs={{0,4},{1,5},{2,6},{3,7},{8,12},{9,13},{10,14},{11,15},{16,20},{17,... | collective-permute-start | bytes 159752 | tf_op jit(solution)/shard_map/ppermute | solution.py:323
  212.7 7.6 %collective-permute-start.60 = (f32[104,128]{1,0:T(8,128)S(1)}, f32[104,128]{1,0:T(8,128)S(1)}, u32[]{:S(2)}, u32[]{:S(2)}) collective-permute-start(f32[104,128]{1,0:T(8,128)S(1)} %get-tuple-element.861), channel_id=1, source_target_pairs={{0,4},{1,5},{2,6},{3,7},{8,12},{9,13},{10,14},{11,15},{16,20},{17,... | collective-permute-start | bytes 159752 | tf_op jit(solution)/shard_map/ppermute | solution.py:323
  223.6 7.9 %collective-permute-start.62 = (f32[104,128]{1,0:T(8,128)S(1)}, f32[104,128]{1,0:T(8,128)S(1)}, u32[]{:S(2)}, u32[]{:S(2)}) collective-permute-start(f32[104,128]{1,0:T(8,128)S(1)} %get-tuple-element.879), channel_id=1, source_target_pairs={{0,4},{1,5},{2,6},{3,7},{8,12},{9,13},{10,14},{11,15},{16,20},{17,... | collective-permute-start | bytes 159752 | tf_op jit(solution)/shard_map/ppermute | solution.py:323
  (53 other events, 118.3 us)

commit v5 on v4

--- a/solution.py
+++ b/solution.py
@@ -8,8 +8,10 @@
 from jax.sharding import PartitionSpec as P
 
 SUBLANES = 8
-VMEM_LIMIT = 16 * 1024 * 1024
+VMEM_LIMIT = 2 * 1024 * 1024
+PREPARE_LIMIT = 12 * 1024 * 1024
 LATERAL_START = 4
+CHUNKS = 4
 
 
 def task_at(tick, place, count, vectors, choose=jnp.where):
@@ -97,17 +99,25 @@
         base[vector] = base[vector] - product(left, spare, rows)
 
 
-def prepare_kernel(block, ready, wide):
-    size, _, lanes = block.shape[-3:]
+def prepare(block, ready, narrow, wide, sems):
+    size, _, lanes = block.shape
     rows = ready.shape[1]
-    lead = (0,) * (len(block.shape) - 3)
+    share = size // CHUNKS
+    copies = [
+        pltpu.make_async_copy(block.at[pl.ds(n * share, share)], narrow.at[pl.ds(n * share, share)], sems.at[n])
+        for n in range(CHUNKS)
+    ]
+    for copy in copies:
+        copy.start()
     wide[pl.ds(size * rows, (rows - size) * rows), :] = jnp.zeros(((rows - size) * rows, lanes), jnp.float32)
 
     def widen(i, _):
-        wide[pl.ds(pl.multiple_of(i * rows, SUBLANES), size), :] = block[(*lead, i)].astype(jnp.float32)
+        wide[pl.ds(pl.multiple_of(i * rows, SUBLANES), size), :] = narrow[i].astype(jnp.float32)
         return 0
 
-    lax.fori_loop(0, size, widen, 0, unroll=4)
+    for n, copy in enumerate(copies):
+        copy.wait()
+        lax.fori_loop(n * share, (n + 1) * share, widen, 0, unroll=5)
 
     def turn(j, _):
         for i in range(0, rows, SUBLANES):
@@ -117,18 +127,29 @@
     lax.fori_loop(0, size, turn, 0, unroll=4)
 
 
-def first_kernel(block, residual, ready, base, source, blank, wide):
-    prepare_kernel(block, ready, wide)
+def first_kernel(block, residual, *refs):
+    hbm_columns, (ready, base, source, blank, *columns), (narrow, wide, sems, column_sems) = (
+        refs[:4], refs[4:12], refs[12:]
+    )
+    copies = [
+        pltpu.make_async_copy(there, here, column_sems.at[n])
+        for n, (there, here) in enumerate(zip(hbm_columns, columns))
+    ]
+    for copy in copies:
+        copy.start()
+    prepare(block, ready, narrow, wide, sems)
     vectors, size, lanes = residual.shape
     rows = base.shape[1]
     base[:, pl.ds(rows - SUBLANES, SUBLANES), :] = jnp.zeros((vectors, SUBLANES, lanes), jnp.float32)
     base[:, pl.ds(0, size), :] = residual[...]
     source[...] = base[...]
     blank[...] = jnp.zeros_like(blank)
-
-
-def later_kernel(block, base_in, ready, base, wide):
-    prepare_kernel(block, ready, wide)
+    for copy in copies:
+        copy.wait()
+
+
+def later_kernel(face, block, base_in, ready, base, narrow, wide, sems):
+    prepare(block.at[(0,) * (len(block.shape) - 4) + (face,)], ready, narrow, wide, sems)
 
 
 def task_kernel(
@@ -207,6 +228,10 @@
     return [pl.BlockSpec(memory_space=pltpu.VMEM)] * count
 
 
+def far(array):
+    return pltpu.with_memory_space_constraint(array, pltpu.HBM)
+
+
 def held(shape):
     return pltpu.VMEM(shape, jnp.float32)
 
@@ -228,39 +253,45 @@
     )(*fixed, *kept)
 
 
-def first_call(block, residual, rows):
+def preparing(size, rows, lanes):
+    return [
+        pltpu.VMEM((size, size, lanes), jnp.bfloat16),
+        held((rows * rows, lanes)),
+        pltpu.SemaphoreType.DMA((CHUNKS,)),
+    ]
+
+
+def first_call(block, residual, columns, rows):
     vectors, size, lanes = residual.shape
     several = (vectors, rows, lanes)
+    in_hbm = pl.BlockSpec(memory_space=pltpu.HBM)
     return pl.pallas_call(
         first_kernel,
-        out_shape=(held((size, rows, lanes)), held(several), held(several), held((rows, lanes))),
-        in_specs=in_vmem(2),
-        out_specs=tuple(in_vmem(4)),
-        scratch_shapes=[held((rows * rows, lanes))],
-        compiler_params=pltpu.CompilerParams(vmem_limit_bytes=VMEM_LIMIT),
+        out_shape=(
+            held((size, rows, lanes)), held(several), held(several), held((rows, lanes)),
+            *(pltpu.VMEM(one.shape, one.dtype) for one in columns),
+        ),
+        in_specs=[in_hbm, *in_vmem(1), *[in_hbm] * 4],
+        out_specs=tuple(in_vmem(8)),
+        scratch_shapes=[*preparing(size, rows, lanes), pltpu.SemaphoreType.DMA((4,))],
+        compiler_params=pltpu.CompilerParams(vmem_limit_bytes=PREPARE_LIMIT),
         name="first",
-    )(block, residual)
+    )(far(block), residual, *(far(one) for one in columns))
 
 
 def later_call(block, face, base):
     size, _, lanes = block.shape[-3:]
     rows = base.shape[1]
-    lead = block.shape[:-3]
-    spec = pl.BlockSpec(
-        (1,) * len(lead) + block.shape[-3:], lambda step: (0,) * (len(lead) - 1) + (face, 0, 0, 0), memory_space=pltpu.VMEM
-    )
-    whole = pl.BlockSpec(memory_space=pltpu.VMEM)
     return pl.pallas_call(
-        later_kernel,
-        grid=(1,),
+        functools.partial(later_kernel, face),
         out_shape=(held((size, rows, lanes)), held(base.shape)),
-        in_specs=[spec, whole],
-        out_specs=(whole, whole),
-        scratch_shapes=[held((rows * rows, lanes))],
+        in_specs=[pl.BlockSpec(memory_space=pltpu.HBM), *in_vmem(1)],
+        out_specs=tuple(in_vmem(2)),
+        scratch_shapes=preparing(size, rows, lanes),
         input_output_aliases={1: 1},
-        compiler_params=pltpu.CompilerParams(vmem_limit_bytes=VMEM_LIMIT),
+        compiler_params=pltpu.CompilerParams(vmem_limit_bytes=PREPARE_LIMIT),
         name="later",
-    )(block, base)
+    )(far(block), base)
 
 
 def per_device(
@@ -283,8 +314,7 @@
     def device(slab, part):
         return slab * parts + part
 
-    diag, base, source, blank = first_call(diag_inverse[0, 0], residual_in[0, 0], rows)
-    up = down = left = right = None
+    diag, base, source, blank, *columns = first_call(diag_inverse[0, 0], residual_in[0, 0], columns, rows)
     latest, out = pl.pallas_call(
         lambda *refs: None,
         out_shape=(held((vectors, rows, lanes)), held((vectors, size, lanes))),
@@ -292,18 +322,22 @@
         name="room",
     )()
     incoming = arrived = blank
-    late_blocks = [(up_block, 0), (side_blocks, 0), (side_blocks, 1), (side_blocks, 2)]
+    late_blocks = [(up_block, 0), *((side_blocks, face) for face in range(3))]
     mats = [diag, blank, blank, blank, blank]
 
+    def tasks_at(tick):
+        return [task_at(tick, place, count, vectors, lambda which, a, b: a if which else b) for place in range(count)]
+
     for tick in range(ticks):
-        tasks = [task_at(tick, place, count, vectors, lambda which, a, b: a if which else b) for place in range(count)]
+        tasks = tasks_at(tick)
         used = 1 + sum(mat is not blank for mat in mats[1:])
+        turning = any(turns(one) for one in tasks)
         *kept, value, cross = call(
             lambda fixed, kept, fresh, spare, used=used, tick=tick, tasks=tasks: task_kernel(
                 tick, tasks, sent[tick], fixed, [*kept[:used], *[None] * (5 - used), *kept[used:]], fresh, spare
             ),
             "task",
-            (*columns, source, incoming, arrived),
+            (*columns, source, incoming, arrived if turning else blank),
             (*mats[:used], base, latest, out),
             ((rows, lanes), (rows, lanes)),
             (rows, lanes),
@@ -311,22 +345,24 @@
         mats[:used] = kept[:used]
         base, latest, out = kept[used:]
 
-        after = [
-            task_at(tick + 1, place, count, vectors, lambda which, a, b: a if which else b) for place in range(count)
-        ]
-        previous, crossing = (arrived, sent[tick - 1] if tick else [-1] * count)
-        if any(urgent[tick]) or any(one[0] and one[2] > 0 for one in after):
+        previous = arrived
+        if any(urgent[tick]) or any(one[0] and one[2] > 0 for one in tasks_at(tick + 1)):
             swap = [(s, s + 1) for s in range(tick & 1, count - 1, 2)]
             alone = [s for s in range(count) if all(s not in two for two in swap)]
             pairs = [(device(a, p), device(b, p)) for a, b in swap for p in range(parts)]
             pairs += [(device(s, a), device(s, b)) for s in alone for a, b in even_pairs]
             incoming = lax.ppermute(value, ("sweep", "span"), closed(pairs, range(count * parts)))
         if any(one >= 0 for one in sent[tick]):
-            arrived = lax.ppermute(cross, "span", closed(odd_pairs if tick & 1 else even_pairs, range(parts)))
-        crossing = [-1 if tick and urgent[tick - 1][s] else one for s, one in enumerate(crossing)]
-        if any(one >= 0 for one in crossing):
+            pairs = [
+                (device(s, a), device(s, b))
+                for s in range(count)
+                for a, b in (odd_pairs if sent[tick][s] >= 0 and (urgent[tick][s] or not tick & 1) else even_pairs)
+            ]
+            arrived = lax.ppermute(cross, ("sweep", "span"), closed(pairs, range(count * parts)))
+        came = [-1 if not tick or urgent[tick - 1][s] else sent[tick - 1][s] for s in range(count)]
+        if any(one >= 0 for one in came):
             mats[3], mats[4], base = call(
-                functools.partial(side_kernel, (tick - 1) & 1, crossing),
+                functools.partial(side_kernel, tick & 1, came),
                 "side",
                 (columns[2], columns[3], previous),
                 (mats[3], mats[4], base),

time: 237 us -> 213 us (0.90); the launches traced: 234 us -> 212 us
  starting transfers between devices: 160 us -> 136 us
  local copies, waits for them, and re-layouts: 15.2 us -> 1.68 us
  waiting for transfers between devices: 26.5 us -> 34.9 us
  Pallas kernels: 31.9 us -> 39.2 us
    ppermute x26, starting transfers between devices: 57.3 us -> 33 us  [per_device(): lax.ppermute(cross, ('sweep', 'span'), closed(pairs, range(count * parts)))]
    unnamed x29 -> x1, local copies, waits for them, and re-layouts: 14.4 us -> 0.94 us
    ppermute x37, waiting for transfers between devices: 16.7 us -> 25.9 us  [per_device(): lax.ppermute(value, ('sweep', 'span'), closed(pairs, range(count * parts)))]
    pallas_call x4, Pallas kernels: 5.89 us -> 11.5 us  [later_call(): pl.pallas_call(functools.partial(later_kernel, face), out_shape=(held((si...]
  transfers between devices with their start and end apart: 63 -> 63, of which waited for: 28 -> 29; matrix products, arithmetic and copies ran while one was open for 0% -> 0% of each run, Pallas kernels for 4% -> 9%
where the time goes in v5:
time: 213 us; the launch traced here: 212 us
  starting transfers between devices  136 us (64%)
  Pallas kernels  39.2 us (18%)
  waiting for transfers between devices  34.9 us (16%)
    ppermute x37, starting transfers between devices, per_device(): lax.ppermute(value, ('sweep', 'span'), closed(pairs, range(count * parts)))  103 us
    ppermute x26, starting transfers between devices, per_device(): lax.ppermute(cross, ('sweep', 'span'), closed(pairs, range(count * parts)))  33 us
    ppermute x37, waiting for transfers between devices, per_device(): lax.ppermute(value, ('sweep', 'span'), closed(pairs, range(count * parts)))  25.9 us
    pallas_call x64, Pallas kernels, call(): pl.pallas_call(body, out_shape=tuple((held(shape) for shape in [*(a.shape...  24.7 us
    pallas_call x4, Pallas kernels, later_call(): pl.pallas_call(functools.partial(later_kernel, face), out_shape=(held((si...  11.5 us
    ppermute x26, waiting for transfers between devices, per_device(): lax.ppermute(cross, ('sweep', 'span'), closed(pairs, range(count * parts)))  9.04 us
  transfers between devices with their start and end apart: 63, of which 29 were waited for; matrix products, arithmetic and copies ran while one was open for 0% of the time, Pallas kernels for 9%

profile of v5, /device:TPU:0, one launch (start us, length us, event | category | flops | bytes accessed | tf_op | source)
XLA Modules:
  0.0 212.3 jit_solution(5916759752723429163)
XLA Ops:
  0.9 3.0 %first.1 = (f32[100,104,128]{2,1,0:T(8,128)S(1)}, f32[4,104,128]{2,1,0:T(8,128)S(1)}, f32[4,104,128]{2,1,0:T(8,128)S(1)}, f32[104,128]{1,0:T(8,128)S(1)}, s32[1,...) custom-call(bf16[100,100,128]{2,1,0:T(8,128)(2,1)} %bitcast.11, ...), custom_call_target="tpu_custom_call" | custom-call | tf_op jit(solution)/shard_map/first/pallas_call | solution.py:268
  5.1 2.5 %collective-permute-start = (f32[104,128]{1,0:T(8,128)S(1)}, f32[104,128]{1,0:T(8,128)S(1)}, u32[]{:S(2)}, u32[]{:S(2)}) collective-permute-start(f32[104,128]{1,0:T(8,128)S(1)} %get-tuple-element.461), channel_id=1, source_target_pairs={{0,4},{1,5},{2,6},{3,7},{8,12},{9,13},{10,14},{11,15},{16,20},{17,... | collective-permute-start | bytes 159752 | tf_op jit(solution)/shard_map/ppermute | solution.py:354
  7.6 2.9 %later.4 = (f32[100,104,128]{2,1,0:T(8,128)S(1)}, f32[4,104,128]{2,1,0:T(8,128)S(1)}) custom-call(bf16[1,1,100,100,128]{4,3,2,1,0:T(8,128)(2,1)} %block.4, f32[4,104,128]{2,1,0:T(8,128)S(1)} %get-tuple-element.463.base_in), custom_call_target="tpu_custom_call", output_to_operand_aliasing={{1}: (1, {})} | custom-call | tf_op jit(solution)/shard_map/later/pallas_call | solution.py:285
  11.1 2.9 %later.5 = (f32[100,104,128]{2,1,0:T(8,128)S(1)}, f32[4,104,128]{2,1,0:T(8,128)S(1)}) custom-call(bf16[1,1,3,100,100,128]{5,4,3,2,1,0:T(8,128)(2,1)} %block.7, f32[4,104,128]{2,1,0:T(8,128)S(1)} %get-tuple-element.471.base_in), custom_call_target="tpu_custom_call", output_to_operand_aliasing={{1}: (1, {})} | custom-call | tf_op jit(solution)/shard_map/later/pallas_call | solution.py:285
  15.1 3.8 %collective-permute-start.2 = (f32[104,128]{1,0:T(8,128)S(1)}, f32[104,128]{1,0:T(8,128)S(1)}, u32[]{:S(2)}, u32[]{:S(2)}) collective-permute-start(f32[104,128]{1,0:T(8,128)S(1)} %get-tuple-element.476), channel_id=1, source_target_pairs={{0,4},{1,5},{2,6},{3,7},{8,12},{9,13},{10,14},{11,15},{16,20},{17,... | collective-permute-start | bytes 159752 | tf_op jit(solution)/shard_map/ppermute | solution.py:354
  18.9 2.9 %later.6 = (f32[100,104,128]{2,1,0:T(8,128)S(1)}, f32[4,104,128]{2,1,0:T(8,128)S(1)}) custom-call(bf16[1,1,3,100,100,128]{5,4,3,2,1,0:T(8,128)(2,1)} %block.7, f32[4,104,128]{2,1,0:T(8,128)S(1)} %get-tuple-element.480.base_in), custom_call_target="tpu_custom_call", output_to_operand_aliasing={{1}: (1, {})} | custom-call | tf_op jit(solution)/shard_map/later/pallas_call | solution.py:285
  22.4 2.9 %later.7 = (f32[100,104,128]{2,1,0:T(8,128)S(1)}, f32[4,104,128]{2,1,0:T(8,128)S(1)}) custom-call(bf16[1,1,3,100,100,128]{5,4,3,2,1,0:T(8,128)(2,1)} %block.7, f32[4,104,128]{2,1,0:T(8,128)S(1)} %get-tuple-element.490.base_in), custom_call_target="tpu_custom_call", output_to_operand_aliasing={{1}: (1, {})} | custom-call | tf_op jit(solution)/shard_map/later/pallas_call | solution.py:285
  25.7 3.9 %collective-permute-start.4 = (f32[104,128]{1,0:T(8,128)S(1)}, f32[104,128]{1,0:T(8,128)S(1)}, u32[]{:S(2)}, u32[]{:S(2)}) collective-permute-start(f32[104,128]{1,0:T(8,128)S(1)} %get-tuple-element.495), channel_id=1, source_target_pairs={{0,4},{1,5},{2,6},{3,7},{8,12},{9,13},{10,14},{11,15},{16,20},{17,... | collective-permute-start | bytes 159752 | tf_op jit(solution)/shard_map/ppermute | solution.py:354
  34.6 5.2 %collective-permute-start.7 = (f32[104,128]{1,0:T(8,128)S(1)}, f32[104,128]{1,0:T(8,128)S(1)}, u32[]{:S(2)}, u32[]{:S(2)}) collective-permute-start(f32[104,128]{1,0:T(8,128)S(1)} %get-tuple-element.517), channel_id=1, source_target_pairs={{0,4},{1,5},{2,6},{3,7},{8,12},{9,13},{10,14},{11,15},{16,20},{17,... | collective-permute-start | bytes 159752 | tf_op jit(solution)/shard_map/ppermute | solution.py:354
  47.1 2.9 %collective-permute-start.12 = (f32[104,128]{1,0:T(8,128)S(1)}, f32[104,128]{1,0:T(8,128)S(1)}, u32[]{:S(2)}, u32[]{:S(2)}) collective-permute-start(f32[104,128]{1,0:T(8,128)S(1)} %get-tuple-element.544), channel_id=1, source_target_pairs={{0,4},{1,5},{2,6},{3,7},{8,12},{9,13},{10,14},{11,15},{16,20},{17,... | collective-permute-start | bytes 159752 | tf_op jit(solution)/shard_map/ppermute | solution.py:354
  61.7 2.4 %collective-permute-start.17 = (f32[104,128]{1,0:T(8,128)S(1)}, f32[104,128]{1,0:T(8,128)S(1)}, u32[]{:S(2)}, u32[]{:S(2)}) collective-permute-start(f32[104,128]{1,0:T(8,128)S(1)} %get-tuple-element.582), channel_id=1, source_target_pairs={{4,8},{5,9},{6,10},{7,11},{12,16},{13,17},{14,18},{15,19},{20,24},... | collective-permute-start | bytes 159752 | tf_op jit(solution)/shard_map/ppermute | solution.py:354
  67.3 2.7 %collective-permute-start.20 = (f32[104,128]{1,0:T(8,128)S(1)}, f32[104,128]{1,0:T(8,128)S(1)}, u32[]{:S(2)}, u32[]{:S(2)}) collective-permute-start(f32[104,128]{1,0:T(8,128)S(1)} %get-tuple-element.596), channel_id=1, source_target_pairs={{0,4},{1,5},{2,6},{3,7},{8,12},{9,13},{10,14},{11,15},{16,20},{17,... | collective-permute-start | bytes 159752 | tf_op jit(solution)/shard_map/ppermute | solution.py:354
  76.1 7.1 %collective-permute-start.24 = (f32[104,128]{1,0:T(8,128)S(1)}, f32[104,128]{1,0:T(8,128)S(1)}, u32[]{:S(2)}, u32[]{:S(2)}) collective-permute-start(f32[104,128]{1,0:T(8,128)S(1)} %get-tuple-element.622), channel_id=1, source_target_pairs={{0,4},{1,5},{2,6},{3,7},{8,12},{9,13},{10,14},{11,15},{16,20},{17,... | collective-permute-start | bytes 159752 | tf_op jit(solution)/shard_map/ppermute | solution.py:354
  88.6 6.5 %collective-permute-start.28 = (f32[104,128]{1,0:T(8,128)S(1)}, f32[104,128]{1,0:T(8,128)S(1)}, u32[]{:S(2)}, u32[]{:S(2)}) collective-permute-start(f32[104,128]{1,0:T(8,128)S(1)} %get-tuple-element.648), channel_id=1, source_target_pairs={{0,4},{1,5},{2,6},{3,7},{8,12},{9,13},{10,14},{11,15},{16,20},{17,... | collective-permute-start | bytes 159752 | tf_op jit(solution)/shard_map/ppermute | solution.py:354
  100.9 6.2 %collective-permute-start.32 = (f32[104,128]{1,0:T(8,128)S(1)}, f32[104,128]{1,0:T(8,128)S(1)}, u32[]{:S(2)}, u32[]{:S(2)}) collective-permute-start(f32[104,128]{1,0:T(8,128)S(1)} %get-tuple-element.674), channel_id=1, source_target_pairs={{0,4},{1,5},{2,6},{3,7},{8,12},{9,13},{10,14},{11,15},{16,20},{17,... | collective-permute-start | bytes 159752 | tf_op jit(solution)/shard_map/ppermute | solution.py:354
  112.9 6.2 %collective-permute-start.36 = (f32[104,128]{1,0:T(8,128)S(1)}, f32[104,128]{1,0:T(8,128)S(1)}, u32[]{:S(2)}, u32[]{:S(2)}) collective-permute-start(f32[104,128]{1,0:T(8,128)S(1)} %get-tuple-element.700), channel_id=1, source_target_pairs={{0,4},{1,5},{2,6},{3,7},{8,12},{9,13},{10,14},{11,15},{16,20},{17,... | collective-permute-start | bytes 159752 | tf_op jit(solution)/shard_map/ppermute | solution.py:354
  124.8 4.5 %collective-permute-start.40 = (f32[104,128]{1,0:T(8,128)S(1)}, f32[104,128]{1,0:T(8,128)S(1)}, u32[]{:S(2)}, u32[]{:S(2)}) collective-permute-start(f32[104,128]{1,0:T(8,128)S(1)} %get-tuple-element.726), channel_id=1, source_target_pairs={{0,4},{1,5},{2,6},{3,7},{8,12},{9,13},{10,14},{11,15},{16,20},{17,... | collective-permute-start | bytes 159752 | tf_op jit(solution)/shard_map/ppermute | solution.py:354
  136.2 4.1 %collective-permute-start.44 = (f32[104,128]{1,0:T(8,128)S(1)}, f32[104,128]{1,0:T(8,128)S(1)}, u32[]{:S(2)}, u32[]{:S(2)}) collective-permute-start(f32[104,128]{1,0:T(8,128)S(1)} %get-tuple-element.752), channel_id=1, source_target_pairs={{0,4},{1,5},{2,6},{3,7},{8,12},{9,13},{10,14},{11,15},{16,20},{17,... | collective-permute-start | bytes 159752 | tf_op jit(solution)/shard_map/ppermute | solution.py:354
  146.4 3.4 %collective-permute-start.48 = (f32[104,128]{1,0:T(8,128)S(1)}, f32[104,128]{1,0:T(8,128)S(1)}, u32[]{:S(2)}, u32[]{:S(2)}) collective-permute-start(f32[104,128]{1,0:T(8,128)S(1)} %get-tuple-element.778), channel_id=1, source_target_pairs={{0,4},{1,5},{2,6},{3,7},{8,12},{9,13},{10,14},{11,15},{16,20},{17,... | collective-permute-start | bytes 159752 | tf_op jit(solution)/shard_map/ppermute | solution.py:354
  156.0 4.0 %collective-permute-start.52 = (f32[104,128]{1,0:T(8,128)S(1)}, f32[104,128]{1,0:T(8,128)S(1)}, u32[]{:S(2)}, u32[]{:S(2)}) collective-permute-start(f32[104,128]{1,0:T(8,128)S(1)} %get-tuple-element.804), channel_id=1, source_target_pairs={{0,4},{1,5},{2,6},{3,7},{8,12},{9,13},{10,14},{11,15},{16,20},{17,... | collective-permute-start | bytes 159752 | tf_op jit(solution)/shard_map/ppermute | solution.py:354
  166.7 6.7 %collective-permute-start.56 = (f32[104,128]{1,0:T(8,128)S(1)}, f32[104,128]{1,0:T(8,128)S(1)}, u32[]{:S(2)}, u32[]{:S(2)}) collective-permute-start(f32[104,128]{1,0:T(8,128)S(1)} %get-tuple-element.830), channel_id=1, source_target_pairs={{0,4},{1,5},{2,6},{3,7},{8,12},{9,13},{10,14},{11,15},{16,20},{17,... | collective-permute-start | bytes 159752 | tf_op jit(solution)/shard_map/ppermute | solution.py:354
  179.1 5.6 %collective-permute-start.58 = (f32[104,128]{1,0:T(8,128)S(1)}, f32[104,128]{1,0:T(8,128)S(1)}, u32[]{:S(2)}, u32[]{:S(2)}) collective-permute-start(f32[104,128]{1,0:T(8,128)S(1)} %get-tuple-element.851), channel_id=1, source_target_pairs={{0,4},{1,5},{2,6},{3,7},{8,12},{9,13},{10,14},{11,15},{16,20},{17,... | collective-permute-start | bytes 159752 | tf_op jit(solution)/shard_map/ppermute | solution.py:354
  190.2 5.8 %collective-permute-start.60 = (f32[104,128]{1,0:T(8,128)S(1)}, f32[104,128]{1,0:T(8,128)S(1)}, u32[]{:S(2)}, u32[]{:S(2)}) collective-permute-start(f32[104,128]{1,0:T(8,128)S(1)} %get-tuple-element.869), channel_id=1, source_target_pairs={{0,4},{1,5},{2,6},{3,7},{8,12},{9,13},{10,14},{11,15},{16,20},{17,... | collective-permute-start | bytes 159752 | tf_op jit(solution)/shard_map/ppermute | solution.py:354
  201.5 6.4 %collective-permute-start.62 = (f32[104,128]{1,0:T(8,128)S(1)}, f32[104,128]{1,0:T(8,128)S(1)}, u32[]{:S(2)}, u32[]{:S(2)}) collective-permute-start(f32[104,128]{1,0:T(8,128)S(1)} %get-tuple-element.887), channel_id=1, source_target_pairs={{0,4},{1,5},{2,6},{3,7},{8,12},{9,13},{10,14},{11,15},{16,20},{17,... | collective-permute-start | bytes 159752 | tf_op jit(solution)/shard_map/ppermute | solution.py:354
  (174 shorter events, 107.3 us)
Async XLA Ops:
  5.1 5.4 %collective-permute-start = (f32[104,128]{1,0:T(8,128)S(1)}, f32[104,128]{1,0:T(8,128)S(1)}, u32[]{:S(2)}, u32[]{:S(2)}) collective-permute-start(f32[104,128]{1,0:T(8,128)S(1)} %get-tuple-element.461), channel_id=1, source_target_pairs={{0,4},{1,5},{2,6},{3,7},{8,12},{9,13},{10,14},{11,15},{16,20},{17,... | collective-permute-start | bytes 159752 | tf_op jit(solution)/shard_map/ppermute | solution.py:354
  15.1 6.7 %collective-permute-start.2 = (f32[104,128]{1,0:T(8,128)S(1)}, f32[104,128]{1,0:T(8,128)S(1)}, u32[]{:S(2)}, u32[]{:S(2)}) collective-permute-start(f32[104,128]{1,0:T(8,128)S(1)} %get-tuple-element.476), channel_id=1, source_target_pairs={{0,4},{1,5},{2,6},{3,7},{8,12},{9,13},{10,14},{11,15},{16,20},{17,... | collective-permute-start | bytes 159752 | tf_op jit(solution)/shard_map/ppermute | solution.py:354
  25.7 6.0 %collective-permute-start.4 = (f32[104,128]{1,0:T(8,128)S(1)}, f32[104,128]{1,0:T(8,128)S(1)}, u32[]{:S(2)}, u32[]{:S(2)}) collective-permute-start(f32[104,128]{1,0:T(8,128)S(1)} %get-tuple-element.495), channel_id=1, source_target_pairs={{0,4},{1,5},{2,6},{3,7},{8,12},{9,13},{10,14},{11,15},{16,20},{17,... | collective-permute-start | bytes 159752 | tf_op jit(solution)/shard_map/ppermute | solution.py:354
  33.3 7.1 %collective-permute-start.8 = (f32[104,128]{1,0:T(8,128)S(1)}, f32[104,128]{1,0:T(8,128)S(1)}, u32[]{:S(2)}, u32[]{:S(2)}) collective-permute-start(f32[104,128]{1,0:T(8,128)S(1)} %get-tuple-element.521), channel_id=1, source_target_pairs={{0,1},{2,3},{4,5},{6,7},{8,9},{10,11},{12,13},{14,15},{16,17},{18,... | collective-permute-start | bytes 159752 | tf_op jit(solution)/shard_map/ppermute | solution.py:361
  34.6 7.3 %collective-permute-start.7 = (f32[104,128]{1,0:T(8,128)S(1)}, f32[104,128]{1,0:T(8,128)S(1)}, u32[]{:S(2)}, u32[]{:S(2)}) collective-permute-start(f32[104,128]{1,0:T(8,128)S(1)} %get-tuple-element.517), channel_id=1, source_target_pairs={{0,4},{1,5},{2,6},{3,7},{8,12},{9,13},{10,14},{11,15},{16,20},{17,... | collective-permute-start | bytes 159752 | tf_op jit(solution)/shard_map/ppermute | solution.py:354
  39.7 6.2 %collective-permute-start.11 = (f32[104,128]{1,0:T(8,128)S(1)}, f32[104,128]{1,0:T(8,128)S(1)}, u32[]{:S(2)}, u32[]{:S(2)}) collective-permute-start(f32[104,128]{1,0:T(8,128)S(1)} %get-tuple-element.535), channel_id=1, source_target_pairs={{1,2},{5,6},{9,10},{13,14},{17,18},{21,22},{25,26},{28,29},{30,31}... | collective-permute-start | bytes 159752 | tf_op jit(solution)/shard_map/ppermute | solution.py:361
  49.9 6.1 %collective-permute-start.15 = (f32[104,128]{1,0:T(8,128)S(1)}, f32[104,128]{1,0:T(8,128)S(1)}, u32[]{:S(2)}, u32[]{:S(2)}) collective-permute-start(f32[104,128]{1,0:T(8,128)S(1)} %get-tuple-element.561), channel_id=1, source_target_pairs={{1,2},{5,6},{9,10},{13,14},{17,18},{21,22},{25,26},{29,30},{2,1},{... | collective-permute-start | bytes 159752 | tf_op jit(solution)/shard_map/ppermute | solution.py:361
  59.4 6.7 %collective-permute-start.19 = (f32[104,128]{1,0:T(8,128)S(1)}, f32[104,128]{1,0:T(8,128)S(1)}, u32[]{:S(2)}, u32[]{:S(2)}) collective-permute-start(f32[104,128]{1,0:T(8,128)S(1)} %get-tuple-element.587), channel_id=1, source_target_pairs={{1,2},{5,6},{9,10},{13,14},{17,18},{21,22},{25,26},{29,30},{2,1},{... | collective-permute-start | bytes 159752 | tf_op jit(solution)/shard_map/ppermute | solution.py:361
  67.3 5.1 %collective-permute-start.20 = (f32[104,128]{1,0:T(8,128)S(1)}, f32[104,128]{1,0:T(8,128)S(1)}, u32[]{:S(2)}, u32[]{:S(2)}) collective-permute-start(f32[104,128]{1,0:T(8,128)S(1)} %get-tuple-element.596), channel_id=1, source_target_pairs={{0,4},{1,5},{2,6},{3,7},{8,12},{9,13},{10,14},{11,15},{16,20},{17,... | collective-permute-start | bytes 159752 | tf_op jit(solution)/shard_map/ppermute | solution.py:354
  69.9 5.0 %collective-permute-start.23 = (f32[104,128]{1,0:T(8,128)S(1)}, f32[104,128]{1,0:T(8,128)S(1)}, u32[]{:S(2)}, u32[]{:S(2)}) collective-permute-start(f32[104,128]{1,0:T(8,128)S(1)} %get-tuple-element.613), channel_id=1, source_target_pairs={{0,1},{2,3},{4,5},{6,7},{8,9},{10,11},{13,14},{17,18},{21,22},{25,... | collective-permute-start | bytes 159752 | tf_op jit(solution)/shard_map/ppermute | solution.py:361
  76.1 9.2 %collective-permute-start.24 = (f32[104,128]{1,0:T(8,128)S(1)}, f32[104,128]{1,0:T(8,128)S(1)}, u32[]{:S(2)}, u32[]{:S(2)}) collective-permute-start(f32[104,128]{1,0:T(8,128)S(1)} %get-tuple-element.622), channel_id=1, source_target_pairs={{0,4},{1,5},{2,6},{3,7},{8,12},{9,13},{10,14},{11,15},{16,20},{17,... | collective-permute-start | bytes 159752 | tf_op jit(solution)/shard_map/ppermute | solution.py:354
  88.6 9.0 %collective-permute-start.28 = (f32[104,128]{1,0:T(8,128)S(1)}, f32[104,128]{1,0:T(8,128)S(1)}, u32[]{:S(2)}, u32[]{:S(2)}) collective-permute-start(f32[104,128]{1,0:T(8,128)S(1)} %get-tuple-element.648), channel_id=1, source_target_pairs={{0,4},{1,5},{2,6},{3,7},{8,12},{9,13},{10,14},{11,15},{16,20},{17,... | collective-permute-start | bytes 159752 | tf_op jit(solution)/shard_map/ppermute | solution.py:354
  100.9 8.8 %collective-permute-start.32 = (f32[104,128]{1,0:T(8,128)S(1)}, f32[104,128]{1,0:T(8,128)S(1)}, u32[]{:S(2)}, u32[]{:S(2)}) collective-permute-start(f32[104,128]{1,0:T(8,128)S(1)} %get-tuple-element.674), channel_id=1, source_target_pairs={{0,4},{1,5},{2,6},{3,7},{8,12},{9,13},{10,14},{11,15},{16,20},{17,... | collective-permute-start | bytes 159752 | tf_op jit(solution)/shard_map/ppermute | solution.py:354
  112.9 8.8 %collective-permute-start.36 = (f32[104,128]{1,0:T(8,128)S(1)}, f32[104,128]{1,0:T(8,128)S(1)}, u32[]{:S(2)}, u32[]{:S(2)}) collective-permute-start(f32[104,128]{1,0:T(8,128)S(1)} %get-tuple-element.700), channel_id=1, source_target_pairs={{0,4},{1,5},{2,6},{3,7},{8,12},{9,13},{10,14},{11,15},{16,20},{17,... | collective-permute-start | bytes 159752 | tf_op jit(solution)/shard_map/ppermute | solution.py:354
  124.8 6.6 %collective-permute-start.40 = (f32[104,128]{1,0:T(8,128)S(1)}, f32[104,128]{1,0:T(8,128)S(1)}, u32[]{:S(2)}, u32[]{:S(2)}) collective-permute-start(f32[104,128]{1,0:T(8,128)S(1)} %get-tuple-element.726), channel_id=1, source_target_pairs={{0,4},{1,5},{2,6},{3,7},{8,12},{9,13},{10,14},{11,15},{16,20},{17,... | collective-permute-start | bytes 159752 | tf_op jit(solution)/shard_map/ppermute | solution.py:354
  129.3 5.7 %collective-permute-start.43 = (f32[104,128]{1,0:T(8,128)S(1)}, f32[104,128]{1,0:T(8,128)S(1)}, u32[]{:S(2)}, u32[]{:S(2)}) collective-permute-start(f32[104,128]{1,0:T(8,128)S(1)} %get-tuple-element.743), channel_id=1, source_target_pairs={{1,2},{5,6},{9,10},{13,14},{17,18},{21,22},{25,26},{28,29},{30,31}... | collective-permute-start | bytes 159752 | tf_op jit(solution)/shard_map/ppermute | solution.py:361
  136.2 6.5 %collective-permute-start.44 = (f32[104,128]{1,0:T(8,128)S(1)}, f32[104,128]{1,0:T(8,128)S(1)}, u32[]{:S(2)}, u32[]{:S(2)}) collective-permute-start(f32[104,128]{1,0:T(8,128)S(1)} %get-tuple-element.752), channel_id=1, source_target_pairs={{0,4},{1,5},{2,6},{3,7},{8,12},{9,13},{10,14},{11,15},{16,20},{17,... | collective-permute-start | bytes 159752 | tf_op jit(solution)/shard_map/ppermute | solution.py:354
  146.4 5.8 %collective-permute-start.48 = (f32[104,128]{1,0:T(8,128)S(1)}, f32[104,128]{1,0:T(8,128)S(1)}, u32[]{:S(2)}, u32[]{:S(2)}) collective-permute-start(f32[104,128]{1,0:T(8,128)S(1)} %get-tuple-element.778), channel_id=1, source_target_pairs={{0,4},{1,5},{2,6},{3,7},{8,12},{9,13},{10,14},{11,15},{16,20},{17,... | collective-permute-start | bytes 159752 | tf_op jit(solution)/shard_map/ppermute | solution.py:354
  156.0 6.4 %collective-permute-start.52 = (f32[104,128]{1,0:T(8,128)S(1)}, f32[104,128]{1,0:T(8,128)S(1)}, u32[]{:S(2)}, u32[]{:S(2)}) collective-permute-start(f32[104,128]{1,0:T(8,128)S(1)} %get-tuple-element.804), channel_id=1, source_target_pairs={{0,4},{1,5},{2,6},{3,7},{8,12},{9,13},{10,14},{11,15},{16,20},{17,... | collective-permute-start | bytes 159752 | tf_op jit(solution)/shard_map/ppermute | solution.py:354
  159.9 5.0 %collective-permute-start.55 = (f32[104,128]{1,0:T(8,128)S(1)}, f32[104,128]{1,0:T(8,128)S(1)}, u32[]{:S(2)}, u32[]{:S(2)}) collective-permute-start(f32[104,128]{1,0:T(8,128)S(1)} %get-tuple-element.821), channel_id=1, source_target_pairs={{0,1},{2,3},{5,6},{9,10},{12,13},{14,15},{16,17},{18,19},{21,22},{... | collective-permute-start | bytes 159752 | tf_op jit(solution)/shard_map/ppermute | solution.py:361
  166.7 9.0 %collective-permute-start.56 = (f32[104,128]{1,0:T(8,128)S(1)}, f32[104,128]{1,0:T(8,128)S(1)}, u32[]{:S(2)}, u32[]{:S(2)}) collective-permute-start(f32[104,128]{1,0:T(8,128)S(1)} %get-tuple-element.830), channel_id=1, source_target_pairs={{0,4},{1,5},{2,6},{3,7},{8,12},{9,13},{10,14},{11,15},{16,20},{17,... | collective-permute-start | bytes 159752 | tf_op jit(solution)/shard_map/ppermute | solution.py:354
  179.1 7.7 %collective-permute-start.58 = (f32[104,128]{1,0:T(8,128)S(1)}, f32[104,128]{1,0:T(8,128)S(1)}, u32[]{:S(2)}, u32[]{:S(2)}) collective-permute-start(f32[104,128]{1,0:T(8,128)S(1)} %get-tuple-element.851), channel_id=1, source_target_pairs={{0,4},{1,5},{2,6},{3,7},{8,12},{9,13},{10,14},{11,15},{16,20},{17,... | collective-permute-start | bytes 159752 | tf_op jit(solution)/shard_map/ppermute | solution.py:354
  190.2 7.9 %collective-permute-start.60 = (f32[104,128]{1,0:T(8,128)S(1)}, f32[104,128]{1,0:T(8,128)S(1)}, u32[]{:S(2)}, u32[]{:S(2)}) collective-permute-start(f32[104,128]{1,0:T(8,128)S(1)} %get-tuple-element.869), channel_id=1, source_target_pairs={{0,4},{1,5},{2,6},{3,7},{8,12},{9,13},{10,14},{11,15},{16,20},{17,... | collective-permute-start | bytes 159752 | tf_op jit(solution)/shard_map/ppermute | solution.py:354
  201.5 8.5 %collective-permute-start.62 = (f32[104,128]{1,0:T(8,128)S(1)}, f32[104,128]{1,0:T(8,128)S(1)}, u32[]{:S(2)}, u32[]{:S(2)}) collective-permute-start(f32[104,128]{1,0:T(8,128)S(1)} %get-tuple-element.887), channel_id=1, source_target_pairs={{0,4},{1,5},{2,6},{3,7},{8,12},{9,13},{10,14},{11,15},{16,20},{17,... | collective-permute-start | bytes 159752 | tf_op jit(solution)/shard_map/ppermute | solution.py:354
  (39 other events, 113.2 us)

commit v6 on v5

--- a/solution.py
+++ b/solution.py
@@ -32,31 +32,41 @@
 
 def lateral_plan(count, vectors):
     ticks = 4 * count + 2 * (vectors - 1)
-    sent = [[-1] * count for _ in range(ticks)]
+    sent = [[None] * count for _ in range(ticks)]
     urgent = [[False] * count for _ in range(ticks)]
     for slab in range(count):
-        waiting = []
+        left = ([], [])
         for half in range(3):
             rank = count - 1 - slab if half & 1 else slab
             for vector in range(vectors):
                 made = 2 * vector + half * count + rank
                 used = 2 * vector + (half + 1) * count + count - 1 - rank
                 if used == made + 1:
-                    sent[made][slab] = vector
+                    sent[made][slab] = (1, (vector,))
                     urgent[made][slab] = True
+                    continue
+                left[1].append((used, made, vector))
+                if used == made + 3:
+                    sent[made + 1][slab] = (0, (vector,))
                 else:
-                    waiting.append((used, made, vector))
-        for parity in range(2):
-            left = sorted(waiting)
-            for tick in range(LATERAL_START + parity, ticks, 2):
-                ready = [one for one in left if one[1] <= tick]
-                if sent[tick][slab] >= 0 or not ready:
-                    continue
-                assert tick <= ready[0][0] - 2
-                sent[tick][slab] = ready[0][2]
-                left.remove(ready[0])
-            assert not left
+                    left[0].append((used, made, vector))
+        for tick in range(LATERAL_START, ticks, 2):
+            ready = [sorted(one for one in waiting if one[1] <= tick)[:2] for waiting in left]
+            if not any(ready):
+                continue
+            pairs = 0 if ready[0] and (not ready[1] or ready[0][0][0] <= ready[1][0][0]) else 1
+            assert tick <= ready[pairs][0][0] - 2
+            sent[tick][slab] = (pairs, tuple(one[2] for one in ready[pairs]))
+            for one in ready[pairs]:
+                left[pairs].remove(one)
+        assert not any(left)
     return sent, urgent
+
+
+def numbers(plan, entry):
+    if entry < 0:
+        return [-1 if one is None else one[0] for one in plan]
+    return [-1 if one is None or len(one[1]) <= entry else one[1][entry] for one in plan]
 
 
 def pick(values, place):
@@ -83,19 +93,19 @@
     return jnp.take_along_axis(value, index, axis=1, mode="promise_in_bounds")
 
 
-def take_lateral(base, vector, left, right, left_cols, right_cols, arrived, spare, parity):
+def take_lateral(base, vector, left, right, left_cols, right_cols, arrived, spare, pairs):
     rows = spare.shape[0]
     part = lax.axis_index("span")
-    on_right = (part & 1) == parity
+    on_right = (part & 1) == pairs
 
     @pl.when(on_right & (part < lax.axis_size("span") - 1))
     def _():
-        spare[...] = gathered(arrived[...], right_cols[...])
+        spare[...] = gathered(arrived, right_cols[...])
         base[vector] = base[vector] - product(right, spare, rows)
 
     @pl.when((on_right ^ True) & (part > 0))
     def _():
-        spare[...] = gathered(arrived[...], left_cols[...])
+        spare[...] = gathered(arrived, left_cols[...])
         base[vector] = base[vector] - product(left, spare, rows)
 
 
@@ -156,7 +166,7 @@
     tick, tasks, sent, columns_and_inputs, kept, values, spare
 ):
     up_cols, down_cols, left_cols, right_cols, source, incoming, arrived = columns_and_inputs
-    value, cross = values
+    value, *cross = values
     diag, up, down, left, right, base, latest, out = kept
     rows = spare.shape[0]
     vectors, size, _ = out.shape
@@ -168,8 +178,8 @@
 
         @pl.when(turns(task))
         def _():
-            take_lateral(base, vector, left, right, left_cols, right_cols, incoming, spare, 0)
-            take_lateral(base, vector, left, right, left_cols, right_cols, arrived, spare, 1)
+            take_lateral(base, vector, left, right, left_cols, right_cols, incoming[...], spare, 0)
+            take_lateral(base, vector, left, right, left_cols, right_cols, arrived[0], spare, 1)
 
     @pl.when(active)
     def _():
@@ -206,22 +216,39 @@
             def _():
                 out[vector] = fresh[:size]
 
-    if any(one >= 0 for one in sent):
-        chosen = pick(sent, place)
-
-        @pl.when(chosen >= 0)
-        def _():
-            cross[...] = latest[chosen]
-
-
-def side_kernel(parity, sent, columns_and_inputs, kept, values, spare):
-    left_cols, right_cols, arrived = columns_and_inputs
-    left, right, base = kept
-    vector = pick(sent, lax.axis_index("sweep"))
-
-    @pl.when(vector >= 0)
-    def _():
-        take_lateral(base, vector, left, right, left_cols, right_cols, arrived, spare, parity)
+    if cross:
+        fill(cross[0], latest, sent, place)
+
+
+def fill(cross, latest, plan, place):
+    for entry in range(cross.shape[0]):
+        chosen = numbers(plan, entry)
+        if any(one >= 0 for one in chosen):
+            vector = pick(chosen, place)
+
+            @pl.when(vector >= 0)
+            def _():
+                cross[entry] = latest[vector]
+
+
+def side_kernel(came, plan, columns_and_inputs, kept, values, spare):
+    left_cols, right_cols, *arrived = columns_and_inputs
+    left, right, base, latest = kept
+    place = lax.axis_index("sweep")
+    if values:
+        fill(values[0], latest, plan, place)
+    if arrived:
+        pairs = pick(numbers(came, -1), place)
+        for entry in range(arrived[0].shape[0]):
+            chosen = numbers(came, entry)
+            if any(one >= 0 for one in chosen):
+                vector = pick(chosen, place)
+
+                @pl.when(vector >= 0)
+                def _():
+                    take_lateral(
+                        base, vector, left, right, left_cols, right_cols, arrived[0][entry], spare, pairs
+                    )
 
 
 def in_vmem(count):
@@ -330,45 +357,49 @@
 
     for tick in range(ticks):
         tasks = tasks_at(tick)
+        plan = sent[tick]
         used = 1 + sum(mat is not blank for mat in mats[1:])
         turning = any(turns(one) for one in tasks)
-        *kept, value, cross = call(
+        at_once = any(plan) and tick & 1 == 1
+        results = call(
             lambda fixed, kept, fresh, spare, used=used, tick=tick, tasks=tasks: task_kernel(
                 tick, tasks, sent[tick], fixed, [*kept[:used], *[None] * (5 - used), *kept[used:]], fresh, spare
             ),
             "task",
             (*columns, source, incoming, arrived if turning else blank),
             (*mats[:used], base, latest, out),
-            ((rows, lanes), (rows, lanes)),
+            ((rows, lanes), *([(1, rows, lanes)] if at_once else [])),
             (rows, lanes),
         )
-        mats[:used] = kept[:used]
-        base, latest, out = kept[used:]
-
-        previous = arrived
+        mats[:used] = results[:used]
+        base, latest, out, value, *cross = results[used:]
+
         if any(urgent[tick]) or any(one[0] and one[2] > 0 for one in tasks_at(tick + 1)):
             swap = [(s, s + 1) for s in range(tick & 1, count - 1, 2)]
             alone = [s for s in range(count) if all(s not in two for two in swap)]
             pairs = [(device(a, p), device(b, p)) for a, b in swap for p in range(parts)]
             pairs += [(device(s, a), device(s, b)) for s in alone for a, b in even_pairs]
             incoming = lax.ppermute(value, ("sweep", "span"), closed(pairs, range(count * parts)))
-        if any(one >= 0 for one in sent[tick]):
+        came = [None if not tick or urgent[tick - 1][s] else sent[tick - 1][s] for s in range(count)]
+        later = any(plan) and not at_once
+        if any(came) or later:
+            mats[3], mats[4], base, latest, *made = call(
+                functools.partial(side_kernel, came, plan),
+                "side",
+                (columns[2], columns[3], *([arrived] if any(came) else [])),
+                (mats[3], mats[4], base, latest),
+                ((2, rows, lanes),) if later else (),
+                (rows, lanes),
+            )
+            cross += made
+        if any(plan):
             pairs = [
                 (device(s, a), device(s, b))
                 for s in range(count)
-                for a, b in (odd_pairs if sent[tick][s] >= 0 and (urgent[tick][s] or not tick & 1) else even_pairs)
+                if plan[s] is not None
+                for a, b in (odd_pairs if plan[s][0] else even_pairs)
             ]
-            arrived = lax.ppermute(cross, ("sweep", "span"), closed(pairs, range(count * parts)))
-        came = [-1 if not tick or urgent[tick - 1][s] else sent[tick - 1][s] for s in range(count)]
-        if any(one >= 0 for one in came):
-            mats[3], mats[4], base = call(
-                functools.partial(side_kernel, tick & 1, came),
-                "side",
-                (columns[2], columns[3], previous),
-                (mats[3], mats[4], base),
-                (),
-                (rows, lanes),
-            )
+            arrived = lax.ppermute(cross[0], ("sweep", "span"), closed(pairs, range(count * parts)))
         if tick < len(late_blocks):
             mats[1 + tick], base = later_call(*late_blocks[tick], base)
     return out[None, None]

time: 213 us -> 200 us (0.939)
  Pallas kernels: 39.2 us -> 32 us
  waiting for transfers between devices: 34.9 us -> 27.7 us
    ppermute x26, starting transfers between devices: 33 us -> 23.8 us  [per_device(): lax.ppermute(cross[0], ('sweep', 'span'), closed(pairs, range(count * par...]
    ppermute x37, starting transfers between devices: 103 us -> 112 us  [per_device(): lax.ppermute(value, ('sweep', 'span'), closed(pairs, range(count * parts)))]
    ppermute x26, waiting for transfers between devices: 9.04 us -> 0.73 us  [per_device(): lax.ppermute(cross[0], ('sweep', 'span'), closed(pairs, range(count * par...]
    pallas_call x64 -> x66, Pallas kernels: 24.7 us -> 17.5 us  [call(): pl.pallas_call(body, out_shape=tuple((held(shape) for shape in [*(a.shape...]
  transfers between devices with their start and end apart: 63 -> 63, of which waited for: 29 -> 29; matrix products, arithmetic and copies ran while one was open for 0% -> 0% of each run, Pallas kernels for 9% -> 10%
where the time goes in v6:
time: 200 us; the launch traced here: 198 us
  starting transfers between devices  135 us (68%)
  Pallas kernels  32 us (16%)
  waiting for transfers between devices  27.7 us (14%)
    ppermute x37, starting transfers between devices, per_device(): lax.ppermute(value, ('sweep', 'span'), closed(pairs, range(count * parts)))  112 us
    ppermute x37, waiting for transfers between devices, per_device(): lax.ppermute(value, ('sweep', 'span'), closed(pairs, range(count * parts)))  27 us
    ppermute x26, starting transfers between devices, per_device(): lax.ppermute(cross[0], ('sweep', 'span'), closed(pairs, range(count * par...  23.8 us
    pallas_call x66, Pallas kernels, call(): pl.pallas_call(body, out_shape=tuple((held(shape) for shape in [*(a.shape...  17.5 us
    pallas_call x4, Pallas kernels, later_call(): pl.pallas_call(functools.partial(later_kernel, face), out_shape=(held((si...  11.5 us
  transfers between devices with their start and end apart: 63, of which 29 were waited for; matrix products, arithmetic and copies ran while one was open for 0% of the time, Pallas kernels for 10%

profile of v6, /device:TPU:0, one launch (start us, length us, event | category | flops | bytes accessed | tf_op | source)
XLA Modules:
  0.0 197.7 jit_solution(4795001422599838747)
XLA Ops:
  0.9 3.0 %first.1 = (f32[100,104,128]{2,1,0:T(8,128)S(1)}, f32[4,104,128]{2,1,0:T(8,128)S(1)}, f32[4,104,128]{2,1,0:T(8,128)S(1)}, f32[104,128]{1,0:T(8,128)S(1)}, s32[1,...) custom-call(bf16[100,100,128]{2,1,0:T(8,128)(2,1)} %bitcast.11, ...), custom_call_target="tpu_custom_call" | custom-call | tf_op jit(solution)/shard_map/first/pallas_call | solution.py:295
  4.4 2.6 %collective-permute-start = (f32[104,128]{1,0:T(8,128)S(1)}, f32[104,128]{1,0:T(8,128)S(1)}, u32[]{:S(2)}, u32[]{:S(2)}) collective-permute-start(f32[104,128]{1,0:T(8,128)S(1)} %get-tuple-element.495), channel_id=1, source_target_pairs={{0,4},{1,5},{2,6},{3,7},{8,12},{9,13},{10,14},{11,15},{16,20},{17,... | collective-permute-start | bytes 159752 | tf_op jit(solution)/shard_map/ppermute | solution.py:382
  7.0 2.9 %later.4 = (f32[100,104,128]{2,1,0:T(8,128)S(1)}, f32[4,104,128]{2,1,0:T(8,128)S(1)}) custom-call(bf16[1,1,100,100,128]{4,3,2,1,0:T(8,128)(2,1)} %block.4, f32[4,104,128]{2,1,0:T(8,128)S(1)} %get-tuple-element.497.base_in), custom_call_target="tpu_custom_call", output_to_operand_aliasing={{1}: (1, {})} | custom-call | tf_op jit(solution)/shard_map/later/pallas_call | solution.py:312
  10.0 2.9 %later.5 = (f32[100,104,128]{2,1,0:T(8,128)S(1)}, f32[4,104,128]{2,1,0:T(8,128)S(1)}) custom-call(bf16[1,1,3,100,100,128]{5,4,3,2,1,0:T(8,128)(2,1)} %block.7, f32[4,104,128]{2,1,0:T(8,128)S(1)} %get-tuple-element.505.base_in), custom_call_target="tpu_custom_call", output_to_operand_aliasing={{1}: (1, {})} | custom-call | tf_op jit(solution)/shard_map/later/pallas_call | solution.py:312
  13.4 3.8 %collective-permute-start.2 = (f32[104,128]{1,0:T(8,128)S(1)}, f32[104,128]{1,0:T(8,128)S(1)}, u32[]{:S(2)}, u32[]{:S(2)}) collective-permute-start(f32[104,128]{1,0:T(8,128)S(1)} %get-tuple-element.510), channel_id=1, source_target_pairs={{0,4},{1,5},{2,6},{3,7},{8,12},{9,13},{10,14},{11,15},{16,20},{17,... | collective-permute-start | bytes 159752 | tf_op jit(solution)/shard_map/ppermute | solution.py:382
  17.2 2.9 %later.6 = (f32[100,104,128]{2,1,0:T(8,128)S(1)}, f32[4,104,128]{2,1,0:T(8,128)S(1)}) custom-call(bf16[1,1,3,100,100,128]{5,4,3,2,1,0:T(8,128)(2,1)} %block.7, f32[4,104,128]{2,1,0:T(8,128)S(1)} %get-tuple-element.514.base_in), custom_call_target="tpu_custom_call", output_to_operand_aliasing={{1}: (1, {})} | custom-call | tf_op jit(solution)/shard_map/later/pallas_call | solution.py:312
  20.2 2.9 %later.7 = (f32[100,104,128]{2,1,0:T(8,128)S(1)}, f32[4,104,128]{2,1,0:T(8,128)S(1)}) custom-call(bf16[1,1,3,100,100,128]{5,4,3,2,1,0:T(8,128)(2,1)} %block.7, f32[4,104,128]{2,1,0:T(8,128)S(1)} %get-tuple-element.524.base_in), custom_call_target="tpu_custom_call", output_to_operand_aliasing={{1}: (1, {})} | custom-call | tf_op jit(solution)/shard_map/later/pallas_call | solution.py:312
  23.5 3.8 %collective-permute-start.4 = (f32[104,128]{1,0:T(8,128)S(1)}, f32[104,128]{1,0:T(8,128)S(1)}, u32[]{:S(2)}, u32[]{:S(2)}) collective-permute-start(f32[104,128]{1,0:T(8,128)S(1)} %get-tuple-element.529), channel_id=1, source_target_pairs={{0,4},{1,5},{2,6},{3,7},{8,12},{9,13},{10,14},{11,15},{16,20},{17,... | collective-permute-start | bytes 159752 | tf_op jit(solution)/shard_map/ppermute | solution.py:382
  31.9 5.5 %collective-permute-start.7 = (f32[104,128]{1,0:T(8,128)S(1)}, f32[104,128]{1,0:T(8,128)S(1)}, u32[]{:S(2)}, u32[]{:S(2)}) collective-permute-start(f32[104,128]{1,0:T(8,128)S(1)} %get-tuple-element.556), channel_id=1, source_target_pairs={{0,4},{1,5},{2,6},{3,7},{8,12},{9,13},{10,14},{11,15},{16,20},{17,... | collective-permute-start | bytes 159752 | tf_op jit(solution)/shard_map/ppermute | solution.py:382
  42.0 5.6 %collective-permute-start.11 = (f32[104,128]{1,0:T(8,128)S(1)}, f32[104,128]{1,0:T(8,128)S(1)}, u32[]{:S(2)}, u32[]{:S(2)}) collective-permute-start(f32[104,128]{1,0:T(8,128)S(1)} %get-tuple-element.584), channel_id=1, source_target_pairs={{0,4},{1,5},{2,6},{3,7},{8,12},{9,13},{10,14},{11,15},{16,20},{17,... | collective-permute-start | bytes 159752 | tf_op jit(solution)/shard_map/ppermute | solution.py:382
  51.9 4.9 %collective-permute-start.15 = (f32[104,128]{1,0:T(8,128)S(1)}, f32[104,128]{1,0:T(8,128)S(1)}, u32[]{:S(2)}, u32[]{:S(2)}) collective-permute-start(f32[104,128]{1,0:T(8,128)S(1)} %get-tuple-element.612), channel_id=1, source_target_pairs={{0,4},{1,5},{2,6},{3,7},{8,12},{9,13},{10,14},{11,15},{16,20},{17,... | collective-permute-start | bytes 159752 | tf_op jit(solution)/shard_map/ppermute | solution.py:382
  61.3 4.7 %collective-permute-start.19 = (f32[104,128]{1,0:T(8,128)S(1)}, f32[104,128]{1,0:T(8,128)S(1)}, u32[]{:S(2)}, u32[]{:S(2)}) collective-permute-start(f32[104,128]{1,0:T(8,128)S(1)} %get-tuple-element.640), channel_id=1, source_target_pairs={{0,4},{1,5},{2,6},{3,7},{8,12},{9,13},{10,14},{11,15},{16,20},{17,... | collective-permute-start | bytes 159752 | tf_op jit(solution)/shard_map/ppermute | solution.py:382
  69.4 7.5 %collective-permute-start.23 = (f32[104,128]{1,0:T(8,128)S(1)}, f32[104,128]{1,0:T(8,128)S(1)}, u32[]{:S(2)}, u32[]{:S(2)}) collective-permute-start(f32[104,128]{1,0:T(8,128)S(1)} %get-tuple-element.668), channel_id=1, source_target_pairs={{0,4},{1,5},{2,6},{3,7},{8,12},{9,13},{10,14},{11,15},{16,20},{17,... | collective-permute-start | bytes 159752 | tf_op jit(solution)/shard_map/ppermute | solution.py:382
  82.1 6.0 %collective-permute-start.27 = (f32[104,128]{1,0:T(8,128)S(1)}, f32[104,128]{1,0:T(8,128)S(1)}, u32[]{:S(2)}, u32[]{:S(2)}) collective-permute-start(f32[104,128]{1,0:T(8,128)S(1)} %get-tuple-element.696), channel_id=1, source_target_pairs={{0,4},{1,5},{2,6},{3,7},{8,12},{9,13},{10,14},{11,15},{16,20},{17,... | collective-permute-start | bytes 159752 | tf_op jit(solution)/shard_map/ppermute | solution.py:382
  93.7 7.2 %collective-permute-start.31 = (f32[104,128]{1,0:T(8,128)S(1)}, f32[104,128]{1,0:T(8,128)S(1)}, u32[]{:S(2)}, u32[]{:S(2)}) collective-permute-start(f32[104,128]{1,0:T(8,128)S(1)} %get-tuple-element.724), channel_id=1, source_target_pairs={{0,4},{1,5},{2,6},{3,7},{8,12},{9,13},{10,14},{11,15},{16,20},{17,... | collective-permute-start | bytes 159752 | tf_op jit(solution)/shard_map/ppermute | solution.py:382
  106.5 5.5 %collective-permute-start.35 = (f32[104,128]{1,0:T(8,128)S(1)}, f32[104,128]{1,0:T(8,128)S(1)}, u32[]{:S(2)}, u32[]{:S(2)}) collective-permute-start(f32[104,128]{1,0:T(8,128)S(1)} %get-tuple-element.752), channel_id=1, source_target_pairs={{0,4},{1,5},{2,6},{3,7},{8,12},{9,13},{10,14},{11,15},{16,20},{17,... | collective-permute-start | bytes 159752 | tf_op jit(solution)/shard_map/ppermute | solution.py:382
  118.2 4.5 %collective-permute-start.39 = (f32[104,128]{1,0:T(8,128)S(1)}, f32[104,128]{1,0:T(8,128)S(1)}, u32[]{:S(2)}, u32[]{:S(2)}) collective-permute-start(f32[104,128]{1,0:T(8,128)S(1)} %get-tuple-element.780), channel_id=1, source_target_pairs={{0,4},{1,5},{2,6},{3,7},{8,12},{9,13},{10,14},{11,15},{16,20},{17,... | collective-permute-start | bytes 159752 | tf_op jit(solution)/shard_map/ppermute | solution.py:382
  127.6 5.5 %collective-permute-start.43 = (f32[104,128]{1,0:T(8,128)S(1)}, f32[104,128]{1,0:T(8,128)S(1)}, u32[]{:S(2)}, u32[]{:S(2)}) collective-permute-start(f32[104,128]{1,0:T(8,128)S(1)} %get-tuple-element.808), channel_id=1, source_target_pairs={{0,4},{1,5},{2,6},{3,7},{8,12},{9,13},{10,14},{11,15},{16,20},{17,... | collective-permute-start | bytes 159752 | tf_op jit(solution)/shard_map/ppermute | solution.py:382
  136.8 5.4 %collective-permute-start.47 = (f32[104,128]{1,0:T(8,128)S(1)}, f32[104,128]{1,0:T(8,128)S(1)}, u32[]{:S(2)}, u32[]{:S(2)}) collective-permute-start(f32[104,128]{1,0:T(8,128)S(1)} %get-tuple-element.836), channel_id=1, source_target_pairs={{0,4},{1,5},{2,6},{3,7},{8,12},{9,13},{10,14},{11,15},{16,20},{17,... | collective-permute-start | bytes 159752 | tf_op jit(solution)/shard_map/ppermute | solution.py:382
  145.6 5.8 %collective-permute-start.51 = (f32[104,128]{1,0:T(8,128)S(1)}, f32[104,128]{1,0:T(8,128)S(1)}, u32[]{:S(2)}, u32[]{:S(2)}) collective-permute-start(f32[104,128]{1,0:T(8,128)S(1)} %get-tuple-element.864), channel_id=1, source_target_pairs={{0,4},{1,5},{2,6},{3,7},{8,12},{9,13},{10,14},{11,15},{16,20},{17,... | collective-permute-start | bytes 159752 | tf_op jit(solution)/shard_map/ppermute | solution.py:382
  154.8 7.1 %collective-permute-start.55 = (f32[104,128]{1,0:T(8,128)S(1)}, f32[104,128]{1,0:T(8,128)S(1)}, u32[]{:S(2)}, u32[]{:S(2)}) collective-permute-start(f32[104,128]{1,0:T(8,128)S(1)} %get-tuple-element.892), channel_id=1, source_target_pairs={{0,4},{1,5},{2,6},{3,7},{8,12},{9,13},{10,14},{11,15},{16,20},{17,... | collective-permute-start | bytes 159752 | tf_op jit(solution)/shard_map/ppermute | solution.py:382
  166.5 6.0 %collective-permute-start.58 = (f32[104,128]{1,0:T(8,128)S(1)}, f32[104,128]{1,0:T(8,128)S(1)}, u32[]{:S(2)}, u32[]{:S(2)}) collective-permute-start(f32[104,128]{1,0:T(8,128)S(1)} %get-tuple-element.919), channel_id=1, source_target_pairs={{0,4},{1,5},{2,6},{3,7},{8,12},{9,13},{10,14},{11,15},{16,20},{17,... | collective-permute-start | bytes 159752 | tf_op jit(solution)/shard_map/ppermute | solution.py:382
  176.8 5.9 %collective-permute-start.60 = (f32[104,128]{1,0:T(8,128)S(1)}, f32[104,128]{1,0:T(8,128)S(1)}, u32[]{:S(2)}, u32[]{:S(2)}) collective-permute-start(f32[104,128]{1,0:T(8,128)S(1)} %get-tuple-element.937), channel_id=1, source_target_pairs={{0,4},{1,5},{2,6},{3,7},{8,12},{9,13},{10,14},{11,15},{16,20},{17,... | collective-permute-start | bytes 159752 | tf_op jit(solution)/shard_map/ppermute | solution.py:382
  187.0 6.3 %collective-permute-start.62 = (f32[104,128]{1,0:T(8,128)S(1)}, f32[104,128]{1,0:T(8,128)S(1)}, u32[]{:S(2)}, u32[]{:S(2)}) collective-permute-start(f32[104,128]{1,0:T(8,128)S(1)} %get-tuple-element.955), channel_id=1, source_target_pairs={{0,4},{1,5},{2,6},{3,7},{8,12},{9,13},{10,14},{11,15},{16,20},{17,... | collective-permute-start | bytes 159752 | tf_op jit(solution)/shard_map/ppermute | solution.py:382
  (176 shorter events, 78.7 us)
Async XLA Ops:
  4.4 5.5 %collective-permute-start = (f32[104,128]{1,0:T(8,128)S(1)}, f32[104,128]{1,0:T(8,128)S(1)}, u32[]{:S(2)}, u32[]{:S(2)}) collective-permute-start(f32[104,128]{1,0:T(8,128)S(1)} %get-tuple-element.495), channel_id=1, source_target_pairs={{0,4},{1,5},{2,6},{3,7},{8,12},{9,13},{10,14},{11,15},{16,20},{17,... | collective-permute-start | bytes 159752 | tf_op jit(solution)/shard_map/ppermute | solution.py:382
  13.4 6.7 %collective-permute-start.2 = (f32[104,128]{1,0:T(8,128)S(1)}, f32[104,128]{1,0:T(8,128)S(1)}, u32[]{:S(2)}, u32[]{:S(2)}) collective-permute-start(f32[104,128]{1,0:T(8,128)S(1)} %get-tuple-element.510), channel_id=1, source_target_pairs={{0,4},{1,5},{2,6},{3,7},{8,12},{9,13},{10,14},{11,15},{16,20},{17,... | collective-permute-start | bytes 159752 | tf_op jit(solution)/shard_map/ppermute | solution.py:382
  23.5 6.0 %collective-permute-start.4 = (f32[104,128]{1,0:T(8,128)S(1)}, f32[104,128]{1,0:T(8,128)S(1)}, u32[]{:S(2)}, u32[]{:S(2)}) collective-permute-start(f32[104,128]{1,0:T(8,128)S(1)} %get-tuple-element.529), channel_id=1, source_target_pairs={{0,4},{1,5},{2,6},{3,7},{8,12},{9,13},{10,14},{11,15},{16,20},{17,... | collective-permute-start | bytes 159752 | tf_op jit(solution)/shard_map/ppermute | solution.py:382
  31.9 7.6 %collective-permute-start.7 = (f32[104,128]{1,0:T(8,128)S(1)}, f32[104,128]{1,0:T(8,128)S(1)}, u32[]{:S(2)}, u32[]{:S(2)}) collective-permute-start(f32[104,128]{1,0:T(8,128)S(1)} %get-tuple-element.556), channel_id=1, source_target_pairs={{0,4},{1,5},{2,6},{3,7},{8,12},{9,13},{10,14},{11,15},{16,20},{17,... | collective-permute-start | bytes 159752 | tf_op jit(solution)/shard_map/ppermute | solution.py:382
  37.5 4.3 %collective-permute-start.10 = (f32[2,104,128]{2,1,0:T(8,128)S(1)}, f32[2,104,128]{2,1,0:T(8,128)S(1)}, u32[]{:S(2)}, u32[]{:S(2)}) collective-permute-start(f32[2,104,128]{2,1,0:T(8,128)S(1)} %get-tuple-element.574), channel_id=1, source_target_pairs={{1,2},{5,6},{9,10},{13,14},{17,18},{20,21},{22,23},{25,26},{2,1},{... | collective-permute-start | bytes 319496 | tf_op jit(solution)/shard_map/ppermute | solution.py:402
  42.0 7.7 %collective-permute-start.11 = (f32[104,128]{1,0:T(8,128)S(1)}, f32[104,128]{1,0:T(8,128)S(1)}, u32[]{:S(2)}, u32[]{:S(2)}) collective-permute-start(f32[104,128]{1,0:T(8,128)S(1)} %get-tuple-element.584), channel_id=1, source_target_pairs={{0,4},{1,5},{2,6},{3,7},{8,12},{9,13},{10,14},{11,15},{16,20},{17,... | collective-permute-start | bytes 159752 | tf_op jit(solution)/shard_map/ppermute | solution.py:382
  51.9 7.0 %collective-permute-start.15 = (f32[104,128]{1,0:T(8,128)S(1)}, f32[104,128]{1,0:T(8,128)S(1)}, u32[]{:S(2)}, u32[]{:S(2)}) collective-permute-start(f32[104,128]{1,0:T(8,128)S(1)} %get-tuple-element.612), channel_id=1, source_target_pairs={{0,4},{1,5},{2,6},{3,7},{8,12},{9,13},{10,14},{11,15},{16,20},{17,... | collective-permute-start | bytes 159752 | tf_op jit(solution)/shard_map/ppermute | solution.py:382
  56.8 4.3 %collective-permute-start.18 = (f32[2,104,128]{2,1,0:T(8,128)S(1)}, f32[2,104,128]{2,1,0:T(8,128)S(1)}, u32[]{:S(2)}, u32[]{:S(2)}) collective-permute-start(f32[2,104,128]{2,1,0:T(8,128)S(1)} %get-tuple-element.630), channel_id=1, source_target_pairs={{1,2},{5,6},{9,10},{13,14},{17,18},{20,21},{22,23},{25,26},{29,30}... | collective-permute-start | bytes 319496 | tf_op jit(solution)/shard_map/ppermute | solution.py:402
  61.3 6.8 %collective-permute-start.19 = (f32[104,128]{1,0:T(8,128)S(1)}, f32[104,128]{1,0:T(8,128)S(1)}, u32[]{:S(2)}, u32[]{:S(2)}) collective-permute-start(f32[104,128]{1,0:T(8,128)S(1)} %get-tuple-element.640), channel_id=1, source_target_pairs={{0,4},{1,5},{2,6},{3,7},{8,12},{9,13},{10,14},{11,15},{16,20},{17,... | collective-permute-start | bytes 159752 | tf_op jit(solution)/shard_map/ppermute | solution.py:382
  69.4 9.6 %collective-permute-start.23 = (f32[104,128]{1,0:T(8,128)S(1)}, f32[104,128]{1,0:T(8,128)S(1)}, u32[]{:S(2)}, u32[]{:S(2)}) collective-permute-start(f32[104,128]{1,0:T(8,128)S(1)} %get-tuple-element.668), channel_id=1, source_target_pairs={{0,4},{1,5},{2,6},{3,7},{8,12},{9,13},{10,14},{11,15},{16,20},{17,... | collective-permute-start | bytes 159752 | tf_op jit(solution)/shard_map/ppermute | solution.py:382
  82.1 8.4 %collective-permute-start.27 = (f32[104,128]{1,0:T(8,128)S(1)}, f32[104,128]{1,0:T(8,128)S(1)}, u32[]{:S(2)}, u32[]{:S(2)}) collective-permute-start(f32[104,128]{1,0:T(8,128)S(1)} %get-tuple-element.696), channel_id=1, source_target_pairs={{0,4},{1,5},{2,6},{3,7},{8,12},{9,13},{10,14},{11,15},{16,20},{17,... | collective-permute-start | bytes 159752 | tf_op jit(solution)/shard_map/ppermute | solution.py:382
  93.7 9.5 %collective-permute-start.31 = (f32[104,128]{1,0:T(8,128)S(1)}, f32[104,128]{1,0:T(8,128)S(1)}, u32[]{:S(2)}, u32[]{:S(2)}) collective-permute-start(f32[104,128]{1,0:T(8,128)S(1)} %get-tuple-element.724), channel_id=1, source_target_pairs={{0,4},{1,5},{2,6},{3,7},{8,12},{9,13},{10,14},{11,15},{16,20},{17,... | collective-permute-start | bytes 159752 | tf_op jit(solution)/shard_map/ppermute | solution.py:382
  101.0 4.4 %collective-permute-start.34 = (f32[2,104,128]{2,1,0:T(8,128)S(1)}, f32[2,104,128]{2,1,0:T(8,128)S(1)}, u32[]{:S(2)}, u32[]{:S(2)}) collective-permute-start(f32[2,104,128]{2,1,0:T(8,128)S(1)} %get-tuple-element.742), channel_id=1, source_target_pairs={{1,2},{5,6},{8,9},{10,11},{13,14},{17,18},{20,21},{22,23},{25,26},... | collective-permute-start | bytes 319496 | tf_op jit(solution)/shard_map/ppermute | solution.py:402
  106.5 7.6 %collective-permute-start.35 = (f32[104,128]{1,0:T(8,128)S(1)}, f32[104,128]{1,0:T(8,128)S(1)}, u32[]{:S(2)}, u32[]{:S(2)}) collective-permute-start(f32[104,128]{1,0:T(8,128)S(1)} %get-tuple-element.752), channel_id=1, source_target_pairs={{0,4},{1,5},{2,6},{3,7},{8,12},{9,13},{10,14},{11,15},{16,20},{17,... | collective-permute-start | bytes 159752 | tf_op jit(solution)/shard_map/ppermute | solution.py:382
  112.1 4.2 %collective-permute-start.38 = (f32[2,104,128]{2,1,0:T(8,128)S(1)}, f32[2,104,128]{2,1,0:T(8,128)S(1)}, u32[]{:S(2)}, u32[]{:S(2)}) collective-permute-start(f32[2,104,128]{2,1,0:T(8,128)S(1)} %get-tuple-element.770), channel_id=1, source_target_pairs={{0,1},{2,3},{5,6},{9,10},{12,13},{14,15},{16,17},{18,19},{21,22},{... | collective-permute-start | bytes 319496 | tf_op jit(solution)/shard_map/ppermute | solution.py:402
  118.2 6.6 %collective-permute-start.39 = (f32[104,128]{1,0:T(8,128)S(1)}, f32[104,128]{1,0:T(8,128)S(1)}, u32[]{:S(2)}, u32[]{:S(2)}) collective-permute-start(f32[104,128]{1,0:T(8,128)S(1)} %get-tuple-element.780), channel_id=1, source_target_pairs={{0,4},{1,5},{2,6},{3,7},{8,12},{9,13},{10,14},{11,15},{16,20},{17,... | collective-permute-start | bytes 159752 | tf_op jit(solution)/shard_map/ppermute | solution.py:382
  122.7 4.7 %collective-permute-start.42 = (f32[2,104,128]{2,1,0:T(8,128)S(1)}, f32[2,104,128]{2,1,0:T(8,128)S(1)}, u32[]{:S(2)}, u32[]{:S(2)}) collective-permute-start(f32[2,104,128]{2,1,0:T(8,128)S(1)} %get-tuple-element.798), channel_id=1, source_target_pairs={{1,2},{4,5},{6,7},{8,9},{10,11},{13,14},{17,18},{20,21},{22,23},{2... | collective-permute-start | bytes 319496 | tf_op jit(solution)/shard_map/ppermute | solution.py:402
  127.6 7.6 %collective-permute-start.43 = (f32[104,128]{1,0:T(8,128)S(1)}, f32[104,128]{1,0:T(8,128)S(1)}, u32[]{:S(2)}, u32[]{:S(2)}) collective-permute-start(f32[104,128]{1,0:T(8,128)S(1)} %get-tuple-element.808), channel_id=1, source_target_pairs={{0,4},{1,5},{2,6},{3,7},{8,12},{9,13},{10,14},{11,15},{16,20},{17,... | collective-permute-start | bytes 159752 | tf_op jit(solution)/shard_map/ppermute | solution.py:382
  136.8 7.5 %collective-permute-start.47 = (f32[104,128]{1,0:T(8,128)S(1)}, f32[104,128]{1,0:T(8,128)S(1)}, u32[]{:S(2)}, u32[]{:S(2)}) collective-permute-start(f32[104,128]{1,0:T(8,128)S(1)} %get-tuple-element.836), channel_id=1, source_target_pairs={{0,4},{1,5},{2,6},{3,7},{8,12},{9,13},{10,14},{11,15},{16,20},{17,... | collective-permute-start | bytes 159752 | tf_op jit(solution)/shard_map/ppermute | solution.py:382
  145.6 7.9 %collective-permute-start.51 = (f32[104,128]{1,0:T(8,128)S(1)}, f32[104,128]{1,0:T(8,128)S(1)}, u32[]{:S(2)}, u32[]{:S(2)}) collective-permute-start(f32[104,128]{1,0:T(8,128)S(1)} %get-tuple-element.864), channel_id=1, source_target_pairs={{0,4},{1,5},{2,6},{3,7},{8,12},{9,13},{10,14},{11,15},{16,20},{17,... | collective-permute-start | bytes 159752 | tf_op jit(solution)/shard_map/ppermute | solution.py:382
  154.8 9.5 %collective-permute-start.55 = (f32[104,128]{1,0:T(8,128)S(1)}, f32[104,128]{1,0:T(8,128)S(1)}, u32[]{:S(2)}, u32[]{:S(2)}) collective-permute-start(f32[104,128]{1,0:T(8,128)S(1)} %get-tuple-element.892), channel_id=1, source_target_pairs={{0,4},{1,5},{2,6},{3,7},{8,12},{9,13},{10,14},{11,15},{16,20},{17,... | collective-permute-start | bytes 159752 | tf_op jit(solution)/shard_map/ppermute | solution.py:382
  166.5 8.1 %collective-permute-start.58 = (f32[104,128]{1,0:T(8,128)S(1)}, f32[104,128]{1,0:T(8,128)S(1)}, u32[]{:S(2)}, u32[]{:S(2)}) collective-permute-start(f32[104,128]{1,0:T(8,128)S(1)} %get-tuple-element.919), channel_id=1, source_target_pairs={{0,4},{1,5},{2,6},{3,7},{8,12},{9,13},{10,14},{11,15},{16,20},{17,... | collective-permute-start | bytes 159752 | tf_op jit(solution)/shard_map/ppermute | solution.py:382
  176.8 8.0 %collective-permute-start.60 = (f32[104,128]{1,0:T(8,128)S(1)}, f32[104,128]{1,0:T(8,128)S(1)}, u32[]{:S(2)}, u32[]{:S(2)}) collective-permute-start(f32[104,128]{1,0:T(8,128)S(1)} %get-tuple-element.937), channel_id=1, source_target_pairs={{0,4},{1,5},{2,6},{3,7},{8,12},{9,13},{10,14},{11,15},{16,20},{17,... | collective-permute-start | bytes 159752 | tf_op jit(solution)/shard_map/ppermute | solution.py:382
  187.0 8.5 %collective-permute-start.62 = (f32[104,128]{1,0:T(8,128)S(1)}, f32[104,128]{1,0:T(8,128)S(1)}, u32[]{:S(2)}, u32[]{:S(2)}) collective-permute-start(f32[104,128]{1,0:T(8,128)S(1)} %get-tuple-element.955), channel_id=1, source_target_pairs={{0,4},{1,5},{2,6},{3,7},{8,12},{9,13},{10,14},{11,15},{16,20},{17,... | collective-permute-start | bytes 159752 | tf_op jit(solution)/shard_map/ppermute | solution.py:382
  (39 other events, 77.1 us)

commit v7 on v6

--- a/solution.py
+++ b/solution.py
@@ -375,11 +375,16 @@
         base, latest, out, value, *cross = results[used:]
 
         if any(urgent[tick]) or any(one[0] and one[2] > 0 for one in tasks_at(tick + 1)):
-            swap = [(s, s + 1) for s in range(tick & 1, count - 1, 2)]
-            alone = [s for s in range(count) if all(s not in two for two in swap)]
-            pairs = [(device(a, p), device(b, p)) for a, b in swap for p in range(parts)]
-            pairs += [(device(s, a), device(s, b)) for s in alone for a, b in even_pairs]
-            incoming = lax.ppermute(value, ("sweep", "span"), closed(pairs, range(count * parts)))
+            pairs = [
+                (device(s, p), device(s + 1 if one[3] else s - 1, p))
+                for s, one in enumerate(tasks)
+                if one[0] and one[2] < count - 1
+                for p in range(parts)
+            ]
+            pairs += [
+                (device(s, x), device(s, y)) for s in range(count) if urgent[tick][s] for a, b in even_pairs for x, y in ((a, b), (b, a))
+            ]
+            incoming = lax.ppermute(value, ("sweep", "span"), pairs)
         came = [None if not tick or urgent[tick - 1][s] else sent[tick - 1][s] for s in range(count)]
         later = any(plan) and not at_once
         if any(came) or later:

time: 200 us -> 281 us (1.41)
  waiting for transfers between devices: 27.7 us -> 80.4 us
  starting transfers between devices: 135 us -> 162 us
    ppermute x26, starting transfers between devices: 23.8 us -> 88 us  [per_device(): lax.ppermute(cross[0], ('sweep', 'span'), closed(pairs, range(count * par...]
    ppermute x37, waiting for transfers between devices: 27 us -> 79.9 us  [per_device(): incoming = lax.ppermute(value, ('sweep', 'span'), pairs)]
    ppermute x37, starting transfers between devices: 112 us -> 73.9 us  [per_device(): incoming = lax.ppermute(value, ('sweep', 'span'), pairs)]
  transfers between devices with their start and end apart: 63 -> 63, of which waited for: 29 -> 9; matrix products, arithmetic and copies ran while one was open for 0% -> 0% of each run, Pallas kernels for 10% -> 8%
where the time goes in v7:
time: 281 us; the launch traced here: 279 us
  starting transfers between devices  162 us (58%)
  waiting for transfers between devices  80.4 us (29%)
  Pallas kernels  33.5 us (12%)
    ppermute x26, starting transfers between devices, per_device(): lax.ppermute(cross[0], ('sweep', 'span'), closed(pairs, range(count * par...  88 us
    ppermute x37, waiting for transfers between devices, per_device(): incoming = lax.ppermute(value, ('sweep', 'span'), pairs)  79.9 us
    ppermute x37, starting transfers between devices, per_device(): incoming = lax.ppermute(value, ('sweep', 'span'), pairs)  73.9 us
    pallas_call x66, Pallas kernels, call(): pl.pallas_call(body, out_shape=tuple((held(shape) for shape in [*(a.shape...  19 us
    pallas_call x4, Pallas kernels, later_call(): pl.pallas_call(functools.partial(later_kernel, face), out_shape=(held((si...  11.5 us
  transfers between devices with their start and end apart: 63, of which 9 were waited for; matrix products, arithmetic and copies ran while one was open for 0% of the time, Pallas kernels for 8%

profile of v7, /device:TPU:0, one launch (start us, length us, event | category | flops | bytes accessed | tf_op | source)
XLA Modules:
  0.0 278.9 jit_solution(1328154402159213037)
XLA Ops:
  0.9 3.0 %first.1 = (f32[100,104,128]{2,1,0:T(8,128)S(1)}, f32[4,104,128]{2,1,0:T(8,128)S(1)}, f32[4,104,128]{2,1,0:T(8,128)S(1)}, f32[104,128]{1,0:T(8,128)S(1)}, s32[1,...) custom-call(bf16[100,100,128]{2,1,0:T(8,128)(2,1)} %bitcast.11, ...), custom_call_target="tpu_custom_call" | custom-call | tf_op jit(solution)/shard_map/first/pallas_call | solution.py:295
  4.4 4.4 %collective-permute-start = (f32[104,128]{1,0:T(8,128)S(1)}, f32[104,128]{1,0:T(8,128)S(1)}, u32[]{:S(2)}, u32[]{:S(2)}) collective-permute-start(f32[104,128]{1,0:T(8,128)S(1)} %get-tuple-element.495), channel_id=1, source_target_pairs={{0,4},{1,5},{2,6},{3,7}} | collective-permute-start | bytes 159752 | tf_op jit(solution)/shard_map/ppermute | solution.py:387
  8.9 2.9 %later.4 = (f32[100,104,128]{2,1,0:T(8,128)S(1)}, f32[4,104,128]{2,1,0:T(8,128)S(1)}) custom-call(bf16[1,1,100,100,128]{4,3,2,1,0:T(8,128)(2,1)} %block.4, f32[4,104,128]{2,1,0:T(8,128)S(1)} %get-tuple-element.497.base_in), custom_call_target="tpu_custom_call", output_to_operand_aliasing={{1}: (1, {})} | custom-call | tf_op jit(solution)/shard_map/later/pallas_call | solution.py:312
  15.8 4.2 %collective-permute-start.2 = (f32[104,128]{1,0:T(8,128)S(1)}, f32[104,128]{1,0:T(8,128)S(1)}, u32[]{:S(2)}, u32[]{:S(2)}) collective-permute-start(f32[104,128]{1,0:T(8,128)S(1)} %get-tuple-element.510), channel_id=1, source_target_pairs={{0,4},{1,5},{2,6},{3,7},{8,12},{9,13},{10,14},{11,15}} | collective-permute-start | bytes 159752 | tf_op jit(solution)/shard_map/ppermute | solution.py:387
  26.9 5.1 %collective-permute-start.4 = (f32[104,128]{1,0:T(8,128)S(1)}, f32[104,128]{1,0:T(8,128)S(1)}, u32[]{:S(2)}, u32[]{:S(2)}) collective-permute-start(f32[104,128]{1,0:T(8,128)S(1)} %get-tuple-element.529), channel_id=1, source_target_pairs={{0,4},{1,5},{2,6},{3,7},{8,12},{9,13},{10,14},{11,15},{16,20},{17,... | collective-permute-start | bytes 159752 | tf_op jit(solution)/shard_map/ppermute | solution.py:387
  32.1 3.3 %collective-permute-start.6 = (f32[2,104,128]{2,1,0:T(8,128)S(1)}, f32[2,104,128]{2,1,0:T(8,128)S(1)}, u32[]{:S(2)}, u32[]{:S(2)}) collective-permute-start(f32[2,104,128]{2,1,0:T(8,128)S(1)} %get-tuple-element.546), channel_id=1, source_target_pairs={{0,1},{2,3},{4,5},{6,7},{8,9},{10,11},{12,13},{14,15},{16,17},{18,... | collective-permute-start | bytes 319496 | tf_op jit(solution)/shard_map/ppermute | solution.py:407
  37.9 6.4 %collective-permute-start.7 = (f32[104,128]{1,0:T(8,128)S(1)}, f32[104,128]{1,0:T(8,128)S(1)}, u32[]{:S(2)}, u32[]{:S(2)}) collective-permute-start(f32[104,128]{1,0:T(8,128)S(1)} %get-tuple-element.556), channel_id=1, source_target_pairs={{0,4},{1,5},{2,6},{3,7},{8,12},{9,13},{10,14},{11,15},{16,20},{17,... | collective-permute-start | bytes 159752 | tf_op jit(solution)/shard_map/ppermute | solution.py:387
  48.3 17.8 %collective-permute-start.14 = (f32[2,104,128]{2,1,0:T(8,128)S(1)}, f32[2,104,128]{2,1,0:T(8,128)S(1)}, u32[]{:S(2)}, u32[]{:S(2)}) collective-permute-start(f32[2,104,128]{2,1,0:T(8,128)S(1)} %get-tuple-element.602), channel_id=1, source_target_pairs={{0,1},{2,3},{4,5},{6,7},{8,9},{10,11},{12,13},{14,15},{16,17},{18,... | collective-permute-start | bytes 319496 | tf_op jit(solution)/shard_map/ppermute | solution.py:407
  69.3 16.0 %collective-permute-start.18 = (f32[2,104,128]{2,1,0:T(8,128)S(1)}, f32[2,104,128]{2,1,0:T(8,128)S(1)}, u32[]{:S(2)}, u32[]{:S(2)}) collective-permute-start(f32[2,104,128]{2,1,0:T(8,128)S(1)} %get-tuple-element.630), channel_id=1, source_target_pairs={{1,2},{5,6},{9,10},{13,14},{17,18},{20,21},{22,23},{25,26},{29,30}... | collective-permute-start | bytes 319496 | tf_op jit(solution)/shard_map/ppermute | solution.py:407
  91.8 18.6 %collective-permute-done.23.refs_5_ = f32[104,128]{1,0:T(8,128)S(1)} collective-permute-done((f32[104,128]{1,0:T(8,128)S(1)}, f32[104,128]{1,0:T(8,128)S(1)}, u32[]{:S(2)}, u32[]{:S(2)}) %collective-permute-start.23) | collective-permute-done | bytes 53280 | tf_op jit(solution)/shard_map/ppermute | solution.py:387
  115.3 6.2 %collective-permute-start.27 = (f32[104,128]{1,0:T(8,128)S(1)}, f32[104,128]{1,0:T(8,128)S(1)}, u32[]{:S(2)}, u32[]{:S(2)}) collective-permute-start(f32[104,128]{1,0:T(8,128)S(1)} %get-tuple-element.696), channel_id=1, source_target_pairs={{0,4},{1,5},{2,6},{3,7},{4,0},{5,1},{6,2},{7,3},{12,8},{13,9},{14,... | collective-permute-start | bytes 159752 | tf_op jit(solution)/shard_map/ppermute | solution.py:387
  121.6 8.7 %collective-permute-start.30 = (f32[2,104,128]{2,1,0:T(8,128)S(1)}, f32[2,104,128]{2,1,0:T(8,128)S(1)}, u32[]{:S(2)}, u32[]{:S(2)}) collective-permute-start(f32[2,104,128]{2,1,0:T(8,128)S(1)} %get-tuple-element.714), channel_id=1, source_target_pairs={{0,1},{2,3},{5,6},{9,10},{12,13},{14,15},{16,17},{18,19},{21,22},{... | collective-permute-start | bytes 319496 | tf_op jit(solution)/shard_map/ppermute | solution.py:407
  135.7 6.9 %collective-permute-start.31 = (f32[104,128]{1,0:T(8,128)S(1)}, f32[104,128]{1,0:T(8,128)S(1)}, u32[]{:S(2)}, u32[]{:S(2)}) collective-permute-start(f32[104,128]{1,0:T(8,128)S(1)} %get-tuple-element.724), channel_id=1, source_target_pairs={{0,4},{1,5},{2,6},{3,7},{4,0},{5,1},{6,2},{7,3},{8,12},{9,13},{10,... | collective-permute-start | bytes 159752 | tf_op jit(solution)/shard_map/ppermute | solution.py:387
  142.7 4.0 %collective-permute-start.34 = (f32[2,104,128]{2,1,0:T(8,128)S(1)}, f32[2,104,128]{2,1,0:T(8,128)S(1)}, u32[]{:S(2)}, u32[]{:S(2)}) collective-permute-start(f32[2,104,128]{2,1,0:T(8,128)S(1)} %get-tuple-element.742), channel_id=1, source_target_pairs={{1,2},{5,6},{8,9},{10,11},{13,14},{17,18},{20,21},{22,23},{25,26},... | collective-permute-start | bytes 319496 | tf_op jit(solution)/shard_map/ppermute | solution.py:407
  147.7 2.9 %collective-permute-start.32 = (f32[104,128]{1,0:T(8,128)S(1)}, f32[104,128]{1,0:T(8,128)S(1)}, u32[]{:S(2)}, u32[]{:S(2)}) collective-permute-start(f32[104,128]{1,0:T(8,128)S(1)} %get-tuple-element.737), channel_id=1, source_target_pairs={{4,8},{5,9},{6,10},{7,11},{8,4},{9,5},{10,6},{11,7},{12,16},{13,17... | collective-permute-start | bytes 159752 | tf_op jit(solution)/shard_map/ppermute | solution.py:387
  152.4 7.3 %collective-permute-start.35 = (f32[104,128]{1,0:T(8,128)S(1)}, f32[104,128]{1,0:T(8,128)S(1)}, u32[]{:S(2)}, u32[]{:S(2)}) collective-permute-start(f32[104,128]{1,0:T(8,128)S(1)} %get-tuple-element.752), channel_id=1, source_target_pairs={{0,4},{1,5},{2,6},{3,7},{4,0},{5,1},{6,2},{7,3},{8,12},{9,13},{10,... | collective-permute-start | bytes 159752 | tf_op jit(solution)/shard_map/ppermute | solution.py:387
  159.7 4.5 %collective-permute-start.38 = (f32[2,104,128]{2,1,0:T(8,128)S(1)}, f32[2,104,128]{2,1,0:T(8,128)S(1)}, u32[]{:S(2)}, u32[]{:S(2)}) collective-permute-start(f32[2,104,128]{2,1,0:T(8,128)S(1)} %get-tuple-element.770), channel_id=1, source_target_pairs={{0,1},{2,3},{5,6},{9,10},{12,13},{14,15},{16,17},{18,19},{21,22},{... | collective-permute-start | bytes 319496 | tf_op jit(solution)/shard_map/ppermute | solution.py:407
  170.1 4.0 %collective-permute-start.39 = (f32[104,128]{1,0:T(8,128)S(1)}, f32[104,128]{1,0:T(8,128)S(1)}, u32[]{:S(2)}, u32[]{:S(2)}) collective-permute-start(f32[104,128]{1,0:T(8,128)S(1)} %get-tuple-element.780), channel_id=1, source_target_pairs={{0,4},{1,5},{2,6},{3,7},{8,12},{9,13},{10,14},{11,15},{16,20},{17,... | collective-permute-start | bytes 159752 | tf_op jit(solution)/shard_map/ppermute | solution.py:387
  174.2 4.1 %collective-permute-start.42 = (f32[2,104,128]{2,1,0:T(8,128)S(1)}, f32[2,104,128]{2,1,0:T(8,128)S(1)}, u32[]{:S(2)}, u32[]{:S(2)}) collective-permute-start(f32[2,104,128]{2,1,0:T(8,128)S(1)} %get-tuple-element.798), channel_id=1, source_target_pairs={{1,2},{4,5},{6,7},{8,9},{10,11},{13,14},{17,18},{20,21},{22,23},{2... | collective-permute-start | bytes 319496 | tf_op jit(solution)/shard_map/ppermute | solution.py:407
  180.6 17.5 %collective-permute-start.46 = (f32[2,104,128]{2,1,0:T(8,128)S(1)}, f32[2,104,128]{2,1,0:T(8,128)S(1)}, u32[]{:S(2)}, u32[]{:S(2)}) collective-permute-start(f32[2,104,128]{2,1,0:T(8,128)S(1)} %get-tuple-element.826), channel_id=1, source_target_pairs={{0,1},{2,3},{4,5},{6,7},{9,10},{12,13},{14,15},{16,17},{18,19},{21... | collective-permute-start | bytes 319496 | tf_op jit(solution)/shard_map/ppermute | solution.py:407
  208.2 27.8 %collective-permute-done.55.refs_5_ = f32[104,128]{1,0:T(8,128)S(1)} collective-permute-done((f32[104,128]{1,0:T(8,128)S(1)}, f32[104,128]{1,0:T(8,128)S(1)}, u32[]{:S(2)}, u32[]{:S(2)}) %collective-permute-start.55) | collective-permute-done | bytes 53280 | tf_op jit(solution)/shard_map/ppermute | solution.py:387
  238.9 11.3 %collective-permute-done.58.refs_5_ = f32[104,128]{1,0:T(8,128)S(1)} collective-permute-done((f32[104,128]{1,0:T(8,128)S(1)}, f32[104,128]{1,0:T(8,128)S(1)}, u32[]{:S(2)}, u32[]{:S(2)}) %collective-permute-start.58) | collective-permute-done | bytes 53280 | tf_op jit(solution)/shard_map/ppermute | solution.py:387
  253.1 10.4 %collective-permute-done.60.refs_5_ = f32[104,128]{1,0:T(8,128)S(1)} collective-permute-done((f32[104,128]{1,0:T(8,128)S(1)}, f32[104,128]{1,0:T(8,128)S(1)}, u32[]{:S(2)}, u32[]{:S(2)}) %collective-permute-start.60) | collective-permute-done | bytes 53280 | tf_op jit(solution)/shard_map/ppermute | solution.py:387
  266.5 10.2 %collective-permute-done.62.refs_5_ = f32[104,128]{1,0:T(8,128)S(1)} collective-permute-done((f32[104,128]{1,0:T(8,128)S(1)}, f32[104,128]{1,0:T(8,128)S(1)}, u32[]{:S(2)}, u32[]{:S(2)}) %collective-permute-start.62) | collective-permute-done | bytes 53280 | tf_op jit(solution)/shard_map/ppermute | solution.py:387
  (176 shorter events, 69.5 us)
Async XLA Ops:
  4.4 7.3 %collective-permute-start = (f32[104,128]{1,0:T(8,128)S(1)}, f32[104,128]{1,0:T(8,128)S(1)}, u32[]{:S(2)}, u32[]{:S(2)}) collective-permute-start(f32[104,128]{1,0:T(8,128)S(1)} %get-tuple-element.495), channel_id=1, source_target_pairs={{0,4},{1,5},{2,6},{3,7}} | collective-permute-start | bytes 159752 | tf_op jit(solution)/shard_map/ppermute | solution.py:387
  15.8 7.1 %collective-permute-start.2 = (f32[104,128]{1,0:T(8,128)S(1)}, f32[104,128]{1,0:T(8,128)S(1)}, u32[]{:S(2)}, u32[]{:S(2)}) collective-permute-start(f32[104,128]{1,0:T(8,128)S(1)} %get-tuple-element.510), channel_id=1, source_target_pairs={{0,4},{1,5},{2,6},{3,7},{8,12},{9,13},{10,14},{11,15}} | collective-permute-start | bytes 159752 | tf_op jit(solution)/shard_map/ppermute | solution.py:387
  26.9 8.4 %collective-permute-start.4 = (f32[104,128]{1,0:T(8,128)S(1)}, f32[104,128]{1,0:T(8,128)S(1)}, u32[]{:S(2)}, u32[]{:S(2)}) collective-permute-start(f32[104,128]{1,0:T(8,128)S(1)} %get-tuple-element.529), channel_id=1, source_target_pairs={{0,4},{1,5},{2,6},{3,7},{8,12},{9,13},{10,14},{11,15},{16,20},{17,... | collective-permute-start | bytes 159752 | tf_op jit(solution)/shard_map/ppermute | solution.py:387
  37.9 8.2 %collective-permute-start.7 = (f32[104,128]{1,0:T(8,128)S(1)}, f32[104,128]{1,0:T(8,128)S(1)}, u32[]{:S(2)}, u32[]{:S(2)}) collective-permute-start(f32[104,128]{1,0:T(8,128)S(1)} %get-tuple-element.556), channel_id=1, source_target_pairs={{0,4},{1,5},{2,6},{3,7},{8,12},{9,13},{10,14},{11,15},{16,20},{17,... | collective-permute-start | bytes 159752 | tf_op jit(solution)/shard_map/ppermute | solution.py:387
  47.6 18.6 %collective-permute-start.11 = (f32[104,128]{1,0:T(8,128)S(1)}, f32[104,128]{1,0:T(8,128)S(1)}, u32[]{:S(2)}, u32[]{:S(2)}) collective-permute-start(f32[104,128]{1,0:T(8,128)S(1)} %get-tuple-element.584), channel_id=1, source_target_pairs={{8,12},{9,13},{10,14},{11,15},{16,20},{17,21},{18,22},{19,23},{24,... | collective-permute-start | bytes 159752 | tf_op jit(solution)/shard_map/ppermute | solution.py:387
  48.3 19.3 %collective-permute-start.14 = (f32[2,104,128]{2,1,0:T(8,128)S(1)}, f32[2,104,128]{2,1,0:T(8,128)S(1)}, u32[]{:S(2)}, u32[]{:S(2)}) collective-permute-start(f32[2,104,128]{2,1,0:T(8,128)S(1)} %get-tuple-element.602), channel_id=1, source_target_pairs={{0,1},{2,3},{4,5},{6,7},{8,9},{10,11},{12,13},{14,15},{16,17},{18,... | collective-permute-start | bytes 319496 | tf_op jit(solution)/shard_map/ppermute | solution.py:407
  68.6 16.8 %collective-permute-start.15 = (f32[104,128]{1,0:T(8,128)S(1)}, f32[104,128]{1,0:T(8,128)S(1)}, u32[]{:S(2)}, u32[]{:S(2)}) collective-permute-start(f32[104,128]{1,0:T(8,128)S(1)} %get-tuple-element.612), channel_id=1, source_target_pairs={{16,20},{17,21},{18,22},{19,23},{20,16},{21,17},{22,18},{23,19},{2... | collective-permute-start | bytes 159752 | tf_op jit(solution)/shard_map/ppermute | solution.py:387
  69.3 17.5 %collective-permute-start.18 = (f32[2,104,128]{2,1,0:T(8,128)S(1)}, f32[2,104,128]{2,1,0:T(8,128)S(1)}, u32[]{:S(2)}, u32[]{:S(2)}) collective-permute-start(f32[2,104,128]{2,1,0:T(8,128)S(1)} %get-tuple-element.630), channel_id=1, source_target_pairs={{1,2},{5,6},{9,10},{13,14},{17,18},{20,21},{22,23},{25,26},{29,30}... | collective-permute-start | bytes 319496 | tf_op jit(solution)/shard_map/ppermute | solution.py:407
  89.8 20.6 %collective-permute-start.23 = (f32[104,128]{1,0:T(8,128)S(1)}, f32[104,128]{1,0:T(8,128)S(1)}, u32[]{:S(2)}, u32[]{:S(2)}) collective-permute-start(f32[104,128]{1,0:T(8,128)S(1)} %get-tuple-element.668), channel_id=1, source_target_pairs={{4,0},{5,1},{6,2},{7,3},{12,8},{13,9},{14,10},{15,11},{20,16},{21,... | collective-permute-start | bytes 159752 | tf_op jit(solution)/shard_map/ppermute | solution.py:387
  91.1 22.8 %collective-permute-start.26 = (f32[2,104,128]{2,1,0:T(8,128)S(1)}, f32[2,104,128]{2,1,0:T(8,128)S(1)}, u32[]{:S(2)}, u32[]{:S(2)}) collective-permute-start(f32[2,104,128]{2,1,0:T(8,128)S(1)} %get-tuple-element.686), channel_id=1, source_target_pairs={{5,6},{8,9},{10,11},{13,14},{17,18},{20,21},{22,23},{24,25},{26,27... | collective-permute-start | bytes 319496 | tf_op jit(solution)/shard_map/ppermute | solution.py:407
  115.3 15.0 %collective-permute-start.27 = (f32[104,128]{1,0:T(8,128)S(1)}, f32[104,128]{1,0:T(8,128)S(1)}, u32[]{:S(2)}, u32[]{:S(2)}) collective-permute-start(f32[104,128]{1,0:T(8,128)S(1)} %get-tuple-element.696), channel_id=1, source_target_pairs={{0,4},{1,5},{2,6},{3,7},{4,0},{5,1},{6,2},{7,3},{12,8},{13,9},{14,... | collective-permute-start | bytes 159752 | tf_op jit(solution)/shard_map/ppermute | solution.py:387
  121.6 12.6 %collective-permute-start.30 = (f32[2,104,128]{2,1,0:T(8,128)S(1)}, f32[2,104,128]{2,1,0:T(8,128)S(1)}, u32[]{:S(2)}, u32[]{:S(2)}) collective-permute-start(f32[2,104,128]{2,1,0:T(8,128)S(1)} %get-tuple-element.714), channel_id=1, source_target_pairs={{0,1},{2,3},{5,6},{9,10},{12,13},{14,15},{16,17},{18,19},{21,22},{... | collective-permute-start | bytes 319496 | tf_op jit(solution)/shard_map/ppermute | solution.py:407
  135.7 11.0 %collective-permute-start.31 = (f32[104,128]{1,0:T(8,128)S(1)}, f32[104,128]{1,0:T(8,128)S(1)}, u32[]{:S(2)}, u32[]{:S(2)}) collective-permute-start(f32[104,128]{1,0:T(8,128)S(1)} %get-tuple-element.724), channel_id=1, source_target_pairs={{0,4},{1,5},{2,6},{3,7},{4,0},{5,1},{6,2},{7,3},{8,12},{9,13},{10,... | collective-permute-start | bytes 159752 | tf_op jit(solution)/shard_map/ppermute | solution.py:387
  142.7 8.6 %collective-permute-start.34 = (f32[2,104,128]{2,1,0:T(8,128)S(1)}, f32[2,104,128]{2,1,0:T(8,128)S(1)}, u32[]{:S(2)}, u32[]{:S(2)}) collective-permute-start(f32[2,104,128]{2,1,0:T(8,128)S(1)} %get-tuple-element.742), channel_id=1, source_target_pairs={{1,2},{5,6},{8,9},{10,11},{13,14},{17,18},{20,21},{22,23},{25,26},... | collective-permute-start | bytes 319496 | tf_op jit(solution)/shard_map/ppermute | solution.py:407
  152.4 11.9 %collective-permute-start.35 = (f32[104,128]{1,0:T(8,128)S(1)}, f32[104,128]{1,0:T(8,128)S(1)}, u32[]{:S(2)}, u32[]{:S(2)}) collective-permute-start(f32[104,128]{1,0:T(8,128)S(1)} %get-tuple-element.752), channel_id=1, source_target_pairs={{0,4},{1,5},{2,6},{3,7},{4,0},{5,1},{6,2},{7,3},{8,12},{9,13},{10,... | collective-permute-start | bytes 159752 | tf_op jit(solution)/shard_map/ppermute | solution.py:387
  159.7 8.4 %collective-permute-start.38 = (f32[2,104,128]{2,1,0:T(8,128)S(1)}, f32[2,104,128]{2,1,0:T(8,128)S(1)}, u32[]{:S(2)}, u32[]{:S(2)}) collective-permute-start(f32[2,104,128]{2,1,0:T(8,128)S(1)} %get-tuple-element.770), channel_id=1, source_target_pairs={{0,1},{2,3},{5,6},{9,10},{12,13},{14,15},{16,17},{18,19},{21,22},{... | collective-permute-start | bytes 319496 | tf_op jit(solution)/shard_map/ppermute | solution.py:407
  170.1 8.2 %collective-permute-start.39 = (f32[104,128]{1,0:T(8,128)S(1)}, f32[104,128]{1,0:T(8,128)S(1)}, u32[]{:S(2)}, u32[]{:S(2)}) collective-permute-start(f32[104,128]{1,0:T(8,128)S(1)} %get-tuple-element.780), channel_id=1, source_target_pairs={{0,4},{1,5},{2,6},{3,7},{8,12},{9,13},{10,14},{11,15},{16,20},{17,... | collective-permute-start | bytes 159752 | tf_op jit(solution)/shard_map/ppermute | solution.py:387
  179.9 18.3 %collective-permute-start.43 = (f32[104,128]{1,0:T(8,128)S(1)}, f32[104,128]{1,0:T(8,128)S(1)}, u32[]{:S(2)}, u32[]{:S(2)}) collective-permute-start(f32[104,128]{1,0:T(8,128)S(1)} %get-tuple-element.808), channel_id=1, source_target_pairs={{8,12},{9,13},{10,14},{11,15},{16,20},{17,21},{18,22},{19,23},{24,... | collective-permute-start | bytes 159752 | tf_op jit(solution)/shard_map/ppermute | solution.py:387
  180.6 19.0 %collective-permute-start.46 = (f32[2,104,128]{2,1,0:T(8,128)S(1)}, f32[2,104,128]{2,1,0:T(8,128)S(1)}, u32[]{:S(2)}, u32[]{:S(2)}) collective-permute-start(f32[2,104,128]{2,1,0:T(8,128)S(1)} %get-tuple-element.826), channel_id=1, source_target_pairs={{0,1},{2,3},{4,5},{6,7},{9,10},{12,13},{14,15},{16,17},{18,19},{21... | collective-permute-start | bytes 319496 | tf_op jit(solution)/shard_map/ppermute | solution.py:407
  206.1 29.8 %collective-permute-start.55 = (f32[104,128]{1,0:T(8,128)S(1)}, f32[104,128]{1,0:T(8,128)S(1)}, u32[]{:S(2)}, u32[]{:S(2)}) collective-permute-start(f32[104,128]{1,0:T(8,128)S(1)} %get-tuple-element.892), channel_id=1, source_target_pairs={{4,0},{5,1},{6,2},{7,3},{12,8},{13,9},{14,10},{15,11},{20,16},{21,... | collective-permute-start | bytes 159752 | tf_op jit(solution)/shard_map/ppermute | solution.py:387
  207.5 30.0 %collective-permute-start.57 = (f32[2,104,128]{2,1,0:T(8,128)S(1)}, f32[2,104,128]{2,1,0:T(8,128)S(1)}, u32[]{:S(2)}, u32[]{:S(2)}) collective-permute-start(f32[2,104,128]{2,1,0:T(8,128)S(1)} %get-tuple-element.909), channel_id=1, source_target_pairs={{8,9},{10,11},{20,21},{22,23},{9,8},{11,10},{21,20},{23,22},{0,0},... | collective-permute-start | bytes 319496 | tf_op jit(solution)/shard_map/ppermute | solution.py:407
  237.6 12.6 %collective-permute-start.58 = (f32[104,128]{1,0:T(8,128)S(1)}, f32[104,128]{1,0:T(8,128)S(1)}, u32[]{:S(2)}, u32[]{:S(2)}) collective-permute-start(f32[104,128]{1,0:T(8,128)S(1)} %get-tuple-element.919), channel_id=1, source_target_pairs={{4,0},{5,1},{6,2},{7,3},{12,8},{13,9},{14,10},{15,11},{20,16},{21,... | collective-permute-start | bytes 159752 | tf_op jit(solution)/shard_map/ppermute | solution.py:387
  251.8 11.7 %collective-permute-start.60 = (f32[104,128]{1,0:T(8,128)S(1)}, f32[104,128]{1,0:T(8,128)S(1)}, u32[]{:S(2)}, u32[]{:S(2)}) collective-permute-start(f32[104,128]{1,0:T(8,128)S(1)} %get-tuple-element.937), channel_id=1, source_target_pairs={{4,0},{5,1},{6,2},{7,3},{12,8},{13,9},{14,10},{15,11}} | collective-permute-start | bytes 159752 | tf_op jit(solution)/shard_map/ppermute | solution.py:387
  265.2 11.5 %collective-permute-start.62 = (f32[104,128]{1,0:T(8,128)S(1)}, f32[104,128]{1,0:T(8,128)S(1)}, u32[]{:S(2)}, u32[]{:S(2)}) collective-permute-start(f32[104,128]{1,0:T(8,128)S(1)} %get-tuple-element.955), channel_id=1, source_target_pairs={{4,0},{5,1},{6,2},{7,3}} | collective-permute-start | bytes 159752 | tf_op jit(solution)/shard_map/ppermute | solution.py:387
  (39 other events, 74.3 us)

commit v8 on v6

--- a/solution.py
+++ b/solution.py
@@ -77,7 +77,7 @@
     return result
 
 
-def product(matrix, vector, rows, unroll=20):
+def product(matrix, vector, rows, unroll=25):
     def body(step, total):
         for inner in range(unroll):
             j = step * unroll + inner
@@ -375,11 +375,17 @@
         base, latest, out, value, *cross = results[used:]
 
         if any(urgent[tick]) or any(one[0] and one[2] > 0 for one in tasks_at(tick + 1)):
+            pairs = []
             swap = [(s, s + 1) for s in range(tick & 1, count - 1, 2)]
+            for a, b in swap:
+                forth, back = (0 if tasks[one][0] else 1 for one in (a, b))
+                if forth and back:
+                    forth = back = 0
+                for p in range(parts):
+                    pairs += [(device(a, p), device(b, p ^ forth)), (device(b, p), device(a, p ^ back))]
             alone = [s for s in range(count) if all(s not in two for two in swap)]
-            pairs = [(device(a, p), device(b, p)) for a, b in swap for p in range(parts)]
-            pairs += [(device(s, a), device(s, b)) for s in alone for a, b in even_pairs]
-            incoming = lax.ppermute(value, ("sweep", "span"), closed(pairs, range(count * parts)))
+            pairs += [(device(s, x), device(s, y)) for s in alone for a, b in even_pairs for x, y in ((a, b), (b, a))]
+            incoming = lax.ppermute(value, ("sweep", "span"), pairs)
         came = [None if not tick or urgent[tick - 1][s] else sent[tick - 1][s] for s in range(count)]
         later = any(plan) and not at_once
         if any(came) or later:

time: 200 us -> 199 us (level)
  waiting for transfers between devices: 27.7 us -> 32 us
  starting transfers between devices: 135 us -> 131 us
    ppermute x37, starting transfers between devices: 112 us -> 107 us  [per_device(): incoming = lax.ppermute(value, ('sweep', 'span'), pairs)]
    ppermute x37, waiting for transfers between devices: 27 us -> 31.3 us  [per_device(): incoming = lax.ppermute(value, ('sweep', 'span'), pairs)]
  transfers between devices with their start and end apart: 63 -> 63, of which waited for: 29 -> 27; matrix products, arithmetic and copies ran while one was open for 0% -> 0% of each run, Pallas kernels for 10% -> 10%
where the time goes in v8:
time: 199 us; the launch traced here: 198 us
  starting transfers between devices  131 us (66%)
  Pallas kernels  32.1 us (16%)
  waiting for transfers between devices  32 us (16%)
    ppermute x37, starting transfers between devices, per_device(): incoming = lax.ppermute(value, ('sweep', 'span'), pairs)  107 us
    ppermute x37, waiting for transfers between devices, per_device(): incoming = lax.ppermute(value, ('sweep', 'span'), pairs)  31.3 us
    ppermute x26, starting transfers between devices, per_device(): lax.ppermute(cross[0], ('sweep', 'span'), closed(pairs, range(count * par...  24.1 us
    pallas_call x66, Pallas kernels, call(): pl.pallas_call(body, out_shape=tuple((held(shape) for shape in [*(a.shape...  17.6 us
    pallas_call x4, Pallas kernels, later_call(): pl.pallas_call(functools.partial(later_kernel, face), out_shape=(held((si...  11.5 us
  transfers between devices with their start and end apart: 63, of which 27 were waited for; matrix products, arithmetic and copies ran while one was open for 0% of the time, Pallas kernels for 10%

profile of v8, /device:TPU:0, one launch (start us, length us, event | category | flops | bytes accessed | tf_op | source)
XLA Modules:
  0.0 198.1 jit_solution(5708034858945828531)
XLA Ops:
  0.9 3.0 %first.1 = (f32[100,104,128]{2,1,0:T(8,128)S(1)}, f32[4,104,128]{2,1,0:T(8,128)S(1)}, f32[4,104,128]{2,1,0:T(8,128)S(1)}, f32[104,128]{1,0:T(8,128)S(1)}, s32[1,...) custom-call(bf16[100,100,128]{2,1,0:T(8,128)(2,1)} %bitcast.11, ...), custom_call_target="tpu_custom_call" | custom-call | tf_op jit(solution)/shard_map/first/pallas_call | solution.py:295
  10.1 2.9 %later.5 = (f32[100,104,128]{2,1,0:T(8,128)S(1)}, f32[4,104,128]{2,1,0:T(8,128)S(1)}) custom-call(bf16[1,1,3,100,100,128]{5,4,3,2,1,0:T(8,128)(2,1)} %block.7, f32[4,104,128]{2,1,0:T(8,128)S(1)} %get-tuple-element.505.base_in), custom_call_target="tpu_custom_call", output_to_operand_aliasing={{1}: (1, {})} | custom-call | tf_op jit(solution)/shard_map/later/pallas_call | solution.py:312
  13.4 3.2 %collective-permute-start.2 = (f32[104,128]{1,0:T(8,128)S(1)}, f32[104,128]{1,0:T(8,128)S(1)}, u32[]{:S(2)}, u32[]{:S(2)}) collective-permute-start(f32[104,128]{1,0:T(8,128)S(1)} %get-tuple-element.510), channel_id=1, source_target_pairs={{0,4},{4,1},{1,5},{5,0},{2,6},{6,3},{3,7},{7,2},{8,12},{12,9},{9,1... | collective-permute-start | bytes 159752 | tf_op jit(solution)/shard_map/ppermute | solution.py:388
  22.9 3.2 %collective-permute-start.4 = (f32[104,128]{1,0:T(8,128)S(1)}, f32[104,128]{1,0:T(8,128)S(1)}, u32[]{:S(2)}, u32[]{:S(2)}) collective-permute-start(f32[104,128]{1,0:T(8,128)S(1)} %get-tuple-element.529), channel_id=1, source_target_pairs={{0,4},{4,1},{1,5},{5,0},{2,6},{6,3},{3,7},{7,2},{8,12},{12,9},{9,1... | collective-permute-start | bytes 159752 | tf_op jit(solution)/shard_map/ppermute | solution.py:388
  30.7 4.9 %collective-permute-start.7 = (f32[104,128]{1,0:T(8,128)S(1)}, f32[104,128]{1,0:T(8,128)S(1)}, u32[]{:S(2)}, u32[]{:S(2)}) collective-permute-start(f32[104,128]{1,0:T(8,128)S(1)} %get-tuple-element.556), channel_id=1, source_target_pairs={{0,4},{4,1},{1,5},{5,0},{2,6},{6,3},{3,7},{7,2},{8,12},{12,9},{9,1... | collective-permute-start | bytes 159752 | tf_op jit(solution)/shard_map/ppermute | solution.py:388
  40.7 4.8 %collective-permute-start.11 = (f32[104,128]{1,0:T(8,128)S(1)}, f32[104,128]{1,0:T(8,128)S(1)}, u32[]{:S(2)}, u32[]{:S(2)}) collective-permute-start(f32[104,128]{1,0:T(8,128)S(1)} %get-tuple-element.584), channel_id=1, source_target_pairs={{0,4},{4,0},{1,5},{5,1},{2,6},{6,2},{3,7},{7,3},{8,12},{12,9},{9,1... | collective-permute-start | bytes 159752 | tf_op jit(solution)/shard_map/ppermute | solution.py:388
  49.7 4.9 %collective-permute-start.15 = (f32[104,128]{1,0:T(8,128)S(1)}, f32[104,128]{1,0:T(8,128)S(1)}, u32[]{:S(2)}, u32[]{:S(2)}) collective-permute-start(f32[104,128]{1,0:T(8,128)S(1)} %get-tuple-element.612), channel_id=1, source_target_pairs={{0,4},{4,0},{1,5},{5,1},{2,6},{6,2},{3,7},{7,3},{8,12},{12,8},{9,1... | collective-permute-start | bytes 159752 | tf_op jit(solution)/shard_map/ppermute | solution.py:388
  59.4 4.8 %collective-permute-start.19 = (f32[104,128]{1,0:T(8,128)S(1)}, f32[104,128]{1,0:T(8,128)S(1)}, u32[]{:S(2)}, u32[]{:S(2)}) collective-permute-start(f32[104,128]{1,0:T(8,128)S(1)} %get-tuple-element.640), channel_id=1, source_target_pairs={{0,4},{4,0},{1,5},{5,1},{2,6},{6,2},{3,7},{7,3},{8,13},{12,8},{9,1... | collective-permute-start | bytes 159752 | tf_op jit(solution)/shard_map/ppermute | solution.py:388
  67.6 6.6 %collective-permute-start.23 = (f32[104,128]{1,0:T(8,128)S(1)}, f32[104,128]{1,0:T(8,128)S(1)}, u32[]{:S(2)}, u32[]{:S(2)}) collective-permute-start(f32[104,128]{1,0:T(8,128)S(1)} %get-tuple-element.668), channel_id=1, source_target_pairs={{0,5},{4,0},{1,4},{5,1},{2,7},{6,2},{3,6},{7,3},{8,13},{12,8},{9,1... | collective-permute-start | bytes 159752 | tf_op jit(solution)/shard_map/ppermute | solution.py:388
  80.5 7.0 %collective-permute-start.27 = (f32[104,128]{1,0:T(8,128)S(1)}, f32[104,128]{1,0:T(8,128)S(1)}, u32[]{:S(2)}, u32[]{:S(2)}) collective-permute-start(f32[104,128]{1,0:T(8,128)S(1)} %get-tuple-element.696), channel_id=1, source_target_pairs={{0,4},{4,0},{1,5},{5,1},{2,6},{6,2},{3,7},{7,3},{8,13},{12,8},{9,1... | collective-permute-start | bytes 159752 | tf_op jit(solution)/shard_map/ppermute | solution.py:388
  92.9 6.8 %collective-permute-start.31 = (f32[104,128]{1,0:T(8,128)S(1)}, f32[104,128]{1,0:T(8,128)S(1)}, u32[]{:S(2)}, u32[]{:S(2)}) collective-permute-start(f32[104,128]{1,0:T(8,128)S(1)} %get-tuple-element.724), channel_id=1, source_target_pairs={{0,4},{4,0},{1,5},{5,1},{2,6},{6,2},{3,7},{7,3},{8,12},{12,8},{9,1... | collective-permute-start | bytes 159752 | tf_op jit(solution)/shard_map/ppermute | solution.py:388
  106.2 4.7 %collective-permute-start.35 = (f32[104,128]{1,0:T(8,128)S(1)}, f32[104,128]{1,0:T(8,128)S(1)}, u32[]{:S(2)}, u32[]{:S(2)}) collective-permute-start(f32[104,128]{1,0:T(8,128)S(1)} %get-tuple-element.752), channel_id=1, source_target_pairs={{0,4},{4,0},{1,5},{5,1},{2,6},{6,2},{3,7},{7,3},{8,12},{12,9},{9,1... | collective-permute-start | bytes 159752 | tf_op jit(solution)/shard_map/ppermute | solution.py:388
  117.7 2.9 %collective-permute-start.39 = (f32[104,128]{1,0:T(8,128)S(1)}, f32[104,128]{1,0:T(8,128)S(1)}, u32[]{:S(2)}, u32[]{:S(2)}) collective-permute-start(f32[104,128]{1,0:T(8,128)S(1)} %get-tuple-element.780), channel_id=1, source_target_pairs={{0,4},{4,1},{1,5},{5,0},{2,6},{6,3},{3,7},{7,2},{8,12},{12,9},{9,1... | collective-permute-start | bytes 159752 | tf_op jit(solution)/shard_map/ppermute | solution.py:388
  122.7 2.9 %collective-permute-start.40 = (f32[104,128]{1,0:T(8,128)S(1)}, f32[104,128]{1,0:T(8,128)S(1)}, u32[]{:S(2)}, u32[]{:S(2)}) collective-permute-start(f32[104,128]{1,0:T(8,128)S(1)} %get-tuple-element.793), channel_id=1, source_target_pairs={{4,8},{8,5},{5,9},{9,4},{6,10},{10,7},{7,11},{11,6},{12,16},{16,13... | collective-permute-start | bytes 159752 | tf_op jit(solution)/shard_map/ppermute | solution.py:388
  126.6 4.9 %collective-permute-start.43 = (f32[104,128]{1,0:T(8,128)S(1)}, f32[104,128]{1,0:T(8,128)S(1)}, u32[]{:S(2)}, u32[]{:S(2)}) collective-permute-start(f32[104,128]{1,0:T(8,128)S(1)} %get-tuple-element.808), channel_id=1, source_target_pairs={{0,4},{4,0},{1,5},{5,1},{2,6},{6,2},{3,7},{7,3},{8,12},{12,9},{9,1... | collective-permute-start | bytes 159752 | tf_op jit(solution)/shard_map/ppermute | solution.py:388
  135.3 5.5 %collective-permute-start.47 = (f32[104,128]{1,0:T(8,128)S(1)}, f32[104,128]{1,0:T(8,128)S(1)}, u32[]{:S(2)}, u32[]{:S(2)}) collective-permute-start(f32[104,128]{1,0:T(8,128)S(1)} %get-tuple-element.836), channel_id=1, source_target_pairs={{0,4},{4,0},{1,5},{5,1},{2,6},{6,2},{3,7},{7,3},{8,12},{12,8},{9,1... | collective-permute-start | bytes 159752 | tf_op jit(solution)/shard_map/ppermute | solution.py:388
  144.1 5.8 %collective-permute-start.51 = (f32[104,128]{1,0:T(8,128)S(1)}, f32[104,128]{1,0:T(8,128)S(1)}, u32[]{:S(2)}, u32[]{:S(2)}) collective-permute-start(f32[104,128]{1,0:T(8,128)S(1)} %get-tuple-element.864), channel_id=1, source_target_pairs={{0,4},{4,0},{1,5},{5,1},{2,6},{6,2},{3,7},{7,3},{8,13},{12,8},{9,1... | collective-permute-start | bytes 159752 | tf_op jit(solution)/shard_map/ppermute | solution.py:388
  153.3 6.1 %collective-permute-start.55 = (f32[104,128]{1,0:T(8,128)S(1)}, f32[104,128]{1,0:T(8,128)S(1)}, u32[]{:S(2)}, u32[]{:S(2)}) collective-permute-start(f32[104,128]{1,0:T(8,128)S(1)} %get-tuple-element.892), channel_id=1, source_target_pairs={{0,5},{4,0},{1,4},{5,1},{2,7},{6,2},{3,6},{7,3},{8,13},{12,8},{9,1... | collective-permute-start | bytes 159752 | tf_op jit(solution)/shard_map/ppermute | solution.py:388
  164.6 6.1 %collective-permute-start.58 = (f32[104,128]{1,0:T(8,128)S(1)}, f32[104,128]{1,0:T(8,128)S(1)}, u32[]{:S(2)}, u32[]{:S(2)}) collective-permute-start(f32[104,128]{1,0:T(8,128)S(1)} %get-tuple-element.919), channel_id=1, source_target_pairs={{0,5},{4,0},{1,4},{5,1},{2,7},{6,2},{3,6},{7,3},{8,13},{12,8},{9,1... | collective-permute-start | bytes 159752 | tf_op jit(solution)/shard_map/ppermute | solution.py:388
  170.7 3.0 %collective-permute-done.58.refs_5_ = f32[104,128]{1,0:T(8,128)S(1)} collective-permute-done((f32[104,128]{1,0:T(8,128)S(1)}, f32[104,128]{1,0:T(8,128)S(1)}, u32[]{:S(2)}, u32[]{:S(2)}) %collective-permute-start.58) | collective-permute-done | bytes 53280 | tf_op jit(solution)/shard_map/ppermute | solution.py:388
  175.8 6.6 %collective-permute-start.60 = (f32[104,128]{1,0:T(8,128)S(1)}, f32[104,128]{1,0:T(8,128)S(1)}, u32[]{:S(2)}, u32[]{:S(2)}) collective-permute-start(f32[104,128]{1,0:T(8,128)S(1)} %get-tuple-element.937), channel_id=1, source_target_pairs={{0,5},{4,0},{1,4},{5,1},{2,7},{6,2},{3,6},{7,3},{8,13},{12,8},{9,1... | collective-permute-start | bytes 159752 | tf_op jit(solution)/shard_map/ppermute | solution.py:388
  182.5 3.3 %collective-permute-done.60.refs_5_ = f32[104,128]{1,0:T(8,128)S(1)} collective-permute-done((f32[104,128]{1,0:T(8,128)S(1)}, f32[104,128]{1,0:T(8,128)S(1)}, u32[]{:S(2)}, u32[]{:S(2)}) %collective-permute-start.60) | collective-permute-done | bytes 53280 | tf_op jit(solution)/shard_map/ppermute | solution.py:388
  187.9 4.6 %collective-permute-start.62 = (f32[104,128]{1,0:T(8,128)S(1)}, f32[104,128]{1,0:T(8,128)S(1)}, u32[]{:S(2)}, u32[]{:S(2)}) collective-permute-start(f32[104,128]{1,0:T(8,128)S(1)} %get-tuple-element.955), channel_id=1, source_target_pairs={{0,5},{4,0},{1,4},{5,1},{2,7},{6,2},{3,6},{7,3},{8,12},{12,8},{9,1... | collective-permute-start | bytes 159752 | tf_op jit(solution)/shard_map/ppermute | solution.py:388
  192.6 3.3 %collective-permute-done.62.refs_5_ = f32[104,128]{1,0:T(8,128)S(1)} collective-permute-done((f32[104,128]{1,0:T(8,128)S(1)}, f32[104,128]{1,0:T(8,128)S(1)}, u32[]{:S(2)}, u32[]{:S(2)}) %collective-permute-start.62) | collective-permute-done | bytes 53280 | tf_op jit(solution)/shard_map/ppermute | solution.py:388
  (176 shorter events, 85.4 us)
Async XLA Ops:
  4.4 5.5 %collective-permute-start = (f32[104,128]{1,0:T(8,128)S(1)}, f32[104,128]{1,0:T(8,128)S(1)}, u32[]{:S(2)}, u32[]{:S(2)}) collective-permute-start(f32[104,128]{1,0:T(8,128)S(1)} %get-tuple-element.495), channel_id=1, source_target_pairs={{0,4},{4,1},{1,5},{5,0},{2,6},{6,3},{3,7},{7,2},{8,12},{12,8},{9,1... | collective-permute-start | bytes 159752 | tf_op jit(solution)/shard_map/ppermute | solution.py:388
  13.4 6.1 %collective-permute-start.2 = (f32[104,128]{1,0:T(8,128)S(1)}, f32[104,128]{1,0:T(8,128)S(1)}, u32[]{:S(2)}, u32[]{:S(2)}) collective-permute-start(f32[104,128]{1,0:T(8,128)S(1)} %get-tuple-element.510), channel_id=1, source_target_pairs={{0,4},{4,1},{1,5},{5,0},{2,6},{6,3},{3,7},{7,2},{8,12},{12,9},{9,1... | collective-permute-start | bytes 159752 | tf_op jit(solution)/shard_map/ppermute | solution.py:388
  22.9 5.2 %collective-permute-start.4 = (f32[104,128]{1,0:T(8,128)S(1)}, f32[104,128]{1,0:T(8,128)S(1)}, u32[]{:S(2)}, u32[]{:S(2)}) collective-permute-start(f32[104,128]{1,0:T(8,128)S(1)} %get-tuple-element.529), channel_id=1, source_target_pairs={{0,4},{4,1},{1,5},{5,0},{2,6},{6,3},{3,7},{7,2},{8,12},{12,9},{9,1... | collective-permute-start | bytes 159752 | tf_op jit(solution)/shard_map/ppermute | solution.py:388
  30.7 6.7 %collective-permute-start.7 = (f32[104,128]{1,0:T(8,128)S(1)}, f32[104,128]{1,0:T(8,128)S(1)}, u32[]{:S(2)}, u32[]{:S(2)}) collective-permute-start(f32[104,128]{1,0:T(8,128)S(1)} %get-tuple-element.556), channel_id=1, source_target_pairs={{0,4},{4,1},{1,5},{5,0},{2,6},{6,3},{3,7},{7,2},{8,12},{12,9},{9,1... | collective-permute-start | bytes 159752 | tf_op jit(solution)/shard_map/ppermute | solution.py:388
  35.6 4.9 %collective-permute-start.10 = (f32[2,104,128]{2,1,0:T(8,128)S(1)}, f32[2,104,128]{2,1,0:T(8,128)S(1)}, u32[]{:S(2)}, u32[]{:S(2)}) collective-permute-start(f32[2,104,128]{2,1,0:T(8,128)S(1)} %get-tuple-element.574), channel_id=1, source_target_pairs={{1,2},{5,6},{9,10},{13,14},{17,18},{20,21},{22,23},{25,26},{2,1},{... | collective-permute-start | bytes 319496 | tf_op jit(solution)/shard_map/ppermute | solution.py:408
  40.7 6.9 %collective-permute-start.11 = (f32[104,128]{1,0:T(8,128)S(1)}, f32[104,128]{1,0:T(8,128)S(1)}, u32[]{:S(2)}, u32[]{:S(2)}) collective-permute-start(f32[104,128]{1,0:T(8,128)S(1)} %get-tuple-element.584), channel_id=1, source_target_pairs={{0,4},{4,0},{1,5},{5,1},{2,6},{6,2},{3,7},{7,3},{8,12},{12,9},{9,1... | collective-permute-start | bytes 159752 | tf_op jit(solution)/shard_map/ppermute | solution.py:388
  49.7 7.1 %collective-permute-start.15 = (f32[104,128]{1,0:T(8,128)S(1)}, f32[104,128]{1,0:T(8,128)S(1)}, u32[]{:S(2)}, u32[]{:S(2)}) collective-permute-start(f32[104,128]{1,0:T(8,128)S(1)} %get-tuple-element.612), channel_id=1, source_target_pairs={{0,4},{4,0},{1,5},{5,1},{2,6},{6,2},{3,7},{7,3},{8,12},{12,8},{9,1... | collective-permute-start | bytes 159752 | tf_op jit(solution)/shard_map/ppermute | solution.py:388
  59.4 7.0 %collective-permute-start.19 = (f32[104,128]{1,0:T(8,128)S(1)}, f32[104,128]{1,0:T(8,128)S(1)}, u32[]{:S(2)}, u32[]{:S(2)}) collective-permute-start(f32[104,128]{1,0:T(8,128)S(1)} %get-tuple-element.640), channel_id=1, source_target_pairs={{0,4},{4,0},{1,5},{5,1},{2,6},{6,2},{3,7},{7,3},{8,13},{12,8},{9,1... | collective-permute-start | bytes 159752 | tf_op jit(solution)/shard_map/ppermute | solution.py:388
  67.6 9.8 %collective-permute-start.23 = (f32[104,128]{1,0:T(8,128)S(1)}, f32[104,128]{1,0:T(8,128)S(1)}, u32[]{:S(2)}, u32[]{:S(2)}) collective-permute-start(f32[104,128]{1,0:T(8,128)S(1)} %get-tuple-element.668), channel_id=1, source_target_pairs={{0,5},{4,0},{1,4},{5,1},{2,7},{6,2},{3,6},{7,3},{8,13},{12,8},{9,1... | collective-permute-start | bytes 159752 | tf_op jit(solution)/shard_map/ppermute | solution.py:388
  74.2 4.8 %collective-permute-start.26 = (f32[2,104,128]{2,1,0:T(8,128)S(1)}, f32[2,104,128]{2,1,0:T(8,128)S(1)}, u32[]{:S(2)}, u32[]{:S(2)}) collective-permute-start(f32[2,104,128]{2,1,0:T(8,128)S(1)} %get-tuple-element.686), channel_id=1, source_target_pairs={{5,6},{8,9},{10,11},{13,14},{17,18},{20,21},{22,23},{24,25},{26,27... | collective-permute-start | bytes 319496 | tf_op jit(solution)/shard_map/ppermute | solution.py:408
  80.5 9.3 %collective-permute-start.27 = (f32[104,128]{1,0:T(8,128)S(1)}, f32[104,128]{1,0:T(8,128)S(1)}, u32[]{:S(2)}, u32[]{:S(2)}) collective-permute-start(f32[104,128]{1,0:T(8,128)S(1)} %get-tuple-element.696), channel_id=1, source_target_pairs={{0,4},{4,0},{1,5},{5,1},{2,6},{6,2},{3,7},{7,3},{8,13},{12,8},{9,1... | collective-permute-start | bytes 159752 | tf_op jit(solution)/shard_map/ppermute | solution.py:388
  92.9 9.0 %collective-permute-start.31 = (f32[104,128]{1,0:T(8,128)S(1)}, f32[104,128]{1,0:T(8,128)S(1)}, u32[]{:S(2)}, u32[]{:S(2)}) collective-permute-start(f32[104,128]{1,0:T(8,128)S(1)} %get-tuple-element.724), channel_id=1, source_target_pairs={{0,4},{4,0},{1,5},{5,1},{2,6},{6,2},{3,7},{7,3},{8,12},{12,8},{9,1... | collective-permute-start | bytes 159752 | tf_op jit(solution)/shard_map/ppermute | solution.py:388
  99.8 5.3 %collective-permute-start.34 = (f32[2,104,128]{2,1,0:T(8,128)S(1)}, f32[2,104,128]{2,1,0:T(8,128)S(1)}, u32[]{:S(2)}, u32[]{:S(2)}) collective-permute-start(f32[2,104,128]{2,1,0:T(8,128)S(1)} %get-tuple-element.742), channel_id=1, source_target_pairs={{1,2},{5,6},{8,9},{10,11},{13,14},{17,18},{20,21},{22,23},{25,26},... | collective-permute-start | bytes 319496 | tf_op jit(solution)/shard_map/ppermute | solution.py:408
  106.2 7.1 %collective-permute-start.35 = (f32[104,128]{1,0:T(8,128)S(1)}, f32[104,128]{1,0:T(8,128)S(1)}, u32[]{:S(2)}, u32[]{:S(2)}) collective-permute-start(f32[104,128]{1,0:T(8,128)S(1)} %get-tuple-element.752), channel_id=1, source_target_pairs={{0,4},{4,0},{1,5},{5,1},{2,6},{6,2},{3,7},{7,3},{8,12},{12,9},{9,1... | collective-permute-start | bytes 159752 | tf_op jit(solution)/shard_map/ppermute | solution.py:388
  110.8 5.0 %collective-permute-start.38 = (f32[2,104,128]{2,1,0:T(8,128)S(1)}, f32[2,104,128]{2,1,0:T(8,128)S(1)}, u32[]{:S(2)}, u32[]{:S(2)}) collective-permute-start(f32[2,104,128]{2,1,0:T(8,128)S(1)} %get-tuple-element.770), channel_id=1, source_target_pairs={{0,1},{2,3},{5,6},{9,10},{12,13},{14,15},{16,17},{18,19},{21,22},{... | collective-permute-start | bytes 319496 | tf_op jit(solution)/shard_map/ppermute | solution.py:408
  117.7 5.0 %collective-permute-start.39 = (f32[104,128]{1,0:T(8,128)S(1)}, f32[104,128]{1,0:T(8,128)S(1)}, u32[]{:S(2)}, u32[]{:S(2)}) collective-permute-start(f32[104,128]{1,0:T(8,128)S(1)} %get-tuple-element.780), channel_id=1, source_target_pairs={{0,4},{4,1},{1,5},{5,0},{2,6},{6,3},{3,7},{7,2},{8,12},{12,9},{9,1... | collective-permute-start | bytes 159752 | tf_op jit(solution)/shard_map/ppermute | solution.py:388
  120.7 5.6 %collective-permute-start.42 = (f32[2,104,128]{2,1,0:T(8,128)S(1)}, f32[2,104,128]{2,1,0:T(8,128)S(1)}, u32[]{:S(2)}, u32[]{:S(2)}) collective-permute-start(f32[2,104,128]{2,1,0:T(8,128)S(1)} %get-tuple-element.798), channel_id=1, source_target_pairs={{1,2},{4,5},{6,7},{8,9},{10,11},{13,14},{17,18},{20,21},{22,23},{2... | collective-permute-start | bytes 319496 | tf_op jit(solution)/shard_map/ppermute | solution.py:408
  126.6 7.4 %collective-permute-start.43 = (f32[104,128]{1,0:T(8,128)S(1)}, f32[104,128]{1,0:T(8,128)S(1)}, u32[]{:S(2)}, u32[]{:S(2)}) collective-permute-start(f32[104,128]{1,0:T(8,128)S(1)} %get-tuple-element.808), channel_id=1, source_target_pairs={{0,4},{4,0},{1,5},{5,1},{2,6},{6,2},{3,7},{7,3},{8,12},{12,9},{9,1... | collective-permute-start | bytes 159752 | tf_op jit(solution)/shard_map/ppermute | solution.py:388
  135.3 7.6 %collective-permute-start.47 = (f32[104,128]{1,0:T(8,128)S(1)}, f32[104,128]{1,0:T(8,128)S(1)}, u32[]{:S(2)}, u32[]{:S(2)}) collective-permute-start(f32[104,128]{1,0:T(8,128)S(1)} %get-tuple-element.836), channel_id=1, source_target_pairs={{0,4},{4,0},{1,5},{5,1},{2,6},{6,2},{3,7},{7,3},{8,12},{12,8},{9,1... | collective-permute-start | bytes 159752 | tf_op jit(solution)/shard_map/ppermute | solution.py:388
  144.1 7.9 %collective-permute-start.51 = (f32[104,128]{1,0:T(8,128)S(1)}, f32[104,128]{1,0:T(8,128)S(1)}, u32[]{:S(2)}, u32[]{:S(2)}) collective-permute-start(f32[104,128]{1,0:T(8,128)S(1)} %get-tuple-element.864), channel_id=1, source_target_pairs={{0,4},{4,0},{1,5},{5,1},{2,6},{6,2},{3,7},{7,3},{8,13},{12,8},{9,1... | collective-permute-start | bytes 159752 | tf_op jit(solution)/shard_map/ppermute | solution.py:388
  153.3 9.1 %collective-permute-start.55 = (f32[104,128]{1,0:T(8,128)S(1)}, f32[104,128]{1,0:T(8,128)S(1)}, u32[]{:S(2)}, u32[]{:S(2)}) collective-permute-start(f32[104,128]{1,0:T(8,128)S(1)} %get-tuple-element.892), channel_id=1, source_target_pairs={{0,5},{4,0},{1,4},{5,1},{2,7},{6,2},{3,6},{7,3},{8,13},{12,8},{9,1... | collective-permute-start | bytes 159752 | tf_op jit(solution)/shard_map/ppermute | solution.py:388
  164.6 9.1 %collective-permute-start.58 = (f32[104,128]{1,0:T(8,128)S(1)}, f32[104,128]{1,0:T(8,128)S(1)}, u32[]{:S(2)}, u32[]{:S(2)}) collective-permute-start(f32[104,128]{1,0:T(8,128)S(1)} %get-tuple-element.919), channel_id=1, source_target_pairs={{0,5},{4,0},{1,4},{5,1},{2,7},{6,2},{3,6},{7,3},{8,13},{12,8},{9,1... | collective-permute-start | bytes 159752 | tf_op jit(solution)/shard_map/ppermute | solution.py:388
  175.8 9.9 %collective-permute-start.60 = (f32[104,128]{1,0:T(8,128)S(1)}, f32[104,128]{1,0:T(8,128)S(1)}, u32[]{:S(2)}, u32[]{:S(2)}) collective-permute-start(f32[104,128]{1,0:T(8,128)S(1)} %get-tuple-element.937), channel_id=1, source_target_pairs={{0,5},{4,0},{1,4},{5,1},{2,7},{6,2},{3,6},{7,3},{8,13},{12,8},{9,1... | collective-permute-start | bytes 159752 | tf_op jit(solution)/shard_map/ppermute | solution.py:388
  187.9 7.9 %collective-permute-start.62 = (f32[104,128]{1,0:T(8,128)S(1)}, f32[104,128]{1,0:T(8,128)S(1)}, u32[]{:S(2)}, u32[]{:S(2)}) collective-permute-start(f32[104,128]{1,0:T(8,128)S(1)} %get-tuple-element.955), channel_id=1, source_target_pairs={{0,5},{4,0},{1,4},{5,1},{2,7},{6,2},{3,6},{7,3},{8,12},{12,8},{9,1... | collective-permute-start | bytes 159752 | tf_op jit(solution)/shard_map/ppermute | solution.py:388
  (39 other events, 81.1 us)

commit v9 on v8

--- a/solution.py
+++ b/solution.py
@@ -42,7 +42,7 @@
                 made = 2 * vector + half * count + rank
                 used = 2 * vector + (half + 1) * count + count - 1 - rank
                 if used == made + 1:
-                    sent[made][slab] = (1, (vector,))
+                    sent[made][slab] = (0, (vector,))
                     urgent[made][slab] = True
                     continue
                 left[1].append((used, made, vector))
@@ -178,8 +178,8 @@
 
         @pl.when(turns(task))
         def _():
-            take_lateral(base, vector, left, right, left_cols, right_cols, incoming[...], spare, 0)
-            take_lateral(base, vector, left, right, left_cols, right_cols, arrived[0], spare, 1)
+            take_lateral(base, vector, left, right, left_cols, right_cols, incoming[...], spare, 1)
+            take_lateral(base, vector, left, right, left_cols, right_cols, arrived[0], spare, 0)
 
     @pl.when(active)
     def _():
@@ -384,7 +384,9 @@
                 for p in range(parts):
                     pairs += [(device(a, p), device(b, p ^ forth)), (device(b, p), device(a, p ^ back))]
             alone = [s for s in range(count) if all(s not in two for two in swap)]
-            pairs += [(device(s, x), device(s, y)) for s in alone for a, b in even_pairs for x, y in ((a, b), (b, a))]
+            for s in alone:
+                chosen = odd_pairs if urgent[tick][s] else even_pairs
+                pairs += [(device(s, x), device(s, y)) for x, y in closed(chosen, range(parts))]
             incoming = lax.ppermute(value, ("sweep", "span"), pairs)
         came = [None if not tick or urgent[tick - 1][s] else sent[tick - 1][s] for s in range(count)]
         later = any(plan) and not at_once

time: 199 us -> 235 us (1.18)
  starting transfers between devices: 131 us -> 161 us
  waiting for transfers between devices: 32 us -> 37.9 us
    ppermute x26, starting transfers between devices: 24.1 us -> 39.5 us  [per_device(): lax.ppermute(cross[0], ('sweep', 'span'), closed(pairs, range(count * par...]
    ppermute x37, starting transfers between devices: 107 us -> 122 us  [per_device(): incoming = lax.ppermute(value, ('sweep', 'span'), pairs)]
    ppermute x37, waiting for transfers between devices: 31.3 us -> 35.9 us  [per_device(): incoming = lax.ppermute(value, ('sweep', 'span'), pairs)]
  transfers between devices with their start and end apart: 63 -> 63, of which waited for: 27 -> 30; matrix products, arithmetic and copies ran while one was open for 0% -> 0% of each run, Pallas kernels for 10% -> 9%
where the time goes in v9:
time: 235 us; the launch traced here: 234 us
  starting transfers between devices  161 us (69%)
  waiting for transfers between devices  37.9 us (16%)
  Pallas kernels  31.7 us (13%)
    ppermute x37, starting transfers between devices, per_device(): incoming = lax.ppermute(value, ('sweep', 'span'), pairs)  122 us
    ppermute x26, starting transfers between devices, per_device(): lax.ppermute(cross[0], ('sweep', 'span'), closed(pairs, range(count * par...  39.5 us
    ppermute x37, waiting for transfers between devices, per_device(): incoming = lax.ppermute(value, ('sweep', 'span'), pairs)  35.9 us
    pallas_call x66, Pallas kernels, call(): pl.pallas_call(body, out_shape=tuple((held(shape) for shape in [*(a.shape...  17.2 us
    pallas_call x4, Pallas kernels, later_call(): pl.pallas_call(functools.partial(later_kernel, face), out_shape=(held((si...  11.5 us
  transfers between devices with their start and end apart: 63, of which 30 were waited for; matrix products, arithmetic and copies ran while one was open for 0% of the time, Pallas kernels for 9%

profile of v9, /device:TPU:0, one launch (start us, length us, event | category | flops | bytes accessed | tf_op | source)
XLA Modules:
  0.0 233.7 jit_solution(3336403042583521602)
XLA Ops:
  13.4 6.3 %collective-permute-start.2 = (f32[104,128]{1,0:T(8,128)S(1)}, f32[104,128]{1,0:T(8,128)S(1)}, u32[]{:S(2)}, u32[]{:S(2)}) collective-permute-start(f32[104,128]{1,0:T(8,128)S(1)} %get-tuple-element.510), channel_id=1, source_target_pairs={{0,4},{4,1},{1,5},{5,0},{2,6},{6,3},{3,7},{7,2},{8,12},{12,9},{9,1... | collective-permute-start | bytes 159752 | tf_op jit(solution)/shard_map/ppermute | solution.py:390
  26.9 6.3 %collective-permute-start.4 = (f32[104,128]{1,0:T(8,128)S(1)}, f32[104,128]{1,0:T(8,128)S(1)}, u32[]{:S(2)}, u32[]{:S(2)}) collective-permute-start(f32[104,128]{1,0:T(8,128)S(1)} %get-tuple-element.529), channel_id=1, source_target_pairs={{0,4},{4,1},{1,5},{5,0},{2,6},{6,3},{3,7},{7,2},{8,12},{12,9},{9,1... | collective-permute-start | bytes 159752 | tf_op jit(solution)/shard_map/ppermute | solution.py:390
  38.4 5.0 %collective-permute-start.7 = (f32[104,128]{1,0:T(8,128)S(1)}, f32[104,128]{1,0:T(8,128)S(1)}, u32[]{:S(2)}, u32[]{:S(2)}) collective-permute-start(f32[104,128]{1,0:T(8,128)S(1)} %get-tuple-element.556), channel_id=1, source_target_pairs={{0,4},{4,1},{1,5},{5,0},{2,6},{6,3},{3,7},{7,2},{8,12},{12,9},{9,1... | collective-permute-start | bytes 159752 | tf_op jit(solution)/shard_map/ppermute | solution.py:390
  45.1 4.0 %collective-permute-start.8 = (f32[104,128]{1,0:T(8,128)S(1)}, f32[104,128]{1,0:T(8,128)S(1)}, u32[]{:S(2)}, u32[]{:S(2)}) collective-permute-start(f32[104,128]{1,0:T(8,128)S(1)} %get-tuple-element.569), channel_id=1, source_target_pairs={{4,8},{8,5},{5,9},{9,4},{6,10},{10,7},{7,11},{11,6},{12,16},{16,13... | collective-permute-start | bytes 159752 | tf_op jit(solution)/shard_map/ppermute | solution.py:390
  50.0 5.2 %collective-permute-start.11 = (f32[104,128]{1,0:T(8,128)S(1)}, f32[104,128]{1,0:T(8,128)S(1)}, u32[]{:S(2)}, u32[]{:S(2)}) collective-permute-start(f32[104,128]{1,0:T(8,128)S(1)} %get-tuple-element.584), channel_id=1, source_target_pairs={{0,4},{4,0},{1,5},{5,1},{2,6},{6,2},{3,7},{7,3},{8,12},{12,9},{9,1... | collective-permute-start | bytes 159752 | tf_op jit(solution)/shard_map/ppermute | solution.py:390
  61.3 4.9 %collective-permute-start.15 = (f32[104,128]{1,0:T(8,128)S(1)}, f32[104,128]{1,0:T(8,128)S(1)}, u32[]{:S(2)}, u32[]{:S(2)}) collective-permute-start(f32[104,128]{1,0:T(8,128)S(1)} %get-tuple-element.612), channel_id=1, source_target_pairs={{0,4},{4,0},{1,5},{5,1},{2,6},{6,2},{3,7},{7,3},{8,12},{12,8},{9,1... | collective-permute-start | bytes 159752 | tf_op jit(solution)/shard_map/ppermute | solution.py:390
  68.4 3.2 %collective-permute-start.16 = (f32[104,128]{1,0:T(8,128)S(1)}, f32[104,128]{1,0:T(8,128)S(1)}, u32[]{:S(2)}, u32[]{:S(2)}) collective-permute-start(f32[104,128]{1,0:T(8,128)S(1)} %get-tuple-element.625), channel_id=1, source_target_pairs={{4,8},{8,4},{5,9},{9,5},{6,10},{10,6},{7,11},{11,7},{12,17},{16,12... | collective-permute-start | bytes 159752 | tf_op jit(solution)/shard_map/ppermute | solution.py:390
  72.4 4.9 %collective-permute-start.19 = (f32[104,128]{1,0:T(8,128)S(1)}, f32[104,128]{1,0:T(8,128)S(1)}, u32[]{:S(2)}, u32[]{:S(2)}) collective-permute-start(f32[104,128]{1,0:T(8,128)S(1)} %get-tuple-element.640), channel_id=1, source_target_pairs={{0,4},{4,0},{1,5},{5,1},{2,6},{6,2},{3,7},{7,3},{8,13},{12,8},{9,1... | collective-permute-start | bytes 159752 | tf_op jit(solution)/shard_map/ppermute | solution.py:390
  82.6 6.8 %collective-permute-start.23 = (f32[104,128]{1,0:T(8,128)S(1)}, f32[104,128]{1,0:T(8,128)S(1)}, u32[]{:S(2)}, u32[]{:S(2)}) collective-permute-start(f32[104,128]{1,0:T(8,128)S(1)} %get-tuple-element.668), channel_id=1, source_target_pairs={{0,5},{4,0},{1,4},{5,1},{2,7},{6,2},{3,6},{7,3},{8,13},{12,8},{9,1... | collective-permute-start | bytes 159752 | tf_op jit(solution)/shard_map/ppermute | solution.py:390
  94.2 3.8 %collective-permute-start.25 = (f32[1,104,128]{2,1,0:T(8,128)S(1)}, f32[1,104,128]{2,1,0:T(8,128)S(1)}, u32[]{:S(2)}, u32[]{:S(2)}) collective-permute-start(f32[1,104,128]{2,1,0:T(8,128)S(1)} %get-tuple-element.682), channel_id=1, source_target_pairs={{0,1},{2,3},{4,5},{6,7},{1,0},{3,2},{5,4},{7,6},{8,8},{9,9},{10,10... | collective-permute-start | bytes 159752 | tf_op jit(solution)/shard_map/ppermute | solution.py:410
  99.7 3.5 %collective-permute-start.27 = (f32[104,128]{1,0:T(8,128)S(1)}, f32[104,128]{1,0:T(8,128)S(1)}, u32[]{:S(2)}, u32[]{:S(2)}) collective-permute-start(f32[104,128]{1,0:T(8,128)S(1)} %get-tuple-element.696), channel_id=1, source_target_pairs={{0,4},{4,0},{1,5},{5,1},{2,6},{6,2},{3,7},{7,3},{8,13},{12,8},{9,1... | collective-permute-start | bytes 159752 | tf_op jit(solution)/shard_map/ppermute | solution.py:390
  107.1 4.7 %collective-permute-start.29 = (f32[1,104,128]{2,1,0:T(8,128)S(1)}, f32[1,104,128]{2,1,0:T(8,128)S(1)}, u32[]{:S(2)}, u32[]{:S(2)}) collective-permute-start(f32[1,104,128]{2,1,0:T(8,128)S(1)} %get-tuple-element.710), channel_id=1, source_target_pairs={{0,1},{2,3},{4,5},{6,7},{1,0},{3,2},{5,4},{7,6},{8,8},{9,9},{10,10... | collective-permute-start | bytes 159752 | tf_op jit(solution)/shard_map/ppermute | solution.py:410
  120.0 4.9 %collective-permute-start.33 = (f32[1,104,128]{2,1,0:T(8,128)S(1)}, f32[1,104,128]{2,1,0:T(8,128)S(1)}, u32[]{:S(2)}, u32[]{:S(2)}) collective-permute-start(f32[1,104,128]{2,1,0:T(8,128)S(1)} %get-tuple-element.738), channel_id=1, source_target_pairs={{0,1},{2,3},{4,5},{6,7},{1,0},{3,2},{5,4},{7,6},{8,8},{9,9},{10,10... | collective-permute-start | bytes 159752 | tf_op jit(solution)/shard_map/ppermute | solution.py:410
  133.0 4.9 %collective-permute-start.37 = (f32[1,104,128]{2,1,0:T(8,128)S(1)}, f32[1,104,128]{2,1,0:T(8,128)S(1)}, u32[]{:S(2)}, u32[]{:S(2)}) collective-permute-start(f32[1,104,128]{2,1,0:T(8,128)S(1)} %get-tuple-element.766), channel_id=1, source_target_pairs={{0,1},{2,3},{4,5},{6,7},{1,0},{3,2},{5,4},{7,6},{8,8},{9,9},{10,10... | collective-permute-start | bytes 159752 | tf_op jit(solution)/shard_map/ppermute | solution.py:410
  147.0 5.4 %collective-permute-start.43 = (f32[104,128]{1,0:T(8,128)S(1)}, f32[104,128]{1,0:T(8,128)S(1)}, u32[]{:S(2)}, u32[]{:S(2)}) collective-permute-start(f32[104,128]{1,0:T(8,128)S(1)} %get-tuple-element.808), channel_id=1, source_target_pairs={{0,4},{4,0},{1,5},{5,1},{2,6},{6,2},{3,7},{7,3},{8,12},{12,9},{9,1... | collective-permute-start | bytes 159752 | tf_op jit(solution)/shard_map/ppermute | solution.py:390
  158.2 5.2 %collective-permute-start.47 = (f32[104,128]{1,0:T(8,128)S(1)}, f32[104,128]{1,0:T(8,128)S(1)}, u32[]{:S(2)}, u32[]{:S(2)}) collective-permute-start(f32[104,128]{1,0:T(8,128)S(1)} %get-tuple-element.836), channel_id=1, source_target_pairs={{0,4},{4,0},{1,5},{5,1},{2,6},{6,2},{3,7},{7,3},{8,12},{12,8},{9,1... | collective-permute-start | bytes 159752 | tf_op jit(solution)/shard_map/ppermute | solution.py:390
  168.7 5.8 %collective-permute-start.51 = (f32[104,128]{1,0:T(8,128)S(1)}, f32[104,128]{1,0:T(8,128)S(1)}, u32[]{:S(2)}, u32[]{:S(2)}) collective-permute-start(f32[104,128]{1,0:T(8,128)S(1)} %get-tuple-element.864), channel_id=1, source_target_pairs={{0,4},{4,0},{1,5},{5,1},{2,6},{6,2},{3,7},{7,3},{8,13},{12,8},{9,1... | collective-permute-start | bytes 159752 | tf_op jit(solution)/shard_map/ppermute | solution.py:390
  179.7 5.9 %collective-permute-start.55 = (f32[104,128]{1,0:T(8,128)S(1)}, f32[104,128]{1,0:T(8,128)S(1)}, u32[]{:S(2)}, u32[]{:S(2)}) collective-permute-start(f32[104,128]{1,0:T(8,128)S(1)} %get-tuple-element.892), channel_id=1, source_target_pairs={{0,5},{4,0},{1,4},{5,1},{2,7},{6,2},{3,6},{7,3},{8,13},{12,8},{9,1... | collective-permute-start | bytes 159752 | tf_op jit(solution)/shard_map/ppermute | solution.py:390
  190.8 9.7 %collective-permute-start.58 = (f32[104,128]{1,0:T(8,128)S(1)}, f32[104,128]{1,0:T(8,128)S(1)}, u32[]{:S(2)}, u32[]{:S(2)}) collective-permute-start(f32[104,128]{1,0:T(8,128)S(1)} %get-tuple-element.919), channel_id=1, source_target_pairs={{0,5},{4,0},{1,4},{5,1},{2,7},{6,2},{3,6},{7,3},{8,13},{12,8},{9,1... | collective-permute-start | bytes 159752 | tf_op jit(solution)/shard_map/ppermute | solution.py:390
  200.5 4.0 %collective-permute-done.58.refs_5_ = f32[104,128]{1,0:T(8,128)S(1)} collective-permute-done((f32[104,128]{1,0:T(8,128)S(1)}, f32[104,128]{1,0:T(8,128)S(1)}, u32[]{:S(2)}, u32[]{:S(2)}) %collective-permute-start.58) | collective-permute-done | bytes 53280 | tf_op jit(solution)/shard_map/ppermute | solution.py:390
  206.7 7.3 %collective-permute-start.60 = (f32[104,128]{1,0:T(8,128)S(1)}, f32[104,128]{1,0:T(8,128)S(1)}, u32[]{:S(2)}, u32[]{:S(2)}) collective-permute-start(f32[104,128]{1,0:T(8,128)S(1)} %get-tuple-element.937), channel_id=1, source_target_pairs={{0,5},{4,0},{1,4},{5,1},{2,7},{6,2},{3,6},{7,3},{8,13},{12,8},{9,1... | collective-permute-start | bytes 159752 | tf_op jit(solution)/shard_map/ppermute | solution.py:390
  214.0 4.0 %collective-permute-done.60.refs_5_ = f32[104,128]{1,0:T(8,128)S(1)} collective-permute-done((f32[104,128]{1,0:T(8,128)S(1)}, f32[104,128]{1,0:T(8,128)S(1)}, u32[]{:S(2)}, u32[]{:S(2)}) %collective-permute-start.60) | collective-permute-done | bytes 53280 | tf_op jit(solution)/shard_map/ppermute | solution.py:390
  220.2 7.2 %collective-permute-start.62 = (f32[104,128]{1,0:T(8,128)S(1)}, f32[104,128]{1,0:T(8,128)S(1)}, u32[]{:S(2)}, u32[]{:S(2)}) collective-permute-start(f32[104,128]{1,0:T(8,128)S(1)} %get-tuple-element.955), channel_id=1, source_target_pairs={{0,5},{4,0},{1,4},{5,1},{2,7},{6,2},{3,6},{7,3},{8,12},{12,8},{9,1... | collective-permute-start | bytes 159752 | tf_op jit(solution)/shard_map/ppermute | solution.py:390
  227.4 4.0 %collective-permute-done.62.refs_5_ = f32[104,128]{1,0:T(8,128)S(1)} collective-permute-done((f32[104,128]{1,0:T(8,128)S(1)}, f32[104,128]{1,0:T(8,128)S(1)}, u32[]{:S(2)}, u32[]{:S(2)}) %collective-permute-start.62) | collective-permute-done | bytes 53280 | tf_op jit(solution)/shard_map/ppermute | solution.py:390
  (176 shorter events, 105.9 us)
Async XLA Ops:
  13.4 9.9 %collective-permute-start.2 = (f32[104,128]{1,0:T(8,128)S(1)}, f32[104,128]{1,0:T(8,128)S(1)}, u32[]{:S(2)}, u32[]{:S(2)}) collective-permute-start(f32[104,128]{1,0:T(8,128)S(1)} %get-tuple-element.510), channel_id=1, source_target_pairs={{0,4},{4,1},{1,5},{5,0},{2,6},{6,3},{3,7},{7,2},{8,12},{12,9},{9,1... | collective-permute-start | bytes 159752 | tf_op jit(solution)/shard_map/ppermute | solution.py:390
  26.9 9.9 %collective-permute-start.4 = (f32[104,128]{1,0:T(8,128)S(1)}, f32[104,128]{1,0:T(8,128)S(1)}, u32[]{:S(2)}, u32[]{:S(2)}) collective-permute-start(f32[104,128]{1,0:T(8,128)S(1)} %get-tuple-element.529), channel_id=1, source_target_pairs={{0,4},{4,1},{1,5},{5,0},{2,6},{6,3},{3,7},{7,2},{8,12},{12,9},{9,1... | collective-permute-start | bytes 159752 | tf_op jit(solution)/shard_map/ppermute | solution.py:390
  38.4 6.7 %collective-permute-start.7 = (f32[104,128]{1,0:T(8,128)S(1)}, f32[104,128]{1,0:T(8,128)S(1)}, u32[]{:S(2)}, u32[]{:S(2)}) collective-permute-start(f32[104,128]{1,0:T(8,128)S(1)} %get-tuple-element.556), channel_id=1, source_target_pairs={{0,4},{4,1},{1,5},{5,0},{2,6},{6,3},{3,7},{7,2},{8,12},{12,9},{9,1... | collective-permute-start | bytes 159752 | tf_op jit(solution)/shard_map/ppermute | solution.py:390
  43.4 6.5 %collective-permute-start.10 = (f32[2,104,128]{2,1,0:T(8,128)S(1)}, f32[2,104,128]{2,1,0:T(8,128)S(1)}, u32[]{:S(2)}, u32[]{:S(2)}) collective-permute-start(f32[2,104,128]{2,1,0:T(8,128)S(1)} %get-tuple-element.574), channel_id=1, source_target_pairs={{1,2},{5,6},{9,10},{13,14},{17,18},{20,21},{22,23},{25,26},{2,1},{... | collective-permute-start | bytes 319496 | tf_op jit(solution)/shard_map/ppermute | solution.py:410
  50.0 7.3 %collective-permute-start.11 = (f32[104,128]{1,0:T(8,128)S(1)}, f32[104,128]{1,0:T(8,128)S(1)}, u32[]{:S(2)}, u32[]{:S(2)}) collective-permute-start(f32[104,128]{1,0:T(8,128)S(1)} %get-tuple-element.584), channel_id=1, source_target_pairs={{0,4},{4,0},{1,5},{5,1},{2,6},{6,2},{3,7},{7,3},{8,12},{12,9},{9,1... | collective-permute-start | bytes 159752 | tf_op jit(solution)/shard_map/ppermute | solution.py:390
  61.3 7.1 %collective-permute-start.15 = (f32[104,128]{1,0:T(8,128)S(1)}, f32[104,128]{1,0:T(8,128)S(1)}, u32[]{:S(2)}, u32[]{:S(2)}) collective-permute-start(f32[104,128]{1,0:T(8,128)S(1)} %get-tuple-element.612), channel_id=1, source_target_pairs={{0,4},{4,0},{1,5},{5,1},{2,6},{6,2},{3,7},{7,3},{8,12},{12,8},{9,1... | collective-permute-start | bytes 159752 | tf_op jit(solution)/shard_map/ppermute | solution.py:390
  66.3 6.0 %collective-permute-start.18 = (f32[2,104,128]{2,1,0:T(8,128)S(1)}, f32[2,104,128]{2,1,0:T(8,128)S(1)}, u32[]{:S(2)}, u32[]{:S(2)}) collective-permute-start(f32[2,104,128]{2,1,0:T(8,128)S(1)} %get-tuple-element.630), channel_id=1, source_target_pairs={{1,2},{5,6},{9,10},{13,14},{17,18},{20,21},{22,23},{25,26},{29,30}... | collective-permute-start | bytes 319496 | tf_op jit(solution)/shard_map/ppermute | solution.py:410
  72.4 7.0 %collective-permute-start.19 = (f32[104,128]{1,0:T(8,128)S(1)}, f32[104,128]{1,0:T(8,128)S(1)}, u32[]{:S(2)}, u32[]{:S(2)}) collective-permute-start(f32[104,128]{1,0:T(8,128)S(1)} %get-tuple-element.640), channel_id=1, source_target_pairs={{0,4},{4,0},{1,5},{5,1},{2,6},{6,2},{3,7},{7,3},{8,13},{12,8},{9,1... | collective-permute-start | bytes 159752 | tf_op jit(solution)/shard_map/ppermute | solution.py:390
  82.6 10.1 %collective-permute-start.23 = (f32[104,128]{1,0:T(8,128)S(1)}, f32[104,128]{1,0:T(8,128)S(1)}, u32[]{:S(2)}, u32[]{:S(2)}) collective-permute-start(f32[104,128]{1,0:T(8,128)S(1)} %get-tuple-element.668), channel_id=1, source_target_pairs={{0,5},{4,0},{1,4},{5,1},{2,7},{6,2},{3,6},{7,3},{8,13},{12,8},{9,1... | collective-permute-start | bytes 159752 | tf_op jit(solution)/shard_map/ppermute | solution.py:390
  89.3 8.6 %collective-permute-start.26 = (f32[2,104,128]{2,1,0:T(8,128)S(1)}, f32[2,104,128]{2,1,0:T(8,128)S(1)}, u32[]{:S(2)}, u32[]{:S(2)}) collective-permute-start(f32[2,104,128]{2,1,0:T(8,128)S(1)} %get-tuple-element.686), channel_id=1, source_target_pairs={{5,6},{8,9},{10,11},{13,14},{17,18},{20,21},{22,23},{24,25},{26,27... | collective-permute-start | bytes 319496 | tf_op jit(solution)/shard_map/ppermute | solution.py:410
  103.2 8.7 %collective-permute-start.30 = (f32[2,104,128]{2,1,0:T(8,128)S(1)}, f32[2,104,128]{2,1,0:T(8,128)S(1)}, u32[]{:S(2)}, u32[]{:S(2)}) collective-permute-start(f32[2,104,128]{2,1,0:T(8,128)S(1)} %get-tuple-element.714), channel_id=1, source_target_pairs={{0,1},{2,3},{5,6},{9,10},{12,13},{14,15},{16,17},{18,19},{21,22},{... | collective-permute-start | bytes 319496 | tf_op jit(solution)/shard_map/ppermute | solution.py:410
  106.4 5.9 %collective-permute-start.28 = (f32[104,128]{1,0:T(8,128)S(1)}, f32[104,128]{1,0:T(8,128)S(1)}, u32[]{:S(2)}, u32[]{:S(2)}) collective-permute-start(f32[104,128]{1,0:T(8,128)S(1)} %get-tuple-element.709), channel_id=1, source_target_pairs={{4,8},{8,4},{5,9},{9,5},{6,10},{10,6},{7,11},{11,7},{12,17},{16,12... | collective-permute-start | bytes 159752 | tf_op jit(solution)/shard_map/ppermute | solution.py:390
  116.3 8.6 %collective-permute-start.34 = (f32[2,104,128]{2,1,0:T(8,128)S(1)}, f32[2,104,128]{2,1,0:T(8,128)S(1)}, u32[]{:S(2)}, u32[]{:S(2)}) collective-permute-start(f32[2,104,128]{2,1,0:T(8,128)S(1)} %get-tuple-element.742), channel_id=1, source_target_pairs={{1,2},{5,6},{8,9},{10,11},{13,14},{17,18},{20,21},{22,23},{25,26},... | collective-permute-start | bytes 319496 | tf_op jit(solution)/shard_map/ppermute | solution.py:410
  129.1 8.7 %collective-permute-start.38 = (f32[2,104,128]{2,1,0:T(8,128)S(1)}, f32[2,104,128]{2,1,0:T(8,128)S(1)}, u32[]{:S(2)}, u32[]{:S(2)}) collective-permute-start(f32[2,104,128]{2,1,0:T(8,128)S(1)} %get-tuple-element.770), channel_id=1, source_target_pairs={{0,1},{2,3},{5,6},{9,10},{12,13},{14,15},{16,17},{18,19},{21,22},{... | collective-permute-start | bytes 319496 | tf_op jit(solution)/shard_map/ppermute | solution.py:410
  132.3 6.5 %collective-permute-start.36 = (f32[104,128]{1,0:T(8,128)S(1)}, f32[104,128]{1,0:T(8,128)S(1)}, u32[]{:S(2)}, u32[]{:S(2)}) collective-permute-start(f32[104,128]{1,0:T(8,128)S(1)} %get-tuple-element.765), channel_id=1, source_target_pairs={{4,8},{8,5},{5,9},{9,4},{6,10},{10,7},{7,11},{11,6},{12,16},{16,13... | collective-permute-start | bytes 159752 | tf_op jit(solution)/shard_map/ppermute | solution.py:390
  133.0 5.9 %collective-permute-start.37 = (f32[1,104,128]{2,1,0:T(8,128)S(1)}, f32[1,104,128]{2,1,0:T(8,128)S(1)}, u32[]{:S(2)}, u32[]{:S(2)}) collective-permute-start(f32[1,104,128]{2,1,0:T(8,128)S(1)} %get-tuple-element.766), channel_id=1, source_target_pairs={{0,1},{2,3},{4,5},{6,7},{1,0},{3,2},{5,4},{7,6},{8,8},{9,9},{10,10... | collective-permute-start | bytes 159752 | tf_op jit(solution)/shard_map/ppermute | solution.py:410
  140.8 6.0 %collective-permute-start.42 = (f32[2,104,128]{2,1,0:T(8,128)S(1)}, f32[2,104,128]{2,1,0:T(8,128)S(1)}, u32[]{:S(2)}, u32[]{:S(2)}) collective-permute-start(f32[2,104,128]{2,1,0:T(8,128)S(1)} %get-tuple-element.798), channel_id=1, source_target_pairs={{1,2},{4,5},{6,7},{8,9},{10,11},{13,14},{17,18},{20,21},{22,23},{2... | collective-permute-start | bytes 319496 | tf_op jit(solution)/shard_map/ppermute | solution.py:410
  147.0 7.5 %collective-permute-start.43 = (f32[104,128]{1,0:T(8,128)S(1)}, f32[104,128]{1,0:T(8,128)S(1)}, u32[]{:S(2)}, u32[]{:S(2)}) collective-permute-start(f32[104,128]{1,0:T(8,128)S(1)} %get-tuple-element.808), channel_id=1, source_target_pairs={{0,4},{4,0},{1,5},{5,1},{2,6},{6,2},{3,7},{7,3},{8,12},{12,9},{9,1... | collective-permute-start | bytes 159752 | tf_op jit(solution)/shard_map/ppermute | solution.py:390
  158.2 7.3 %collective-permute-start.47 = (f32[104,128]{1,0:T(8,128)S(1)}, f32[104,128]{1,0:T(8,128)S(1)}, u32[]{:S(2)}, u32[]{:S(2)}) collective-permute-start(f32[104,128]{1,0:T(8,128)S(1)} %get-tuple-element.836), channel_id=1, source_target_pairs={{0,4},{4,0},{1,5},{5,1},{2,6},{6,2},{3,7},{7,3},{8,12},{12,8},{9,1... | collective-permute-start | bytes 159752 | tf_op jit(solution)/shard_map/ppermute | solution.py:390
  168.7 7.9 %collective-permute-start.51 = (f32[104,128]{1,0:T(8,128)S(1)}, f32[104,128]{1,0:T(8,128)S(1)}, u32[]{:S(2)}, u32[]{:S(2)}) collective-permute-start(f32[104,128]{1,0:T(8,128)S(1)} %get-tuple-element.864), channel_id=1, source_target_pairs={{0,4},{4,0},{1,5},{5,1},{2,6},{6,2},{3,7},{7,3},{8,13},{12,8},{9,1... | collective-permute-start | bytes 159752 | tf_op jit(solution)/shard_map/ppermute | solution.py:390
  179.7 8.9 %collective-permute-start.55 = (f32[104,128]{1,0:T(8,128)S(1)}, f32[104,128]{1,0:T(8,128)S(1)}, u32[]{:S(2)}, u32[]{:S(2)}) collective-permute-start(f32[104,128]{1,0:T(8,128)S(1)} %get-tuple-element.892), channel_id=1, source_target_pairs={{0,5},{4,0},{1,4},{5,1},{2,7},{6,2},{3,6},{7,3},{8,13},{12,8},{9,1... | collective-permute-start | bytes 159752 | tf_op jit(solution)/shard_map/ppermute | solution.py:390
  190.8 13.8 %collective-permute-start.58 = (f32[104,128]{1,0:T(8,128)S(1)}, f32[104,128]{1,0:T(8,128)S(1)}, u32[]{:S(2)}, u32[]{:S(2)}) collective-permute-start(f32[104,128]{1,0:T(8,128)S(1)} %get-tuple-element.919), channel_id=1, source_target_pairs={{0,5},{4,0},{1,4},{5,1},{2,7},{6,2},{3,6},{7,3},{8,13},{12,8},{9,1... | collective-permute-start | bytes 159752 | tf_op jit(solution)/shard_map/ppermute | solution.py:390
  206.7 11.3 %collective-permute-start.60 = (f32[104,128]{1,0:T(8,128)S(1)}, f32[104,128]{1,0:T(8,128)S(1)}, u32[]{:S(2)}, u32[]{:S(2)}) collective-permute-start(f32[104,128]{1,0:T(8,128)S(1)} %get-tuple-element.937), channel_id=1, source_target_pairs={{0,5},{4,0},{1,4},{5,1},{2,7},{6,2},{3,6},{7,3},{8,13},{12,8},{9,1... | collective-permute-start | bytes 159752 | tf_op jit(solution)/shard_map/ppermute | solution.py:390
  220.2 11.3 %collective-permute-start.62 = (f32[104,128]{1,0:T(8,128)S(1)}, f32[104,128]{1,0:T(8,128)S(1)}, u32[]{:S(2)}, u32[]{:S(2)}) collective-permute-start(f32[104,128]{1,0:T(8,128)S(1)} %get-tuple-element.955), channel_id=1, source_target_pairs={{0,5},{4,0},{1,4},{5,1},{2,7},{6,2},{3,6},{7,3},{8,12},{12,8},{9,1... | collective-permute-start | bytes 159752 | tf_op jit(solution)/shard_map/ppermute | solution.py:390
  (39 other events, 132.8 us)

commit v10 on v9

--- a/solution.py
+++ b/solution.py
@@ -387,7 +387,7 @@
             for s in alone:
                 chosen = odd_pairs if urgent[tick][s] else even_pairs
                 pairs += [(device(s, x), device(s, y)) for x, y in closed(chosen, range(parts))]
-            incoming = lax.ppermute(value, ("sweep", "span"), pairs)
+            incoming = lax.ppermute(value, ("sweep", "span"), sorted(pairs))
         came = [None if not tick or urgent[tick - 1][s] else sent[tick - 1][s] for s in range(count)]
         later = any(plan) and not at_once
         if any(came) or later:
@@ -407,7 +407,7 @@
                 if plan[s] is not None
                 for a, b in (odd_pairs if plan[s][0] else even_pairs)
             ]
-            arrived = lax.ppermute(cross[0], ("sweep", "span"), closed(pairs, range(count * parts)))
+            arrived = lax.ppermute(cross[0], ("sweep", "span"), sorted(closed(pairs, range(count * parts))))
         if tick < len(late_blocks):
             mats[1 + tick], base = later_call(*late_blocks[tick], base)
     return out[None, None]

time: 235 us -> 235 us (level)
  no operation moved by 1% of the time
where the time goes in v10:
time: 235 us; the launch traced here: 234 us
  starting transfers between devices  161 us (69%)
  waiting for transfers between devices  37.9 us (16%)
  Pallas kernels  31.7 us (13%)
    ppermute x37, starting transfers between devices, per_device(): incoming = lax.ppermute(value, ('sweep', 'span'), sorted(pairs))  122 us
    ppermute x26, starting transfers between devices, per_device(): lax.ppermute(cross[0], ('sweep', 'span'), sorted(closed(pairs, range(coun...  39.5 us
    ppermute x37, waiting for transfers between devices, per_device(): incoming = lax.ppermute(value, ('sweep', 'span'), sorted(pairs))  35.9 us
    pallas_call x66, Pallas kernels, call(): pl.pallas_call(body, out_shape=tuple((held(shape) for shape in [*(a.shape...  17.2 us
    pallas_call x4, Pallas kernels, later_call(): pl.pallas_call(functools.partial(later_kernel, face), out_shape=(held((si...  11.5 us
  transfers between devices with their start and end apart: 63, of which 30 were waited for; matrix products, arithmetic and copies ran while one was open for 0% of the time, Pallas kernels for 9%

profile of v10, /device:TPU:0, one launch (start us, length us, event | category | flops | bytes accessed | tf_op | source)
XLA Modules:
  0.0 233.7 jit_solution(3336403042583521602)
XLA Ops:
  13.4 6.3 %collective-permute-start.2 = (f32[104,128]{1,0:T(8,128)S(1)}, f32[104,128]{1,0:T(8,128)S(1)}, u32[]{:S(2)}, u32[]{:S(2)}) collective-permute-start(f32[104,128]{1,0:T(8,128)S(1)} %get-tuple-element.510), channel_id=1, source_target_pairs={{0,4},{1,5},{2,6},{3,7},{4,1},{5,0},{6,3},{7,2},{8,12},{9,13},{10,... | collective-permute-start | bytes 159752 | tf_op jit(solution)/shard_map/ppermute | solution.py:390
  26.9 6.3 %collective-permute-start.4 = (f32[104,128]{1,0:T(8,128)S(1)}, f32[104,128]{1,0:T(8,128)S(1)}, u32[]{:S(2)}, u32[]{:S(2)}) collective-permute-start(f32[104,128]{1,0:T(8,128)S(1)} %get-tuple-element.529), channel_id=1, source_target_pairs={{0,4},{1,5},{2,6},{3,7},{4,1},{5,0},{6,3},{7,2},{8,12},{9,13},{10,... | collective-permute-start | bytes 159752 | tf_op jit(solution)/shard_map/ppermute | solution.py:390
  38.4 5.0 %collective-permute-start.7 = (f32[104,128]{1,0:T(8,128)S(1)}, f32[104,128]{1,0:T(8,128)S(1)}, u32[]{:S(2)}, u32[]{:S(2)}) collective-permute-start(f32[104,128]{1,0:T(8,128)S(1)} %get-tuple-element.556), channel_id=1, source_target_pairs={{0,4},{1,5},{2,6},{3,7},{4,1},{5,0},{6,3},{7,2},{8,12},{9,13},{10,... | collective-permute-start | bytes 159752 | tf_op jit(solution)/shard_map/ppermute | solution.py:390
  45.1 4.0 %collective-permute-start.8 = (f32[104,128]{1,0:T(8,128)S(1)}, f32[104,128]{1,0:T(8,128)S(1)}, u32[]{:S(2)}, u32[]{:S(2)}) collective-permute-start(f32[104,128]{1,0:T(8,128)S(1)} %get-tuple-element.569), channel_id=1, source_target_pairs={{0,1},{1,0},{2,3},{3,2},{4,8},{5,9},{6,10},{7,11},{8,5},{9,4},{10,... | collective-permute-start | bytes 159752 | tf_op jit(solution)/shard_map/ppermute | solution.py:390
  50.0 5.2 %collective-permute-start.11 = (f32[104,128]{1,0:T(8,128)S(1)}, f32[104,128]{1,0:T(8,128)S(1)}, u32[]{:S(2)}, u32[]{:S(2)}) collective-permute-start(f32[104,128]{1,0:T(8,128)S(1)} %get-tuple-element.584), channel_id=1, source_target_pairs={{0,4},{1,5},{2,6},{3,7},{4,0},{5,1},{6,2},{7,3},{8,12},{9,13},{10,... | collective-permute-start | bytes 159752 | tf_op jit(solution)/shard_map/ppermute | solution.py:390
  61.3 4.9 %collective-permute-start.15 = (f32[104,128]{1,0:T(8,128)S(1)}, f32[104,128]{1,0:T(8,128)S(1)}, u32[]{:S(2)}, u32[]{:S(2)}) collective-permute-start(f32[104,128]{1,0:T(8,128)S(1)} %get-tuple-element.612), channel_id=1, source_target_pairs={{0,4},{1,5},{2,6},{3,7},{4,0},{5,1},{6,2},{7,3},{8,12},{9,13},{10,... | collective-permute-start | bytes 159752 | tf_op jit(solution)/shard_map/ppermute | solution.py:390
  68.4 3.2 %collective-permute-start.16 = (f32[104,128]{1,0:T(8,128)S(1)}, f32[104,128]{1,0:T(8,128)S(1)}, u32[]{:S(2)}, u32[]{:S(2)}) collective-permute-start(f32[104,128]{1,0:T(8,128)S(1)} %get-tuple-element.625), channel_id=1, source_target_pairs={{0,1},{1,0},{2,3},{3,2},{4,8},{5,9},{6,10},{7,11},{8,4},{9,5},{10,... | collective-permute-start | bytes 159752 | tf_op jit(solution)/shard_map/ppermute | solution.py:390
  72.4 4.9 %collective-permute-start.19 = (f32[104,128]{1,0:T(8,128)S(1)}, f32[104,128]{1,0:T(8,128)S(1)}, u32[]{:S(2)}, u32[]{:S(2)}) collective-permute-start(f32[104,128]{1,0:T(8,128)S(1)} %get-tuple-element.640), channel_id=1, source_target_pairs={{0,4},{1,5},{2,6},{3,7},{4,0},{5,1},{6,2},{7,3},{8,13},{9,12},{10,... | collective-permute-start | bytes 159752 | tf_op jit(solution)/shard_map/ppermute | solution.py:390
  82.6 6.8 %collective-permute-start.23 = (f32[104,128]{1,0:T(8,128)S(1)}, f32[104,128]{1,0:T(8,128)S(1)}, u32[]{:S(2)}, u32[]{:S(2)}) collective-permute-start(f32[104,128]{1,0:T(8,128)S(1)} %get-tuple-element.668), channel_id=1, source_target_pairs={{0,5},{1,4},{2,7},{3,6},{4,0},{5,1},{6,2},{7,3},{8,13},{9,12},{10,... | collective-permute-start | bytes 159752 | tf_op jit(solution)/shard_map/ppermute | solution.py:390
  94.2 3.8 %collective-permute-start.25 = (f32[1,104,128]{2,1,0:T(8,128)S(1)}, f32[1,104,128]{2,1,0:T(8,128)S(1)}, u32[]{:S(2)}, u32[]{:S(2)}) collective-permute-start(f32[1,104,128]{2,1,0:T(8,128)S(1)} %get-tuple-element.682), channel_id=1, source_target_pairs={{0,1},{1,0},{2,3},{3,2},{4,5},{5,4},{6,7},{7,6},{8,8},{9,9},{10,10... | collective-permute-start | bytes 159752 | tf_op jit(solution)/shard_map/ppermute | solution.py:410
  99.7 3.5 %collective-permute-start.27 = (f32[104,128]{1,0:T(8,128)S(1)}, f32[104,128]{1,0:T(8,128)S(1)}, u32[]{:S(2)}, u32[]{:S(2)}) collective-permute-start(f32[104,128]{1,0:T(8,128)S(1)} %get-tuple-element.696), channel_id=1, source_target_pairs={{0,4},{1,5},{2,6},{3,7},{4,0},{5,1},{6,2},{7,3},{8,13},{9,12},{10,... | collective-permute-start | bytes 159752 | tf_op jit(solution)/shard_map/ppermute | solution.py:390
  107.1 4.7 %collective-permute-start.29 = (f32[1,104,128]{2,1,0:T(8,128)S(1)}, f32[1,104,128]{2,1,0:T(8,128)S(1)}, u32[]{:S(2)}, u32[]{:S(2)}) collective-permute-start(f32[1,104,128]{2,1,0:T(8,128)S(1)} %get-tuple-element.710), channel_id=1, source_target_pairs={{0,1},{1,0},{2,3},{3,2},{4,5},{5,4},{6,7},{7,6},{8,8},{9,9},{10,10... | collective-permute-start | bytes 159752 | tf_op jit(solution)/shard_map/ppermute | solution.py:410
  120.0 4.9 %collective-permute-start.33 = (f32[1,104,128]{2,1,0:T(8,128)S(1)}, f32[1,104,128]{2,1,0:T(8,128)S(1)}, u32[]{:S(2)}, u32[]{:S(2)}) collective-permute-start(f32[1,104,128]{2,1,0:T(8,128)S(1)} %get-tuple-element.738), channel_id=1, source_target_pairs={{0,1},{1,0},{2,3},{3,2},{4,5},{5,4},{6,7},{7,6},{8,8},{9,9},{10,10... | collective-permute-start | bytes 159752 | tf_op jit(solution)/shard_map/ppermute | solution.py:410
  133.0 4.9 %collective-permute-start.37 = (f32[1,104,128]{2,1,0:T(8,128)S(1)}, f32[1,104,128]{2,1,0:T(8,128)S(1)}, u32[]{:S(2)}, u32[]{:S(2)}) collective-permute-start(f32[1,104,128]{2,1,0:T(8,128)S(1)} %get-tuple-element.766), channel_id=1, source_target_pairs={{0,1},{1,0},{2,3},{3,2},{4,5},{5,4},{6,7},{7,6},{8,8},{9,9},{10,10... | collective-permute-start | bytes 159752 | tf_op jit(solution)/shard_map/ppermute | solution.py:410
  147.0 5.4 %collective-permute-start.43 = (f32[104,128]{1,0:T(8,128)S(1)}, f32[104,128]{1,0:T(8,128)S(1)}, u32[]{:S(2)}, u32[]{:S(2)}) collective-permute-start(f32[104,128]{1,0:T(8,128)S(1)} %get-tuple-element.808), channel_id=1, source_target_pairs={{0,4},{1,5},{2,6},{3,7},{4,0},{5,1},{6,2},{7,3},{8,12},{9,13},{10,... | collective-permute-start | bytes 159752 | tf_op jit(solution)/shard_map/ppermute | solution.py:390
  158.2 5.2 %collective-permute-start.47 = (f32[104,128]{1,0:T(8,128)S(1)}, f32[104,128]{1,0:T(8,128)S(1)}, u32[]{:S(2)}, u32[]{:S(2)}) collective-permute-start(f32[104,128]{1,0:T(8,128)S(1)} %get-tuple-element.836), channel_id=1, source_target_pairs={{0,4},{1,5},{2,6},{3,7},{4,0},{5,1},{6,2},{7,3},{8,12},{9,13},{10,... | collective-permute-start | bytes 159752 | tf_op jit(solution)/shard_map/ppermute | solution.py:390
  168.7 5.8 %collective-permute-start.51 = (f32[104,128]{1,0:T(8,128)S(1)}, f32[104,128]{1,0:T(8,128)S(1)}, u32[]{:S(2)}, u32[]{:S(2)}) collective-permute-start(f32[104,128]{1,0:T(8,128)S(1)} %get-tuple-element.864), channel_id=1, source_target_pairs={{0,4},{1,5},{2,6},{3,7},{4,0},{5,1},{6,2},{7,3},{8,13},{9,12},{10,... | collective-permute-start | bytes 159752 | tf_op jit(solution)/shard_map/ppermute | solution.py:390
  179.7 5.9 %collective-permute-start.55 = (f32[104,128]{1,0:T(8,128)S(1)}, f32[104,128]{1,0:T(8,128)S(1)}, u32[]{:S(2)}, u32[]{:S(2)}) collective-permute-start(f32[104,128]{1,0:T(8,128)S(1)} %get-tuple-element.892), channel_id=1, source_target_pairs={{0,5},{1,4},{2,7},{3,6},{4,0},{5,1},{6,2},{7,3},{8,13},{9,12},{10,... | collective-permute-start | bytes 159752 | tf_op jit(solution)/shard_map/ppermute | solution.py:390
  190.8 9.7 %collective-permute-start.58 = (f32[104,128]{1,0:T(8,128)S(1)}, f32[104,128]{1,0:T(8,128)S(1)}, u32[]{:S(2)}, u32[]{:S(2)}) collective-permute-start(f32[104,128]{1,0:T(8,128)S(1)} %get-tuple-element.919), channel_id=1, source_target_pairs={{0,5},{1,4},{2,7},{3,6},{4,0},{5,1},{6,2},{7,3},{8,13},{9,12},{10,... | collective-permute-start | bytes 159752 | tf_op jit(solution)/shard_map/ppermute | solution.py:390
  200.5 4.0 %collective-permute-done.58.refs_5_ = f32[104,128]{1,0:T(8,128)S(1)} collective-permute-done((f32[104,128]{1,0:T(8,128)S(1)}, f32[104,128]{1,0:T(8,128)S(1)}, u32[]{:S(2)}, u32[]{:S(2)}) %collective-permute-start.58) | collective-permute-done | bytes 53280 | tf_op jit(solution)/shard_map/ppermute | solution.py:390
  206.7 7.3 %collective-permute-start.60 = (f32[104,128]{1,0:T(8,128)S(1)}, f32[104,128]{1,0:T(8,128)S(1)}, u32[]{:S(2)}, u32[]{:S(2)}) collective-permute-start(f32[104,128]{1,0:T(8,128)S(1)} %get-tuple-element.937), channel_id=1, source_target_pairs={{0,5},{1,4},{2,7},{3,6},{4,0},{5,1},{6,2},{7,3},{8,13},{9,12},{10,... | collective-permute-start | bytes 159752 | tf_op jit(solution)/shard_map/ppermute | solution.py:390
  214.0 4.0 %collective-permute-done.60.refs_5_ = f32[104,128]{1,0:T(8,128)S(1)} collective-permute-done((f32[104,128]{1,0:T(8,128)S(1)}, f32[104,128]{1,0:T(8,128)S(1)}, u32[]{:S(2)}, u32[]{:S(2)}) %collective-permute-start.60) | collective-permute-done | bytes 53280 | tf_op jit(solution)/shard_map/ppermute | solution.py:390
  220.2 7.2 %collective-permute-start.62 = (f32[104,128]{1,0:T(8,128)S(1)}, f32[104,128]{1,0:T(8,128)S(1)}, u32[]{:S(2)}, u32[]{:S(2)}) collective-permute-start(f32[104,128]{1,0:T(8,128)S(1)} %get-tuple-element.955), channel_id=1, source_target_pairs={{0,5},{1,4},{2,7},{3,6},{4,0},{5,1},{6,2},{7,3},{8,12},{9,13},{10,... | collective-permute-start | bytes 159752 | tf_op jit(solution)/shard_map/ppermute | solution.py:390
  227.4 4.0 %collective-permute-done.62.refs_5_ = f32[104,128]{1,0:T(8,128)S(1)} collective-permute-done((f32[104,128]{1,0:T(8,128)S(1)}, f32[104,128]{1,0:T(8,128)S(1)}, u32[]{:S(2)}, u32[]{:S(2)}) %collective-permute-start.62) | collective-permute-done | bytes 53280 | tf_op jit(solution)/shard_map/ppermute | solution.py:390
  (176 shorter events, 105.9 us)
Async XLA Ops:
  13.4 9.9 %collective-permute-start.2 = (f32[104,128]{1,0:T(8,128)S(1)}, f32[104,128]{1,0:T(8,128)S(1)}, u32[]{:S(2)}, u32[]{:S(2)}) collective-permute-start(f32[104,128]{1,0:T(8,128)S(1)} %get-tuple-element.510), channel_id=1, source_target_pairs={{0,4},{1,5},{2,6},{3,7},{4,1},{5,0},{6,3},{7,2},{8,12},{9,13},{10,... | collective-permute-start | bytes 159752 | tf_op jit(solution)/shard_map/ppermute | solution.py:390
  26.9 9.9 %collective-permute-start.4 = (f32[104,128]{1,0:T(8,128)S(1)}, f32[104,128]{1,0:T(8,128)S(1)}, u32[]{:S(2)}, u32[]{:S(2)}) collective-permute-start(f32[104,128]{1,0:T(8,128)S(1)} %get-tuple-element.529), channel_id=1, source_target_pairs={{0,4},{1,5},{2,6},{3,7},{4,1},{5,0},{6,3},{7,2},{8,12},{9,13},{10,... | collective-permute-start | bytes 159752 | tf_op jit(solution)/shard_map/ppermute | solution.py:390
  38.4 6.7 %collective-permute-start.7 = (f32[104,128]{1,0:T(8,128)S(1)}, f32[104,128]{1,0:T(8,128)S(1)}, u32[]{:S(2)}, u32[]{:S(2)}) collective-permute-start(f32[104,128]{1,0:T(8,128)S(1)} %get-tuple-element.556), channel_id=1, source_target_pairs={{0,4},{1,5},{2,6},{3,7},{4,1},{5,0},{6,3},{7,2},{8,12},{9,13},{10,... | collective-permute-start | bytes 159752 | tf_op jit(solution)/shard_map/ppermute | solution.py:390
  43.4 6.5 %collective-permute-start.10 = (f32[2,104,128]{2,1,0:T(8,128)S(1)}, f32[2,104,128]{2,1,0:T(8,128)S(1)}, u32[]{:S(2)}, u32[]{:S(2)}) collective-permute-start(f32[2,104,128]{2,1,0:T(8,128)S(1)} %get-tuple-element.574), channel_id=1, source_target_pairs={{0,0},{1,2},{2,1},{3,3},{4,4},{5,6},{6,5},{7,7},{8,8},{9,10},{10,9... | collective-permute-start | bytes 319496 | tf_op jit(solution)/shard_map/ppermute | solution.py:410
  50.0 7.3 %collective-permute-start.11 = (f32[104,128]{1,0:T(8,128)S(1)}, f32[104,128]{1,0:T(8,128)S(1)}, u32[]{:S(2)}, u32[]{:S(2)}) collective-permute-start(f32[104,128]{1,0:T(8,128)S(1)} %get-tuple-element.584), channel_id=1, source_target_pairs={{0,4},{1,5},{2,6},{3,7},{4,0},{5,1},{6,2},{7,3},{8,12},{9,13},{10,... | collective-permute-start | bytes 159752 | tf_op jit(solution)/shard_map/ppermute | solution.py:390
  61.3 7.1 %collective-permute-start.15 = (f32[104,128]{1,0:T(8,128)S(1)}, f32[104,128]{1,0:T(8,128)S(1)}, u32[]{:S(2)}, u32[]{:S(2)}) collective-permute-start(f32[104,128]{1,0:T(8,128)S(1)} %get-tuple-element.612), channel_id=1, source_target_pairs={{0,4},{1,5},{2,6},{3,7},{4,0},{5,1},{6,2},{7,3},{8,12},{9,13},{10,... | collective-permute-start | bytes 159752 | tf_op jit(solution)/shard_map/ppermute | solution.py:390
  66.3 6.0 %collective-permute-start.18 = (f32[2,104,128]{2,1,0:T(8,128)S(1)}, f32[2,104,128]{2,1,0:T(8,128)S(1)}, u32[]{:S(2)}, u32[]{:S(2)}) collective-permute-start(f32[2,104,128]{2,1,0:T(8,128)S(1)} %get-tuple-element.630), channel_id=1, source_target_pairs={{0,0},{1,2},{2,1},{3,3},{4,4},{5,6},{6,5},{7,7},{8,8},{9,10},{10,9... | collective-permute-start | bytes 319496 | tf_op jit(solution)/shard_map/ppermute | solution.py:410
  72.4 7.0 %collective-permute-start.19 = (f32[104,128]{1,0:T(8,128)S(1)}, f32[104,128]{1,0:T(8,128)S(1)}, u32[]{:S(2)}, u32[]{:S(2)}) collective-permute-start(f32[104,128]{1,0:T(8,128)S(1)} %get-tuple-element.640), channel_id=1, source_target_pairs={{0,4},{1,5},{2,6},{3,7},{4,0},{5,1},{6,2},{7,3},{8,13},{9,12},{10,... | collective-permute-start | bytes 159752 | tf_op jit(solution)/shard_map/ppermute | solution.py:390
  82.6 10.1 %collective-permute-start.23 = (f32[104,128]{1,0:T(8,128)S(1)}, f32[104,128]{1,0:T(8,128)S(1)}, u32[]{:S(2)}, u32[]{:S(2)}) collective-permute-start(f32[104,128]{1,0:T(8,128)S(1)} %get-tuple-element.668), channel_id=1, source_target_pairs={{0,5},{1,4},{2,7},{3,6},{4,0},{5,1},{6,2},{7,3},{8,13},{9,12},{10,... | collective-permute-start | bytes 159752 | tf_op jit(solution)/shard_map/ppermute | solution.py:390
  89.3 8.6 %collective-permute-start.26 = (f32[2,104,128]{2,1,0:T(8,128)S(1)}, f32[2,104,128]{2,1,0:T(8,128)S(1)}, u32[]{:S(2)}, u32[]{:S(2)}) collective-permute-start(f32[2,104,128]{2,1,0:T(8,128)S(1)} %get-tuple-element.686), channel_id=1, source_target_pairs={{0,0},{1,1},{2,2},{3,3},{4,4},{5,6},{6,5},{7,7},{8,9},{9,8},{10,11... | collective-permute-start | bytes 319496 | tf_op jit(solution)/shard_map/ppermute | solution.py:410
  103.2 8.7 %collective-permute-start.30 = (f32[2,104,128]{2,1,0:T(8,128)S(1)}, f32[2,104,128]{2,1,0:T(8,128)S(1)}, u32[]{:S(2)}, u32[]{:S(2)}) collective-permute-start(f32[2,104,128]{2,1,0:T(8,128)S(1)} %get-tuple-element.714), channel_id=1, source_target_pairs={{0,1},{1,0},{2,3},{3,2},{4,4},{5,6},{6,5},{7,7},{8,8},{9,10},{10,9... | collective-permute-start | bytes 319496 | tf_op jit(solution)/shard_map/ppermute | solution.py:410
  106.4 5.9 %collective-permute-start.28 = (f32[104,128]{1,0:T(8,128)S(1)}, f32[104,128]{1,0:T(8,128)S(1)}, u32[]{:S(2)}, u32[]{:S(2)}) collective-permute-start(f32[104,128]{1,0:T(8,128)S(1)} %get-tuple-element.709), channel_id=1, source_target_pairs={{0,0},{1,2},{2,1},{3,3},{4,8},{5,9},{6,10},{7,11},{8,4},{9,5},{10,... | collective-permute-start | bytes 159752 | tf_op jit(solution)/shard_map/ppermute | solution.py:390
  116.3 8.6 %collective-permute-start.34 = (f32[2,104,128]{2,1,0:T(8,128)S(1)}, f32[2,104,128]{2,1,0:T(8,128)S(1)}, u32[]{:S(2)}, u32[]{:S(2)}) collective-permute-start(f32[2,104,128]{2,1,0:T(8,128)S(1)} %get-tuple-element.742), channel_id=1, source_target_pairs={{0,0},{1,2},{2,1},{3,3},{4,4},{5,6},{6,5},{7,7},{8,9},{9,8},{10,11... | collective-permute-start | bytes 319496 | tf_op jit(solution)/shard_map/ppermute | solution.py:410
  129.1 8.7 %collective-permute-start.38 = (f32[2,104,128]{2,1,0:T(8,128)S(1)}, f32[2,104,128]{2,1,0:T(8,128)S(1)}, u32[]{:S(2)}, u32[]{:S(2)}) collective-permute-start(f32[2,104,128]{2,1,0:T(8,128)S(1)} %get-tuple-element.770), channel_id=1, source_target_pairs={{0,1},{1,0},{2,3},{3,2},{4,4},{5,6},{6,5},{7,7},{8,8},{9,10},{10,9... | collective-permute-start | bytes 319496 | tf_op jit(solution)/shard_map/ppermute | solution.py:410
  132.3 6.5 %collective-permute-start.36 = (f32[104,128]{1,0:T(8,128)S(1)}, f32[104,128]{1,0:T(8,128)S(1)}, u32[]{:S(2)}, u32[]{:S(2)}) collective-permute-start(f32[104,128]{1,0:T(8,128)S(1)} %get-tuple-element.765), channel_id=1, source_target_pairs={{0,0},{1,2},{2,1},{3,3},{4,8},{5,9},{6,10},{7,11},{8,5},{9,4},{10,... | collective-permute-start | bytes 159752 | tf_op jit(solution)/shard_map/ppermute | solution.py:390
  133.0 5.9 %collective-permute-start.37 = (f32[1,104,128]{2,1,0:T(8,128)S(1)}, f32[1,104,128]{2,1,0:T(8,128)S(1)}, u32[]{:S(2)}, u32[]{:S(2)}) collective-permute-start(f32[1,104,128]{2,1,0:T(8,128)S(1)} %get-tuple-element.766), channel_id=1, source_target_pairs={{0,1},{1,0},{2,3},{3,2},{4,5},{5,4},{6,7},{7,6},{8,8},{9,9},{10,10... | collective-permute-start | bytes 159752 | tf_op jit(solution)/shard_map/ppermute | solution.py:410
  140.8 6.0 %collective-permute-start.42 = (f32[2,104,128]{2,1,0:T(8,128)S(1)}, f32[2,104,128]{2,1,0:T(8,128)S(1)}, u32[]{:S(2)}, u32[]{:S(2)}) collective-permute-start(f32[2,104,128]{2,1,0:T(8,128)S(1)} %get-tuple-element.798), channel_id=1, source_target_pairs={{0,0},{1,2},{2,1},{3,3},{4,5},{5,4},{6,7},{7,6},{8,9},{9,8},{10,11... | collective-permute-start | bytes 319496 | tf_op jit(solution)/shard_map/ppermute | solution.py:410
  147.0 7.5 %collective-permute-start.43 = (f32[104,128]{1,0:T(8,128)S(1)}, f32[104,128]{1,0:T(8,128)S(1)}, u32[]{:S(2)}, u32[]{:S(2)}) collective-permute-start(f32[104,128]{1,0:T(8,128)S(1)} %get-tuple-element.808), channel_id=1, source_target_pairs={{0,4},{1,5},{2,6},{3,7},{4,0},{5,1},{6,2},{7,3},{8,12},{9,13},{10,... | collective-permute-start | bytes 159752 | tf_op jit(solution)/shard_map/ppermute | solution.py:390
  158.2 7.3 %collective-permute-start.47 = (f32[104,128]{1,0:T(8,128)S(1)}, f32[104,128]{1,0:T(8,128)S(1)}, u32[]{:S(2)}, u32[]{:S(2)}) collective-permute-start(f32[104,128]{1,0:T(8,128)S(1)} %get-tuple-element.836), channel_id=1, source_target_pairs={{0,4},{1,5},{2,6},{3,7},{4,0},{5,1},{6,2},{7,3},{8,12},{9,13},{10,... | collective-permute-start | bytes 159752 | tf_op jit(solution)/shard_map/ppermute | solution.py:390
  168.7 7.9 %collective-permute-start.51 = (f32[104,128]{1,0:T(8,128)S(1)}, f32[104,128]{1,0:T(8,128)S(1)}, u32[]{:S(2)}, u32[]{:S(2)}) collective-permute-start(f32[104,128]{1,0:T(8,128)S(1)} %get-tuple-element.864), channel_id=1, source_target_pairs={{0,4},{1,5},{2,6},{3,7},{4,0},{5,1},{6,2},{7,3},{8,13},{9,12},{10,... | collective-permute-start | bytes 159752 | tf_op jit(solution)/shard_map/ppermute | solution.py:390
  179.7 8.9 %collective-permute-start.55 = (f32[104,128]{1,0:T(8,128)S(1)}, f32[104,128]{1,0:T(8,128)S(1)}, u32[]{:S(2)}, u32[]{:S(2)}) collective-permute-start(f32[104,128]{1,0:T(8,128)S(1)} %get-tuple-element.892), channel_id=1, source_target_pairs={{0,5},{1,4},{2,7},{3,6},{4,0},{5,1},{6,2},{7,3},{8,13},{9,12},{10,... | collective-permute-start | bytes 159752 | tf_op jit(solution)/shard_map/ppermute | solution.py:390
  190.8 13.8 %collective-permute-start.58 = (f32[104,128]{1,0:T(8,128)S(1)}, f32[104,128]{1,0:T(8,128)S(1)}, u32[]{:S(2)}, u32[]{:S(2)}) collective-permute-start(f32[104,128]{1,0:T(8,128)S(1)} %get-tuple-element.919), channel_id=1, source_target_pairs={{0,5},{1,4},{2,7},{3,6},{4,0},{5,1},{6,2},{7,3},{8,13},{9,12},{10,... | collective-permute-start | bytes 159752 | tf_op jit(solution)/shard_map/ppermute | solution.py:390
  206.7 11.3 %collective-permute-start.60 = (f32[104,128]{1,0:T(8,128)S(1)}, f32[104,128]{1,0:T(8,128)S(1)}, u32[]{:S(2)}, u32[]{:S(2)}) collective-permute-start(f32[104,128]{1,0:T(8,128)S(1)} %get-tuple-element.937), channel_id=1, source_target_pairs={{0,5},{1,4},{2,7},{3,6},{4,0},{5,1},{6,2},{7,3},{8,13},{9,12},{10,... | collective-permute-start | bytes 159752 | tf_op jit(solution)/shard_map/ppermute | solution.py:390
  220.2 11.3 %collective-permute-start.62 = (f32[104,128]{1,0:T(8,128)S(1)}, f32[104,128]{1,0:T(8,128)S(1)}, u32[]{:S(2)}, u32[]{:S(2)}) collective-permute-start(f32[104,128]{1,0:T(8,128)S(1)} %get-tuple-element.955), channel_id=1, source_target_pairs={{0,5},{1,4},{2,7},{3,6},{4,0},{5,1},{6,2},{7,3},{8,12},{9,13},{10,... | collective-permute-start | bytes 159752 | tf_op jit(solution)/shard_map/ppermute | solution.py:390
  (39 other events, 132.8 us)
